TPU v7x, 512 devices: a whole 4x8x8 slice. The times are simulated.
512 devices in a mesh: group: 16 (over z, core), member: 32 (over x, y).
Axes of the slice: x: 4, y: 8, z: 8, core: 2. Of those that a mesh axis runs over, the one named last changes fastest.
Arguments:
- entities: bfloat16 [524288, 256], P(('group', 'member')), may hold values from -1.5 to 1.5
- relations: bfloat16 [64, 256, 256], P('group'), may hold values from -0.375 to 0.375
- src_block: int32 [16, 32, 16], P('group'), may hold values from 0 to 7
- dst_member: int32 [16, 32, 16], P('group'), may hold values from 0 to 31, all different within a row
- dst_block: int32 [16, 32, 16], P('group'), may hold values from 0 to 7
- rel_id: int32 [16, 32, 16], P('group'), may hold values from 0 to 3
- neg_block: int32 [16, 32, 16], P(None, 'member'), may hold values from 0 to 7
- pos_mask: int32 [16, 32, 16, 128, 128], P('group', 'member'), may hold values 0 or 1
Outputs:
- entity_grad: float32 [524288, 256], P(('group', 'member'))
- relation_grad: float32 [64, 256, 256], P('group', 'member')
Inputs may be any that keep to these rules, and one draw needn't show every extreme that they name: `dst_member`: the 16 tiles of one device name 16 different members.
All inputs are finite; a program needn't handle non-finite values. No bound on the sum of `pos_mask` on one device may be relied on, other than what follows from the above.
Results may differ from a plain program's by a relative error of at most 0.0039.
Values may be sent and summed in bfloat16 or wider, within the bound.
No kernel may reach another device: no remote copies, remote signals or barrier semaphores. Data moves between devices by JAX's collectives and lax.ppermute only.
A program may use at most 64 MiB of HBM per device.

v0:
```python
import jax
import jax.numpy as jnp
from jax import lax
from jax.sharding import PartitionSpec as P

D = 256
B = 128
NB_DEV = 8


HI = lax.Precision.HIGHEST


def pick_row(table, index):
    return lax.dynamic_index_in_dim(table, index, 0, keepdims=False)


def per_device(entities, relations, src_block, dst_member, dst_block, rel_id, neg_block, pos_mask):
    members = lax.axis_size("member")
    groups = lax.axis_size("group")
    my_member = lax.axis_index("member")
    my_group = lax.axis_index("group")
    nblocks = NB_DEV
    rows = B
    width = D
    tiles = members // 2
    rounds = tiles // groups
    blocks = entities.reshape(nblocks, rows, width)
    my_src = pick_row(src_block[0], my_member)
    my_dst = pick_row(dst_member[0], my_member)
    my_rel = pick_row(rel_id[0], my_member)
    match = dst_member[0] == my_member
    wanted = jnp.any(match, axis=1)
    which = jnp.sum(jnp.where(match, dst_block[0], 0), axis=1)
    block_ids = jnp.arange(nblocks, dtype=jnp.int32)
    send_onehot = jnp.logical_and(wanted[:, None], which[:, None] == block_ids[None, :])
    outgoing = jnp.einsum(
        "pj,jbd->pbd", send_onehot.astype(jnp.bfloat16), blocks, preferred_element_type=jnp.float32
    ).astype(jnp.bfloat16)
    received = lax.all_to_all(outgoing, "member", split_axis=0, concat_axis=0, tiled=True)
    neg_want = lax.dynamic_index_in_dim(neg_block[:, 0, :], my_group, 1, keepdims=False)
    neg_out = jnp.take(blocks, neg_want, axis=0)
    neg_in = lax.all_to_all(neg_out, "group", split_axis=0, concat_axis=0, tiled=True)
    neg_slot = jnp.arange(tiles, dtype=jnp.int32) % groups
    src_tiles = jnp.take(blocks, my_src, axis=0)
    dst_tiles = jnp.take(received, my_dst, axis=0)
    neg_tiles = jnp.take(neg_in, neg_slot, axis=0)
    rel_tiles = jnp.take(relations, my_rel, axis=0)
    transformed = jnp.einsum(
        "kbd,kde->kbe", src_tiles, rel_tiles, preferred_element_type=jnp.float32
    ).astype(jnp.bfloat16)
    pos_scores = jnp.einsum(
        "kbe,kce->kbc", transformed, dst_tiles, preferred_element_type=jnp.float32
    )
    neg_scores = jnp.einsum(
        "kbe,kce->kbc", transformed, neg_tiles, preferred_element_type=jnp.float32
    )
    mask = pos_mask[0, 0].astype(jnp.float32)
    grad_pos = (-mask * jax.nn.sigmoid(-pos_scores)).astype(jnp.bfloat16)
    grad_neg = (0.125 * jax.nn.sigmoid(neg_scores)).astype(jnp.bfloat16)
    grad_h = (
        jnp.einsum("kbc,kce->kbe", grad_pos, dst_tiles, preferred_element_type=jnp.float32)
        + jnp.einsum("kbc,kce->kbe", grad_neg, neg_tiles, preferred_element_type=jnp.float32)
    ).astype(jnp.bfloat16)
    grad_src = jnp.einsum("kbe,kde->kbd", grad_h, rel_tiles, preferred_element_type=jnp.float32)
    grad_rel = jnp.einsum("kbd,kbe->kde", src_tiles, grad_h, preferred_element_type=jnp.float32)
    src_onehot = (my_src[:, None] == block_ids[None, :]).astype(jnp.float32)
    entity_acc = jnp.einsum("kj,kbd->jbd", src_onehot, grad_src, precision=HI)
    send_weights = send_onehot.astype(jnp.float32)
    want_onehot = (neg_want[:, None] == block_ids[None, :]).astype(jnp.float32)
    peer_ids = jnp.arange(members, dtype=jnp.int32)
    dst_onehot = my_dst[:, None] == peer_ids[None, :]
    grad_dst = jnp.einsum("kbc,kbe->kce", grad_pos, transformed, preferred_element_type=jnp.float32)
    grad_negb = jnp.einsum(
        "kbc,kbe->kce", grad_neg, transformed, preferred_element_type=jnp.float32
    )
    back_buf = jnp.einsum("kp,kce->pce", dst_onehot.astype(jnp.float32), grad_dst, precision=HI)
    back_in = lax.all_to_all(back_buf, "member", split_axis=0, concat_axis=0, tiled=True)
    entity_acc = entity_acc + jnp.einsum("pj,pbd->jbd", send_weights, back_in, precision=HI)
    neg_buf = jnp.sum(grad_negb.reshape(rounds, groups, rows, width), axis=0)
    neg_back = lax.all_to_all(
        neg_buf.astype(jnp.bfloat16), "group", split_axis=0, concat_axis=0, tiled=True
    ).astype(neg_buf.dtype)
    entity_acc = entity_acc + jnp.einsum("pj,pbd->jbd", want_onehot, neg_back, precision=HI)
    rel_onehot = (
        my_rel[:, None] == jnp.arange(relations.shape[0], dtype=jnp.int32)[None, :]
    ).astype(jnp.float32)
    rel_part = jnp.einsum("kr,kde->rde", rel_onehot, grad_rel, precision=HI)
    relation_grad = lax.psum_scatter(rel_part, "member", scatter_dimension=1, tiled=True)
    return (entity_acc.reshape(nblocks * rows, width), relation_grad)


def solution(mesh):
    placed = (
        P(("group", "member"), None),
        P("group", None, None),
        P("group", None, None),
        P("group", None, None),
        P("group", None, None),
        P("group", None, None),
        P(None, "member", None),
        P("group", "member", None, None, None),
    )
    return jax.shard_map(
        per_device,
        mesh=mesh,
        in_specs=placed,
        out_specs=(P(("group", "member"), None), P("group", "member", None)),
        check_vma=False,
    )
```

profile of v0, /device:TPU:64, one launch (start us, length us, event | category | flops | bytes accessed | tf_op | source)
XLA Modules:
  0.0 357.6 jit_solution(2562621787470753099)
XLA Ops:
  7.2 1.2 dynamic-slice_reduce_fusion
  8.4 0.9 dynamic-slice_reduce_fusion.3
  10.0 1.1 broadcast_select_fusion.1
  11.1 10.0 %all-to-all-start.1 = ((bf16[16,128,256]{2,1,0:T(8,128)(2,1)}), bf16[16,128,256]{2,1,0:T(8,128)(2,1)S(1)}, u32[]{:S(2)}, u32[]{:S(2)}) async-start(bf16[16,128,256]{2,1,0:T(8,128)(2,1)} %broadcast_select_fusion.1), calls=%async_computation.1 | async-start | bytes 2097152 | tf_op jit(solution)/shard_map/all_to_all | solution.py:43
  21.1 0.8 convolution_convert_fusion
  21.9 2.5 copy.34
  24.4 21.4 %all-to-all-done.1 = bf16[16,128,256]{2,1,0:T(8,128)(2,1)S(1)} async-done(((bf16[16,128,256]{2,1,0:T(8,128)(2,1)}), bf16[16,128,256]{2,1,0:T(8,128)(2,1)S(1)}, u32[]{:S(2)}, u32[]{:S(2)}) %all-to-all-start.1) | async-done | bytes 1048608 | tf_op jit(solution)/shard_map/all_to_all | solution.py:43
  45.8 10.1 %all-to-all-start = ((bf16[32,128,256]{2,1,0:T(8,128)(2,1)}), bf16[32,128,256]{2,1,0:T(8,128)(2,1)}, u32[]{:S(2)}, u32[]{:S(2)}) async-start(bf16[32,128,256]{2,1,0:T(8,128)(2,1)} %copy.34), calls=%async_computation | async-start | bytes 4194304 | tf_op jit(solution)/shard_map/all_to_all | solution.py:40
  56.0 1.6 gather_fusion.3
  58.7 3.3 convolution_convert_fusion.1
  62.0 2.8 gather_fusion.2
  64.9 2.2 fusion.22
  67.1 1.5 convolution_convert_fusion.2
  68.5 37.9 %all-to-all-done = bf16[32,128,256]{2,1,0:T(8,128)(2,1)} async-done(((bf16[32,128,256]{2,1,0:T(8,128)(2,1)}), bf16[32,128,256]{2,1,0:T(8,128)(2,1)}, u32[]{:S(2)}, u32[]{:S(2)}) %all-to-all-start) | async-done | bytes 2097184 | tf_op jit(solution)/shard_map/all_to_all | solution.py:40
  106.4 6.5 %all-to-all-start.3 = ((bf16[16,128,256]{2,1,0:T(8,128)(2,1)}), bf16[16,128,256]{2,1,0:T(8,128)(2,1)S(1)}, u32[]{:S(2)}, u32[]{:S(2)}) async-start(bf16[16,128,256]{2,1,0:T(8,128)(2,1)} %convolution_convert_fusion.2), calls=%async_computation.3 | async-start | bytes 2097152 | tf_op jit(solution)/shard_map/all_to_all | solution.py:81
  112.9 3.3 gather_fusion.1
  116.2 2.1 fusion.21
  119.1 2.9 fusion.4
  122.1 4.4 %copy.38 = f32[32,128,256]{2,1,0:T(8,128)} copy(f32[32,128,256]{2,0,1:T(8,128)S(1)} %fusion.4) | data formatting | bytes 8388608 | tf_op jit(solution)/shard_map/kp,kce->pce/dot_general | solution.py:77
  126.4 11.2 %all-to-all-done.3 = bf16[16,128,256]{2,1,0:T(8,128)(2,1)S(1)} async-done(((bf16[16,128,256]{2,1,0:T(8,128)(2,1)}), bf16[16,128,256]{2,1,0:T(8,128)(2,1)S(1)}, u32[]{:S(2)}, u32[]{:S(2)}) %all-to-all-start.3) | async-done | bytes 1048608 | tf_op jit(solution)/shard_map/all_to_all | solution.py:81
  137.7 1.0 copy-done.8
  138.7 6.7 %all-to-all-start.2 = ((f32[32,128,256]{2,1,0:T(8,128)}), f32[32,128,256]{2,1,0:T(8,128)}, u32[]{:S(2)}, u32[]{:S(2)}) async-start(f32[32,128,256]{2,1,0:T(8,128)} %copy.38), calls=%async_computation.2 | async-start | bytes 8388608 | tf_op jit(solution)/shard_map/all_to_all | solution.py:78
  145.7 1.6 fusion.27
  148.5 1.2 fusion.28
  149.8 5.0 %fusion = f32[4,256,256]{2,0,1:T(4,128)} fusion(f32[16,256,256]{2,1,0:T(8,128)S(1)} %fusion.28, s32[16]{0:T(128)S(1)} %dynamic-slice_reduce_fusion.2), kind=kOutput, calls=%fused_computation.5 | convolution fusion | flops 50331712 | bytes 5242944 | tf_op jit(solution)/shard_map/kr,kde->rde/dot_general | solution.py:88
  154.9 1.3 dynamic-slice.4
  156.8 1.6 fusion.23
  158.4 2.3 fusion.25
  160.7 179.3 %all-reduce.3.cloned.1.call-done = f32[4,256,256]{2,0,1:T(4,128)} async-done(((f32[4,256,256]{2,0,1:T(4,128)}), f32[4,256,256]{2,0,1:T(4,128)}) %all-reduce.3.cloned.1.call-update) | async-done | bytes 1048592
  341.4 6.0 %fusion.2 = f32[8,128,256]{2,0,1:T(8,128)S(1)} fusion(f32[32,128,256]{2,1,0:T(8,128)} %all-to-all-done.2, s32[32]{0:T(128)S(1)} %select_reduce_fusion, pred[32]{0:T(512)(128)(4,1)S(1)} %get-tuple-element.11), kind=kOutput, calls=%fused_computation.7 | convolution fusion | flops 100663808 | bytes 5243040 | tf_op jit(solution)/shard_map/pj,pbd->jbd/dot_general | solution.py:79
  347.4 2.1 fusion.11
  349.5 1.3 copy.42
  (58 shorter events, 5.5 us)
Async XLA Ops:
  7.2 2.1 copy-start
  9.9 11.1 %copy-start.14 = (s32[1,32,16]{1,2,0:T(8,128)S(1)}, s32[1,32,16]{1,2,0:T(8,128)}, u32[]{:S(2)}) copy-start(s32[1,32,16]{1,2,0:T(8,128)} %param.13) | copy-start | bytes 6148
  9.9 11.2 %copy-start.16 = (s32[1,32,16]{1,2,0:T(8,128)S(1)}, s32[1,32,16]{1,2,0:T(8,128)}, u32[]{:S(2)}) copy-start(s32[1,32,16]{1,2,0:T(8,128)} %param.14) | copy-start | bytes 6148
  11.1 34.7 %all-to-all-start.1 = ((bf16[16,128,256]{2,1,0:T(8,128)(2,1)}), bf16[16,128,256]{2,1,0:T(8,128)(2,1)S(1)}, u32[]{:S(2)}, u32[]{:S(2)}) async-start(bf16[16,128,256]{2,1,0:T(8,128)(2,1)} %broadcast_select_fusion.1), calls=%async_computation.1 | async-start | bytes 2097152 | tf_op jit(solution)/shard_map/all_to_all | solution.py:43
  45.8 10.1 %copy-start.10 = (bf16[16,128,256]{2,1,0:T(8,128)(2,1)}, bf16[16,128,256]{2,1,0:T(8,128)(2,1)S(1)}, u32[]{:S(2)}) copy-start(bf16[16,128,256]{2,1,0:T(8,128)(2,1)S(1)} %all-to-all-done.1) | copy-start | bytes 3145732
  45.8 60.6 %all-to-all-start = ((bf16[32,128,256]{2,1,0:T(8,128)(2,1)}), bf16[32,128,256]{2,1,0:T(8,128)(2,1)}, u32[]{:S(2)}, u32[]{:S(2)}) async-start(bf16[32,128,256]{2,1,0:T(8,128)(2,1)} %copy.34), calls=%async_computation | async-start | bytes 4194304 | tf_op jit(solution)/shard_map/all_to_all | solution.py:40
  55.9 1.6 copy-start.15
  55.9 1.8 copy-start.4
  58.5 3.6 %copy-start.1 = (bf16[16,256,256]{2,1,0:T(8,128)(2,1)}, bf16[16,256,256]{2,1,0:T(8,128)(2,1)S(1)}, u32[]{:S(2)}) copy-start(bf16[16,256,256]{2,1,0:T(8,128)(2,1)S(1)} %gather_fusion) | copy-start | bytes 6291460
  64.9 2.2 copy-start.7
  106.4 31.3 %all-to-all-start.3 = ((bf16[16,128,256]{2,1,0:T(8,128)(2,1)}), bf16[16,128,256]{2,1,0:T(8,128)(2,1)S(1)}, u32[]{:S(2)}, u32[]{:S(2)}) async-start(bf16[16,128,256]{2,1,0:T(8,128)(2,1)} %convolution_convert_fusion.2), calls=%async_computation.3 | async-start | bytes 2097152 | tf_op jit(solution)/shard_map/all_to_all | solution.py:81
  118.3 0.8 copy-start.13
  126.4 19.3 %copy-start.12 = (bf16[16,128,256]{2,1,0:T(8,128)(2,1)S(1)}, bf16[16,128,256]{2,1,0:T(8,128)(2,1)}, u32[]{:S(2)}) copy-start(bf16[16,128,256]{2,1,0:T(8,128)(2,1)} %gather_fusion.1) | copy-start | bytes 3145732
  137.7 1.0 copy-start.8
  138.7 202.7 %all-to-all-start.2 = ((f32[32,128,256]{2,1,0:T(8,128)}), f32[32,128,256]{2,1,0:T(8,128)}, u32[]{:S(2)}, u32[]{:S(2)}) async-start(f32[32,128,256]{2,1,0:T(8,128)} %copy.38), calls=%async_computation.2 | async-start | bytes 8388608 | tf_op jit(solution)/shard_map/all_to_all | solution.py:78
  145.4 1.9 copy-start.6
  145.4 194.6 %all-reduce.3.cloned.1.call-start = ((), (), s32[]{:S(2)}) async-start(), calls=%async_computation.4 | async-start | bytes 2097152
  147.3 1.2 copy-start.5
  149.8 7.0 %copy-start.9 = (bf16[16,128,256]{2,1,0:T(8,128)(2,1)S(1)}, bf16[16,128,256]{2,1,0:T(8,128)(2,1)}, u32[]{:S(2)}) copy-start(bf16[16,128,256]{2,1,0:T(8,128)(2,1)} %copy-done.8) | copy-start | bytes 3145732
  156.8 1.7 copy-start.2
  341.4 6.0 %copy-start.3 = (f32[16,128,256]{2,1,0:T(8,128)S(1)}, f32[16,128,256]{2,1,0:T(8,128)}, u32[]{:S(2)}) copy-start(f32[16,128,256]{2,1,0:T(8,128)} %fusion.25) | copy-start | bytes 6291460
  341.4 6.0 %copy-start.11 = (f32[8,128,256]{2,0,1:T(8,128)S(1)}, f32[8,128,256]{2,0,1:T(8,128)}, u32[]{:S(2)}) copy-start(f32[8,128,256]{2,0,1:T(8,128)} %fusion.23) | copy-start | bytes 3145732
Sparse Core Ops, SparseCore 0:
  155.0 184.9 all-reduce.2
where the time goes:
time: 358 us
  waiting for transfers between devices  250 us (70%)
  starting transfers between devices  33.6 us (9%)
  matrix products  33.6 us (9%)
  local copies, waits for them, and re-layouts  24.3 us (7%)
  between operations  15 us (4%)
    unnamed x2, waiting for transfers between devices  179 us
    all_to_all x1, waiting for transfers between devices, per_device(): lax.all_to_all(outgoing, 'member', split_axis=0, concat_axis=0, tiled=True)  37.9 us
    all_to_all x1, waiting for transfers between devices, per_device(): lax.all_to_all(neg_out, 'group', split_axis=0, concat_axis=0, tiled=True)  21.4 us
    all_to_all x1, waiting for transfers between devices, per_device(): lax.all_to_all(neg_buf.astype(jnp.bfloat16), 'group', split_axis=0, conca...  11.2 us
    all_to_all x1, starting transfers between devices, per_device(): lax.all_to_all(outgoing, 'member', split_axis=0, concat_axis=0, tiled=True)  10.1 us
    all_to_all x1, starting transfers between devices, per_device(): lax.all_to_all(neg_out, 'group', split_axis=0, concat_axis=0, tiled=True)  9.98 us
  transfers between devices with their start and end apart: 5, of which 4 were waited for; matrix products, arithmetic and copies ran while one was open for 12% of the time, Pallas kernels for 0%

commit v1 on v0

v1 whole, which is shorter than its diff:
```python
import jax
import jax.numpy as jnp
from jax import lax
from jax.experimental import pallas as pl
from jax.experimental.pallas import tpu as pltpu
from jax.sharding import PartitionSpec as P

D = 256
B = 128
NB_DEV = 8
TILES = 16
RELS = 4
F32 = jnp.float32
BF16 = jnp.bfloat16

PARAMS = pltpu.CompilerParams(vmem_limit_bytes=24 * 1024 * 1024)
VMEM = pl.BlockSpec(memory_space=pltpu.VMEM)
SMEM = pl.BlockSpec(memory_space=pltpu.SMEM)


def sds(shape, dtype):
    return jax.ShapeDtypeStruct(shape, dtype)


def dot(a, b, dims):
    return lax.dot_general(a, b, (dims, ((), ())), preferred_element_type=F32)


NN = ((1,), (0,))
NT = ((1,), (1,))
TN = ((0,), (0,))


def call(body, ins, outs, flops, nbytes, scratch=(), alias=None):
    return pl.pallas_call(
        body,
        out_shape=outs,
        in_specs=ins,
        out_specs=jax.tree.map(lambda _: VMEM, outs),
        scratch_shapes=scratch,
        compiler_params=PARAMS,
        input_output_aliases=alias or {},
        cost_estimate=pl.CostEstimate(flops=flops, bytes_accessed=nbytes, transcendentals=0),
    )


def pick_body(idx, blocks, *outs):
    n = 0
    for o in outs:
        for t in range(o.shape[0]):
            o[t] = blocks[idx[n]]
            n += 1


def h_body(src, rel, blocks, rels, h):
    for k in range(TILES):
        h[k] = dot(blocks[src[k]], rels[rel[k]], NN).astype(BF16)


def neg_body(tile_of, h, *refs):
    own, sib, gq = refs[:8], refs[8], refs[9]
    outs = refs[10:]
    for s in range(8):
        for t in range(2):
            k = tile_of[2 * s + t]
            neg = own[s][0] if t == 0 else sib[s]
            hk = h[k]
            q = (0.125 * jax.nn.sigmoid(dot(hk, neg, NT))).astype(BF16)
            gq[2 * s + t] = q
            outs[s][t] = dot(q, hk, TN).astype(BF16)


def pos_body(dst, h, received, mask, gp, back):
    for k in range(TILES):
        hk = h[k]
        p = dot(hk, received[dst[k]], NT)
        g = (-mask[k].astype(F32) * jax.nn.sigmoid(-p)).astype(BF16)
        gp[k] = g
        back[dst[k]] = dot(g, hk, TN).astype(BF16)


def own_body(tile_of, dst, src, rel, blocks, rels, received, gp, gq, *refs):
    own, sib, acc, racc = refs[:8], refs[8], refs[9], refs[10]
    acc[...] = jnp.zeros(acc.shape, F32)
    racc[...] = jnp.zeros(racc.shape, F32)
    for s in range(8):
        for t in range(2):
            k = tile_of[2 * s + t]
            neg = own[s][0] if t == 0 else sib[s]
            gh = dot(gp[k], received[dst[k]], NN) + dot(gq[2 * s + t], neg, NN)
            gh = gh.astype(BF16)
            j = src[k]
            r = rel[k]
            acc[j] += dot(gh, rels[r], NT)
            racc[r] += dot(blocks[j], gh, TN)


def add_neg_body(idx, acc_in, *refs):
    own, sib, acc = refs[:8], refs[8], refs[9]
    acc[...] = acc_in[...]
    for s in range(8):
        for t in range(2):
            j = idx[2 * s + t]
            val = own[s][0] if t == 0 else sib[s]
            acc[j] += val.astype(F32)


def add_dst_body(which, wanted, acc_in, back, acc):
    acc[...] = acc_in[...]
    for p in range(back.shape[0]):
        @pl.when(wanted[p] > 0)
        def _():
            j = which[p]
            acc[j] += back[p].astype(F32)


def per_device(entities, relations, src_block, dst_member, dst_block, rel_id, neg_block, pos_mask):
    me = lax.axis_index("member")
    grp = lax.axis_index("group")
    z = grp // 2
    core = grp % 2
    blocks = entities.reshape(NB_DEV, B, D)

    match = dst_member[0] == me
    wanted = jnp.any(match, axis=1).astype(jnp.int32)
    which = jnp.sum(jnp.where(match, dst_block[0], 0), axis=1)
    src = lax.dynamic_index_in_dim(src_block[0], me, 0, keepdims=False)
    dst = lax.dynamic_index_in_dim(dst_member[0], me, 0, keepdims=False)
    rel = lax.dynamic_index_in_dim(rel_id[0], me, 0, keepdims=False)

    outgoing = pick(which, blocks, (32,))[0]
    received = lax.all_to_all(outgoing, "member", split_axis=0, concat_axis=0, tiled=True)

    steps = jnp.arange(8, dtype=jnp.int32)
    sides = jnp.stack([core, 1 - core])
    neg_want = lax.dynamic_index_in_dim(neg_block[:, 0, :], grp, 1, keepdims=False)
    ahead = ((((z + steps) % 8) * 2)[:, None] + sides[None, :]).reshape(16)
    tile_of = ((((z + 8 - steps) % 8) * 2)[:, None] + sides[None, :]).reshape(16)
    ahead_blocks = jnp.take(neg_want, ahead)
    parts = pick(ahead_blocks, blocks, (2,) * 8)
    got = [parts[0]] + [zshift(parts[s], s) for s in range(1, 8)]
    sib = swap(jnp.stack([g[1] for g in got]))

    h = call(h_body, [SMEM, SMEM, VMEM, VMEM], sds((TILES, B, D), BF16), 1 << 28, 2 << 20)(
        src, rel, blocks, relations
    )
    gq, *gn = call(
        neg_body,
        [SMEM] + [VMEM] * 10,
        [sds((TILES, B, B), BF16)] + [sds((2, B, D), BF16)] * 8,
        1 << 28,
        4 << 20,
    )(tile_of, h, *got, sib)
    gp, back = call(
        pos_body,
        [SMEM, VMEM, VMEM, VMEM],
        [sds((TILES, B, B), BF16), sds((32, B, D), BF16)],
        1 << 28,
        6 << 20,
    )(dst, h, received, pos_mask[0, 0])
    back_in = lax.all_to_all(back, "member", split_axis=0, concat_axis=0, tiled=True)

    neg_got = [gn[0]] + [zshift(gn[s], 8 - s) for s in range(1, 8)]
    neg_sib = swap(jnp.stack([g[1] for g in neg_got]))

    acc, racc = call(
        own_body,
        [SMEM] * 4 + [VMEM] * 14,
        [sds((NB_DEV, B, D), F32), sds((RELS, D, D), F32)],
        1 << 29,
        8 << 20,
    )(tile_of, dst, src, rel, blocks, relations, received, gp, gq, *got, sib)

    part = racc.reshape(RELS, 32, 8, D)
    span = 32
    while span > 1:
        span //= 2
        bit = (me // span) % 2
        keep = lax.dynamic_slice_in_dim(part, bit * span, span, 1)
        give = lax.dynamic_slice_in_dim(part, (1 - bit) * span, span, 1)
        part = keep + lax.ppermute(give, "member", [(i, i ^ span) for i in range(32)])
    relation_grad = part.reshape(RELS, 8, D)

    acc = call(
        add_neg_body, [SMEM] + [VMEM] * 10, sds((NB_DEV, B, D), F32), 1 << 20, 3 << 20
    )(ahead_blocks, acc, *neg_got, neg_sib)
    out = call(
        add_dst_body, [SMEM, SMEM, VMEM, VMEM], sds((NB_DEV, B, D), F32), 1 << 20, 4 << 20
    )(which, wanted, acc, back_in)
    return out.reshape(NB_DEV * B, D), relation_grad


def pick(idx, blocks, sizes):
    outs = [sds((n, B, D), BF16) for n in sizes]
    return call(pick_body, [SMEM, VMEM], outs, 0, 3 << 20)(idx, blocks)


def zshift(v, s):
    return lax.ppermute(
        v, "group", [(a * 2 + c, ((a + s) % 8) * 2 + c) for a in range(8) for c in range(2)]
    )


def swap(v):
    return lax.ppermute(v, "group", [(i, i ^ 1) for i in range(16)])


def solution(mesh):
    placed = (
        P(("group", "member"), None),
        P("group", None, None),
        P("group", None, None),
        P("group", None, None),
        P("group", None, None),
        P("group", None, None),
        P(None, "member", None),
        P("group", "member", None, None, None),
    )
    return jax.shard_map(
        per_device,
        mesh=mesh,
        in_specs=placed,
        out_specs=(P(("group", "member"), None), P("group", "member", None)),
        check_vma=False,
    )
```

time: 358 us -> 188 us (0.53)
  the two profiles are of different devices: /device:TPU:64 before, /device:TPU:72 now
where the time goes in v1:
time: 188 us; the launch traced here: 186 us
  starting transfers between devices  107 us (57%)
  local copies, waits for them, and re-layouts  36.1 us (19%)
  waiting for transfers between devices  23.5 us (12%)
  Pallas kernels  14.4 us (8%)
  other arithmetic  3.44 us (2%)
    ppermute x14, starting transfers between devices, zshift(): lax.ppermute(v, 'group', [(a * 2 + c, (a + s) % 8 * 2 + c) for a in range...  58.5 us
    unnamed x121, local copies, waits for them, and re-layouts  31.7 us
    ppermute x5, starting transfers between devices, per_device(): lax.ppermute(give, 'member', [(i, i ^ span) for i in range(32)])  24.6 us
    ppermute x5, waiting for transfers between devices, per_device(): lax.ppermute(give, 'member', [(i, i ^ span) for i in range(32)])  18.5 us
    all_to_all x1, starting transfers between devices, per_device(): lax.all_to_all(outgoing, 'member', split_axis=0, concat_axis=0, tiled=True)  10.3 us
    all_to_all x1, starting transfers between devices, per_device(): lax.all_to_all(back, 'member', split_axis=0, concat_axis=0, tiled=True)  9.84 us
    ppermute x14, waiting for transfers between devices, zshift(): lax.ppermute(v, 'group', [(a * 2 + c, (a + s) % 8 * 2 + c) for a in range...  5.04 us
    pallas_call x1, Pallas kernels, per_device(): call(own_body, [SMEM] * 4 + [VMEM] * 14, [sds((NB_DEV, B, D), F32), sds((...  4.35 us
  transfers between devices with their start and end apart: 23, of which 6 were waited for; matrix products, arithmetic and copies ran while one was open for 8% of the time, Pallas kernels for 6%

profile of v1, /device:TPU:72, one launch (start us, length us, event | category | flops | bytes accessed | tf_op | source)
XLA Modules:
  0.0 186.0 jit_solution(12174057708836111216)
XLA Ops:
  5.6 10.3 %all-to-all-start = ((bf16[32,128,256]{2,1,0:T(8,128)(2,1)}), bf16[32,128,256]{2,1,0:T(8,128)(2,1)S(1)}, u32[]{:S(2)}, u32[]{:S(2)}) async-start(bf16[32,128,256]{2,1,0:T(8,128)(2,1)} %copy-done.1), calls=%async_computation | async-start | bytes 4194304 | tf_op jit(solution)/shard_map/all_to_all | solution.py:132
  18.7 4.3 %collective-permute-start = (bf16[2,128,256]{2,1,0:T(8,128)(2,1)S(1)}, bf16[2,128,256]{2,1,0:T(8,128)(2,1)S(1)}, u32[]{:S(2)}, u32[]{:S(2)}) collective-permute-start(bf16[2,128,256]{2,1,0:T(8,128)(2,1)S(1)} %get-tuple-element.25), channel_id=1, source_target_pairs={{0,64},{32,96},{64,128},{96,160},{128,192},{160,224},{192,256},{22... | collective-permute-start | bytes 393224 | tf_op jit(solution)/shard_map/ppermute | solution.py:199
  23.0 7.3 %collective-permute-start.1 = (bf16[2,128,256]{2,1,0:T(8,128)(2,1)S(1)}, bf16[2,128,256]{2,1,0:T(8,128)(2,1)S(1)}, u32[]{:S(2)}, u32[]{:S(2)}) collective-permute-start(bf16[2,128,256]{2,1,0:T(8,128)(2,1)S(1)} %get-tuple-element.26), channel_id=1, source_target_pairs={{0,128},{32,160},{64,192},{96,224},{128,256},{160,288},{192,320},{... | collective-permute-start | bytes 393224 | tf_op jit(solution)/shard_map/ppermute | solution.py:199
  30.3 5.2 %collective-permute-start.2 = (bf16[2,128,256]{2,1,0:T(8,128)(2,1)S(1)}, bf16[2,128,256]{2,1,0:T(8,128)(2,1)S(1)}, u32[]{:S(2)}, u32[]{:S(2)}) collective-permute-start(bf16[2,128,256]{2,1,0:T(8,128)(2,1)S(1)} %get-tuple-element.27), channel_id=1, source_target_pairs={{0,192},{32,224},{64,256},{96,288},{128,320},{160,352},{192,384},{... | collective-permute-start | bytes 393224 | tf_op jit(solution)/shard_map/ppermute | solution.py:199
  35.5 1.9 %collective-permute-start.3 = (bf16[2,128,256]{2,1,0:T(8,128)(2,1)S(1)}, bf16[2,128,256]{2,1,0:T(8,128)(2,1)S(1)}, u32[]{:S(2)}, u32[]{:S(2)}) collective-permute-start(bf16[2,128,256]{2,1,0:T(8,128)(2,1)S(1)} %get-tuple-element.28), channel_id=1, source_target_pairs={{0,256},{32,288},{64,320},{96,352},{128,384},{160,416},{192,448},{... | collective-permute-start | bytes 393224 | tf_op jit(solution)/shard_map/ppermute | solution.py:199
  37.4 6.4 %collective-permute-start.4 = (bf16[2,128,256]{2,1,0:T(8,128)(2,1)S(1)}, bf16[2,128,256]{2,1,0:T(8,128)(2,1)S(1)}, u32[]{:S(2)}, u32[]{:S(2)}) collective-permute-start(bf16[2,128,256]{2,1,0:T(8,128)(2,1)S(1)} %get-tuple-element.29), channel_id=1, source_target_pairs={{0,320},{32,352},{64,384},{96,416},{128,448},{160,480},{192,0},{22... | collective-permute-start | bytes 393224 | tf_op jit(solution)/shard_map/ppermute | solution.py:199
  44.4 3.9 %collective-permute-start.5 = (bf16[2,128,256]{2,1,0:T(8,128)(2,1)S(1)}, bf16[2,128,256]{2,1,0:T(8,128)(2,1)S(1)}, u32[]{:S(2)}, u32[]{:S(2)}) collective-permute-start(bf16[2,128,256]{2,1,0:T(8,128)(2,1)S(1)} %get-tuple-element.30), channel_id=1, source_target_pairs={{0,384},{32,416},{64,448},{96,480},{128,0},{160,32},{192,64},{224,... | collective-permute-start | bytes 393224 | tf_op jit(solution)/shard_map/ppermute | solution.py:199
  49.0 3.7 %collective-permute-start.6 = (bf16[2,128,256]{2,1,0:T(8,128)(2,1)S(1)}, bf16[2,128,256]{2,1,0:T(8,128)(2,1)S(1)}, u32[]{:S(2)}, u32[]{:S(2)}) collective-permute-start(bf16[2,128,256]{2,1,0:T(8,128)(2,1)S(1)} %get-tuple-element.31), channel_id=1, source_target_pairs={{0,448},{32,480},{64,0},{96,32},{128,64},{160,96},{192,128},{224,1... | collective-permute-start | bytes 393224 | tf_op jit(solution)/shard_map/ppermute | solution.py:199
  57.1 4.9 %collective-permute-done.5.refs_6_ = bf16[2,128,256]{2,1,0:T(8,128)(2,1)S(1)} collective-permute-done((bf16[2,128,256]{2,1,0:T(8,128)(2,1)S(1)}, bf16[2,128,256]{2,1,0:T(8,128)(2,1)S(1)}, u32[]{:S(2)}, u32[]{:S(2)}) %collective-permute-start.5) | collective-permute-done | bytes 131104 | tf_op jit(solution)/shard_map/ppermute | solution.py:199
  64.7 1.9 %collective-permute-start.7 = (bf16[8,128,256]{2,1,0:T(8,128)(2,1)}, bf16[8,128,256]{2,1,0:T(8,128)(2,1)}, u32[]{:S(2)}, u32[]{:S(2)}) collective-permute-start(bf16[8,128,256]{2,1,0:T(8,128)(2,1)} %slice_dynamic-update-slice_fusion.7), channel_id=1, source_target_pairs={{0,32},{32,0},{64,96},{96,64},{128,160},{160,128},{192,224},{224,1... | collective-permute-start | bytes 1572872 | tf_op jit(solution)/shard_map/ppermute | solution.py:205
  71.9 1.6 shard_map.97
  75.7 9.8 %all-to-all-start.1 = ((bf16[32,128,256]{2,1,0:T(8,128)(2,1)}), bf16[32,128,256]{2,1,0:T(8,128)(2,1)}, u32[]{:S(2)}, u32[]{:S(2)}) async-start(bf16[32,128,256]{2,1,0:T(8,128)(2,1)} %copy-done.6), calls=%async_computation.1 | async-start | bytes 4194304 | tf_op jit(solution)/shard_map/all_to_all | solution.py:161
  92.3 2.2 %shard_map.99 = (bf16[16,128,128]{2,1,0:T(8,128)(2,1)S(1)}, bf16[2,128,256]{2,1,0:T(8,128)(2,1)S(1)}, bf16[2,128,256]{2,1,0:T(8,128)(2,1)S(1)}, bf16[2,128,256]{...) custom-call(s32[16]{0:T(128)S(1)} %copy-done.45, ...), custom_call_target="tpu_custom_call" | custom-call | flops 268435456 | bytes 4194304 | tf_op jit(solution)/shard_map/pallas_call | solution.py:147
  94.5 1.9 %collective-permute-start.8 = (bf16[2,128,256]{2,1,0:T(8,128)(2,1)S(1)}, bf16[2,128,256]{2,1,0:T(8,128)(2,1)S(1)}, u32[]{:S(2)}, u32[]{:S(2)}) collective-permute-start(bf16[2,128,256]{2,1,0:T(8,128)(2,1)S(1)} %get-tuple-element.35), channel_id=1, source_target_pairs={{0,448},{32,480},{64,0},{96,32},{128,64},{160,96},{192,128},{224,1... | collective-permute-start | bytes 393224 | tf_op jit(solution)/shard_map/ppermute | solution.py:199
  96.4 4.5 %collective-permute-start.9 = (bf16[2,128,256]{2,1,0:T(8,128)(2,1)S(1)}, bf16[2,128,256]{2,1,0:T(8,128)(2,1)S(1)}, u32[]{:S(2)}, u32[]{:S(2)}) collective-permute-start(bf16[2,128,256]{2,1,0:T(8,128)(2,1)S(1)} %get-tuple-element.36), channel_id=1, source_target_pairs={{0,384},{32,416},{64,448},{96,480},{128,0},{160,32},{192,64},{224,... | collective-permute-start | bytes 393224 | tf_op jit(solution)/shard_map/ppermute | solution.py:199
  100.9 5.3 %collective-permute-start.10 = (bf16[2,128,256]{2,1,0:T(8,128)(2,1)S(1)}, bf16[2,128,256]{2,1,0:T(8,128)(2,1)S(1)}, u32[]{:S(2)}, u32[]{:S(2)}) collective-permute-start(bf16[2,128,256]{2,1,0:T(8,128)(2,1)S(1)} %get-tuple-element.37), channel_id=1, source_target_pairs={{0,320},{32,352},{64,384},{96,416},{128,448},{160,480},{192,0},{22... | collective-permute-start | bytes 393224 | tf_op jit(solution)/shard_map/ppermute | solution.py:199
  106.2 4.2 %collective-permute-start.11 = (bf16[2,128,256]{2,1,0:T(8,128)(2,1)S(1)}, bf16[2,128,256]{2,1,0:T(8,128)(2,1)S(1)}, u32[]{:S(2)}, u32[]{:S(2)}) collective-permute-start(bf16[2,128,256]{2,1,0:T(8,128)(2,1)S(1)} %get-tuple-element.38), channel_id=1, source_target_pairs={{0,256},{32,288},{64,320},{96,352},{128,384},{160,416},{192,448},{... | collective-permute-start | bytes 393224 | tf_op jit(solution)/shard_map/ppermute | solution.py:199
  110.4 4.3 %collective-permute-start.12 = (bf16[2,128,256]{2,1,0:T(8,128)(2,1)S(1)}, bf16[2,128,256]{2,1,0:T(8,128)(2,1)S(1)}, u32[]{:S(2)}, u32[]{:S(2)}) collective-permute-start(bf16[2,128,256]{2,1,0:T(8,128)(2,1)S(1)} %get-tuple-element.39), channel_id=1, source_target_pairs={{0,192},{32,224},{64,256},{96,288},{128,320},{160,352},{192,384},{... | collective-permute-start | bytes 393224 | tf_op jit(solution)/shard_map/ppermute | solution.py:199
  115.4 2.8 %collective-permute-start.13 = (bf16[2,128,256]{2,1,0:T(8,128)(2,1)S(1)}, bf16[2,128,256]{2,1,0:T(8,128)(2,1)S(1)}, u32[]{:S(2)}, u32[]{:S(2)}) collective-permute-start(bf16[2,128,256]{2,1,0:T(8,128)(2,1)S(1)} %get-tuple-element.40), channel_id=1, source_target_pairs={{0,128},{32,160},{64,192},{96,224},{128,256},{160,288},{192,320},{... | collective-permute-start | bytes 393224 | tf_op jit(solution)/shard_map/ppermute | solution.py:199
  120.2 4.3 %shard_map.100 = (f32[8,128,256]{2,1,0:T(8,128)S(1)}, f32[4,256,256]{2,1,0:T(8,128)S(1)}) custom-call(s32[16]{0:T(128)S(1)} %copy-done.46, s32[16]{0:T(128)S(1)} %dynamic-slice_reduce_fusion.2.dst, s32[16]{0:T(128)S(1)} %copy-done.44, s32[16]{0:T(128)S(1)} %copy-done.42, bf16[8,128,256]{2,1,0:T(8,128)(2,1)S(1)} %bitcast.13, ...), custom_call_target="tpu_custom_call" | custom-call | flops 536870912 | bytes 8388608 | tf_op jit(solution)/shard_map/pallas_call | solution.py:166
  124.7 4.9 %collective-permute-start.16 = (f32[4,16,8,256]{3,2,0,1:T(8,128)S(1)}, f32[4,16,8,256]{3,2,0,1:T(8,128)S(1)}, u32[]{:S(2)}, u32[]{:S(2)}) collective-permute-start(f32[4,16,8,256]{3,2,0,1:T(8,128)S(1)} %copy.15), channel_id=1, source_target_pairs={{0,16},{1,17},{2,18},{3,19},{4,20},{5,21},{6,22},{7,23},{8,24},{9,... | collective-permute-start | bytes 1572872 | tf_op jit(solution)/shard_map/ppermute | solution.py:181
  130.2 2.9 %collective-permute-start.14 = (bf16[2,128,256]{2,1,0:T(8,128)(2,1)S(1)}, bf16[2,128,256]{2,1,0:T(8,128)(2,1)S(1)}, u32[]{:S(2)}, u32[]{:S(2)}) collective-permute-start(bf16[2,128,256]{2,1,0:T(8,128)(2,1)S(1)} %get-tuple-element.41), channel_id=1, source_target_pairs={{0,64},{32,96},{64,128},{96,160},{128,192},{160,224},{192,256},{22... | collective-permute-start | bytes 393224 | tf_op jit(solution)/shard_map/ppermute | solution.py:199
  134.4 8.6 %collective-permute-done.16 = f32[4,16,8,256]{3,2,0,1:T(8,128)S(1)} collective-permute-done((f32[4,16,8,256]{3,2,0,1:T(8,128)S(1)}, f32[4,16,8,256]{3,2,0,1:T(8,128)S(1)}, u32[]{:S(2)}, u32[]{:S(2)}) %collective-permute-start.16) | collective-permute-done | bytes 524320 | tf_op jit(solution)/shard_map/ppermute | solution.py:181
  143.2 3.4 %collective-permute-start.17 = (f32[4,8,8,256]{3,2,0,1:T(8,128)S(1)}, f32[4,8,8,256]{3,2,0,1:T(8,128)S(1)}, u32[]{:S(2)}, u32[]{:S(2)}) collective-permute-start(f32[4,8,8,256]{3,2,0,1:T(8,128)S(1)} %constant_dynamic-slice_fusion.3), channel_id=1, source_target_pairs={{0,8},{1,9},{2,10},{3,11},{4,12},{5,13},{6,14},{7,15},{8,0},{9,1},... | collective-permute-start | bytes 786440 | tf_op jit(solution)/shard_map/ppermute | solution.py:181
  147.9 3.5 %collective-permute-done.17 = f32[4,8,8,256]{3,2,0,1:T(8,128)S(1)} collective-permute-done((f32[4,8,8,256]{3,2,0,1:T(8,128)S(1)}, f32[4,8,8,256]{3,2,0,1:T(8,128)S(1)}, u32[]{:S(2)}, u32[]{:S(2)}) %collective-permute-start.17) | collective-permute-done | bytes 262176 | tf_op jit(solution)/shard_map/ppermute | solution.py:181
  151.5 5.3 %collective-permute-start.18 = (f32[4,4,8,256]{3,2,0,1:T(8,128)S(1)}, f32[4,4,8,256]{3,2,0,1:T(8,128)S(1)}, u32[]{:S(2)}, u32[]{:S(2)}) collective-permute-start(f32[4,4,8,256]{3,2,0,1:T(8,128)S(1)} %constant_dynamic-slice_fusion.2), channel_id=1, source_target_pairs={{0,4},{1,5},{2,6},{3,7},{4,0},{5,1},{6,2},{7,3},{8,12},{9,13},{10,... | collective-permute-start | bytes 393224 | tf_op jit(solution)/shard_map/ppermute | solution.py:181
  157.5 1.9 %collective-permute-start.15 = (bf16[8,128,256]{2,1,0:T(8,128)(2,1)}, bf16[8,128,256]{2,1,0:T(8,128)(2,1)S(1)}, u32[]{:S(2)}, u32[]{:S(2)}) collective-permute-start(bf16[8,128,256]{2,1,0:T(8,128)(2,1)} %slice_dynamic-update-slice_fusion), channel_id=1, source_target_pairs={{0,32},{32,0},{64,96},{96,64},{128,160},{160,128},{192,224},{224,1... | collective-permute-start | bytes 1572872 | tf_op jit(solution)/shard_map/ppermute | solution.py:205
  159.4 3.0 %collective-permute-done.18 = f32[4,4,8,256]{3,2,0,1:T(8,128)S(1)} collective-permute-done((f32[4,4,8,256]{3,2,0,1:T(8,128)S(1)}, f32[4,4,8,256]{3,2,0,1:T(8,128)S(1)}, u32[]{:S(2)}, u32[]{:S(2)}) %collective-permute-start.18) | collective-permute-done | bytes 131104 | tf_op jit(solution)/shard_map/ppermute | solution.py:181
  162.5 3.8 %collective-permute-start.19 = (f32[4,2,8,256]{3,2,0,1:T(8,128)S(1)}, f32[4,2,8,256]{3,2,0,1:T(8,128)S(1)}, u32[]{:S(2)}, u32[]{:S(2)}) collective-permute-start(f32[4,2,8,256]{3,2,0,1:T(8,128)S(1)} %constant_dynamic-slice_fusion.1), channel_id=1, source_target_pairs={{0,2},{1,3},{2,0},{3,1},{4,6},{5,7},{6,4},{7,5},{8,10},{9,11},{10,... | collective-permute-start | bytes 196616 | tf_op jit(solution)/shard_map/ppermute | solution.py:181
  166.3 3.3 %collective-permute-done.19 = f32[4,2,8,256]{3,2,0,1:T(8,128)S(1)} collective-permute-done((f32[4,2,8,256]{3,2,0,1:T(8,128)S(1)}, f32[4,2,8,256]{3,2,0,1:T(8,128)S(1)}, u32[]{:S(2)}, u32[]{:S(2)}) %collective-permute-start.19) | collective-permute-done | bytes 65568 | tf_op jit(solution)/shard_map/ppermute | solution.py:181
  169.6 7.3 %collective-permute-start.20 = (f32[4,1,8,256]{3,2,0,1:T(8,128)S(1)}, f32[4,1,8,256]{3,2,0,1:T(8,128)S(1)}, u32[]{:S(2)}, u32[]{:S(2)}) collective-permute-start(f32[4,1,8,256]{3,2,0,1:T(8,128)S(1)} %constant_dynamic-slice_fusion), channel_id=1, source_target_pairs={{0,1},{1,0},{2,3},{3,2},{4,5},{5,4},{6,7},{7,6},{8,9},{9,8},{10,11... | collective-permute-start | bytes 98312 | tf_op jit(solution)/shard_map/ppermute | solution.py:181
  183.0 3.1 %shard_map.102 = f32[8,128,256]{2,1,0:T(8,128)} custom-call(s32[32]{0:T(128)S(1)} %select_reduce_fusion.idx.which, s32[32]{0:T(128)S(1)} %convert_element_type.3.wanted, f32[8,128,256]{2,1,0:T(8,128)S(1)} %shard_map.101.acc_in, bf16[32,128,256]{2,1,0:T(8,128)(2,1)} %all-to-all-done.1.back), custom_call_target="tpu_custom_call" | custom-call | flops 1048576 | bytes 4194304 | tf_op jit(solution)/shard_map/pallas_call | solution.py:187
  (171 shorter events, 42.7 us)
Async XLA Ops:
  5.6 65.0 %all-to-all-start = ((bf16[32,128,256]{2,1,0:T(8,128)(2,1)}), bf16[32,128,256]{2,1,0:T(8,128)(2,1)S(1)}, u32[]{:S(2)}, u32[]{:S(2)}) async-start(bf16[32,128,256]{2,1,0:T(8,128)(2,1)} %copy-done.1), calls=%async_computation | async-start | bytes 4194304 | tf_op jit(solution)/shard_map/all_to_all | solution.py:132
  15.9 50.7 %copy-start.49 = (s32[1,32,16]{1,2,0:T(8,128)S(1)}, s32[1,32,16]{1,2,0:T(8,128)}, u32[]{:S(2)}) copy-start(s32[1,32,16]{1,2,0:T(8,128)} %param.11) | copy-start | bytes 6148
  16.0 50.8 %copy-start.50 = (s32[1,32,16]{1,2,0:T(8,128)S(1)}, s32[1,32,16]{1,2,0:T(8,128)}, u32[]{:S(2)}) copy-start(s32[1,32,16]{1,2,0:T(8,128)} %param.13) | copy-start | bytes 6148
  16.0 50.8 %copy-start.51 = (s32[1,32,16]{1,2,0:T(8,128)S(1)}, s32[1,32,16]{1,2,0:T(8,128)}, u32[]{:S(2)}) copy-start(s32[1,32,16]{1,2,0:T(8,128)} %param.10) | copy-start | bytes 6148
  18.1 46.0 %copy-start.47 = (s32[16]{0:T(128)}, s32[16]{0:T(128)S(1)}, u32[]{:S(2)}) copy-start(s32[16]{0:T(128)S(1)} %and_select_fusion.1.idx) | copy-start | bytes 196
  18.7 25.7 %collective-permute-start = (bf16[2,128,256]{2,1,0:T(8,128)(2,1)S(1)}, bf16[2,128,256]{2,1,0:T(8,128)(2,1)S(1)}, u32[]{:S(2)}, u32[]{:S(2)}) collective-permute-start(bf16[2,128,256]{2,1,0:T(8,128)(2,1)S(1)} %get-tuple-element.25), channel_id=1, source_target_pairs={{0,64},{32,96},{64,128},{96,160},{128,192},{160,224},{192,256},{22... | collective-permute-start | bytes 393224 | tf_op jit(solution)/shard_map/ppermute | solution.py:199
  23.0 26.0 %collective-permute-start.1 = (bf16[2,128,256]{2,1,0:T(8,128)(2,1)S(1)}, bf16[2,128,256]{2,1,0:T(8,128)(2,1)S(1)}, u32[]{:S(2)}, u32[]{:S(2)}) collective-permute-start(bf16[2,128,256]{2,1,0:T(8,128)(2,1)S(1)} %get-tuple-element.26), channel_id=1, source_target_pairs={{0,128},{32,160},{64,192},{96,224},{128,256},{160,288},{192,320},{... | collective-permute-start | bytes 393224 | tf_op jit(solution)/shard_map/ppermute | solution.py:199
  30.3 23.0 %collective-permute-start.2 = (bf16[2,128,256]{2,1,0:T(8,128)(2,1)S(1)}, bf16[2,128,256]{2,1,0:T(8,128)(2,1)S(1)}, u32[]{:S(2)}, u32[]{:S(2)}) collective-permute-start(bf16[2,128,256]{2,1,0:T(8,128)(2,1)S(1)} %get-tuple-element.27), channel_id=1, source_target_pairs={{0,192},{32,224},{64,256},{96,288},{128,320},{160,352},{192,384},{... | collective-permute-start | bytes 393224 | tf_op jit(solution)/shard_map/ppermute | solution.py:199
  35.5 19.1 %collective-permute-start.3 = (bf16[2,128,256]{2,1,0:T(8,128)(2,1)S(1)}, bf16[2,128,256]{2,1,0:T(8,128)(2,1)S(1)}, u32[]{:S(2)}, u32[]{:S(2)}) collective-permute-start(bf16[2,128,256]{2,1,0:T(8,128)(2,1)S(1)} %get-tuple-element.28), channel_id=1, source_target_pairs={{0,256},{32,288},{64,320},{96,352},{128,384},{160,416},{192,448},{... | collective-permute-start | bytes 393224 | tf_op jit(solution)/shard_map/ppermute | solution.py:199
  37.4 18.4 %collective-permute-start.4 = (bf16[2,128,256]{2,1,0:T(8,128)(2,1)S(1)}, bf16[2,128,256]{2,1,0:T(8,128)(2,1)S(1)}, u32[]{:S(2)}, u32[]{:S(2)}) collective-permute-start(bf16[2,128,256]{2,1,0:T(8,128)(2,1)S(1)} %get-tuple-element.29), channel_id=1, source_target_pairs={{0,320},{32,352},{64,384},{96,416},{128,448},{160,480},{192,0},{22... | collective-permute-start | bytes 393224 | tf_op jit(solution)/shard_map/ppermute | solution.py:199
  44.4 17.6 %collective-permute-start.5 = (bf16[2,128,256]{2,1,0:T(8,128)(2,1)S(1)}, bf16[2,128,256]{2,1,0:T(8,128)(2,1)S(1)}, u32[]{:S(2)}, u32[]{:S(2)}) collective-permute-start(bf16[2,128,256]{2,1,0:T(8,128)(2,1)S(1)} %get-tuple-element.30), channel_id=1, source_target_pairs={{0,384},{32,416},{64,448},{96,480},{128,0},{160,32},{192,64},{224,... | collective-permute-start | bytes 393224 | tf_op jit(solution)/shard_map/ppermute | solution.py:199
  49.0 14.4 %collective-permute-start.6 = (bf16[2,128,256]{2,1,0:T(8,128)(2,1)S(1)}, bf16[2,128,256]{2,1,0:T(8,128)(2,1)S(1)}, u32[]{:S(2)}, u32[]{:S(2)}) collective-permute-start(bf16[2,128,256]{2,1,0:T(8,128)(2,1)S(1)} %get-tuple-element.31), channel_id=1, source_target_pairs={{0,448},{32,480},{64,0},{96,32},{128,64},{160,96},{192,128},{224,1... | collective-permute-start | bytes 393224 | tf_op jit(solution)/shard_map/ppermute | solution.py:199
  64.7 22.3 %collective-permute-start.7 = (bf16[8,128,256]{2,1,0:T(8,128)(2,1)}, bf16[8,128,256]{2,1,0:T(8,128)(2,1)}, u32[]{:S(2)}, u32[]{:S(2)}) collective-permute-start(bf16[8,128,256]{2,1,0:T(8,128)(2,1)} %slice_dynamic-update-slice_fusion.7), channel_id=1, source_target_pairs={{0,32},{32,0},{64,96},{96,64},{128,160},{160,128},{192,224},{224,1... | collective-permute-start | bytes 1572872 | tf_op jit(solution)/shard_map/ppermute | solution.py:205
  75.7 107.3 %all-to-all-start.1 = ((bf16[32,128,256]{2,1,0:T(8,128)(2,1)}), bf16[32,128,256]{2,1,0:T(8,128)(2,1)}, u32[]{:S(2)}, u32[]{:S(2)}) async-start(bf16[32,128,256]{2,1,0:T(8,128)(2,1)} %copy-done.6), calls=%async_computation.1 | async-start | bytes 4194304 | tf_op jit(solution)/shard_map/all_to_all | solution.py:161
  94.5 20.9 %collective-permute-start.8 = (bf16[2,128,256]{2,1,0:T(8,128)(2,1)S(1)}, bf16[2,128,256]{2,1,0:T(8,128)(2,1)S(1)}, u32[]{:S(2)}, u32[]{:S(2)}) collective-permute-start(bf16[2,128,256]{2,1,0:T(8,128)(2,1)S(1)} %get-tuple-element.35), channel_id=1, source_target_pairs={{0,448},{32,480},{64,0},{96,32},{128,64},{160,96},{192,128},{224,1... | collective-permute-start | bytes 393224 | tf_op jit(solution)/shard_map/ppermute | solution.py:199
  96.4 28.3 %collective-permute-start.9 = (bf16[2,128,256]{2,1,0:T(8,128)(2,1)S(1)}, bf16[2,128,256]{2,1,0:T(8,128)(2,1)S(1)}, u32[]{:S(2)}, u32[]{:S(2)}) collective-permute-start(bf16[2,128,256]{2,1,0:T(8,128)(2,1)S(1)} %get-tuple-element.36), channel_id=1, source_target_pairs={{0,384},{32,416},{64,448},{96,480},{128,0},{160,32},{192,64},{224,... | collective-permute-start | bytes 393224 | tf_op jit(solution)/shard_map/ppermute | solution.py:199
  100.9 29.3 %collective-permute-start.10 = (bf16[2,128,256]{2,1,0:T(8,128)(2,1)S(1)}, bf16[2,128,256]{2,1,0:T(8,128)(2,1)S(1)}, u32[]{:S(2)}, u32[]{:S(2)}) collective-permute-start(bf16[2,128,256]{2,1,0:T(8,128)(2,1)S(1)} %get-tuple-element.37), channel_id=1, source_target_pairs={{0,320},{32,352},{64,384},{96,416},{128,448},{160,480},{192,0},{22... | collective-permute-start | bytes 393224 | tf_op jit(solution)/shard_map/ppermute | solution.py:199
  106.2 27.5 %collective-permute-start.11 = (bf16[2,128,256]{2,1,0:T(8,128)(2,1)S(1)}, bf16[2,128,256]{2,1,0:T(8,128)(2,1)S(1)}, u32[]{:S(2)}, u32[]{:S(2)}) collective-permute-start(bf16[2,128,256]{2,1,0:T(8,128)(2,1)S(1)} %get-tuple-element.38), channel_id=1, source_target_pairs={{0,256},{32,288},{64,320},{96,352},{128,384},{160,416},{192,448},{... | collective-permute-start | bytes 393224 | tf_op jit(solution)/shard_map/ppermute | solution.py:199
  110.4 36.1 %collective-permute-start.12 = (bf16[2,128,256]{2,1,0:T(8,128)(2,1)S(1)}, bf16[2,128,256]{2,1,0:T(8,128)(2,1)S(1)}, u32[]{:S(2)}, u32[]{:S(2)}) collective-permute-start(bf16[2,128,256]{2,1,0:T(8,128)(2,1)S(1)} %get-tuple-element.39), channel_id=1, source_target_pairs={{0,192},{32,224},{64,256},{96,288},{128,320},{160,352},{192,384},{... | collective-permute-start | bytes 393224 | tf_op jit(solution)/shard_map/ppermute | solution.py:199
  115.4 31.8 %collective-permute-start.13 = (bf16[2,128,256]{2,1,0:T(8,128)(2,1)S(1)}, bf16[2,128,256]{2,1,0:T(8,128)(2,1)S(1)}, u32[]{:S(2)}, u32[]{:S(2)}) collective-permute-start(bf16[2,128,256]{2,1,0:T(8,128)(2,1)S(1)} %get-tuple-element.40), channel_id=1, source_target_pairs={{0,128},{32,160},{64,192},{96,224},{128,256},{160,288},{192,320},{... | collective-permute-start | bytes 393224 | tf_op jit(solution)/shard_map/ppermute | solution.py:199
  124.7 37.7 %copy-start.31 = (bf16[2,128,256]{2,1,0:T(8,128)(2,1)}, bf16[2,128,256]{2,1,0:T(8,128)(2,1)S(1)}, u32[]{:S(2)}) copy-start(bf16[2,128,256]{2,1,0:T(8,128)(2,1)S(1)} %collective-permute-done.9.refs_2_) | copy-start | bytes 393220
  124.7 18.3 %collective-permute-start.16 = (f32[4,16,8,256]{3,2,0,1:T(8,128)S(1)}, f32[4,16,8,256]{3,2,0,1:T(8,128)S(1)}, u32[]{:S(2)}, u32[]{:S(2)}) collective-permute-start(f32[4,16,8,256]{3,2,0,1:T(8,128)S(1)} %copy.15), channel_id=1, source_target_pairs={{0,16},{1,17},{2,18},{3,19},{4,20},{5,21},{6,22},{7,23},{8,24},{9,... | collective-permute-start | bytes 1572872 | tf_op jit(solution)/shard_map/ppermute | solution.py:181
  130.2 26.6 %collective-permute-start.14 = (bf16[2,128,256]{2,1,0:T(8,128)(2,1)S(1)}, bf16[2,128,256]{2,1,0:T(8,128)(2,1)S(1)}, u32[]{:S(2)}, u32[]{:S(2)}) collective-permute-start(bf16[2,128,256]{2,1,0:T(8,128)(2,1)S(1)} %get-tuple-element.41), channel_id=1, source_target_pairs={{0,64},{32,96},{64,128},{96,160},{128,192},{160,224},{192,256},{22... | collective-permute-start | bytes 393224 | tf_op jit(solution)/shard_map/ppermute | solution.py:199
  143.0 33.9 %copy-start.28 = (bf16[2,128,256]{2,1,0:T(8,128)(2,1)S(1)}, bf16[2,128,256]{2,1,0:T(8,128)(2,1)}, u32[]{:S(2)}) copy-start(bf16[2,128,256]{2,1,0:T(8,128)(2,1)} %copy-done.27) | copy-start | bytes 393220
  143.0 33.9 %copy-start.30 = (bf16[2,128,256]{2,1,0:T(8,128)(2,1)S(1)}, bf16[2,128,256]{2,1,0:T(8,128)(2,1)}, u32[]{:S(2)}) copy-start(bf16[2,128,256]{2,1,0:T(8,128)(2,1)} %copy-done.29) | copy-start | bytes 393220
  143.0 33.9 %copy-start.48 = (s32[16]{0:T(128)S(1)}, s32[16]{0:T(128)}, u32[]{:S(2)}) copy-start(s32[16]{0:T(128)} %copy-done.47) | copy-start | bytes 196
  143.1 33.8 %copy-start.52 = (pred[32]{0:T(512)(128)(4,1)S(1)}, pred[32]{0:T(512)(128)(4,1)}, u32[]{:S(2)}) copy-start(pred[32]{0:T(512)(128)(4,1)} %get-tuple-element.44) | copy-start | bytes 100
  143.2 8.3 %collective-permute-start.17 = (f32[4,8,8,256]{3,2,0,1:T(8,128)S(1)}, f32[4,8,8,256]{3,2,0,1:T(8,128)S(1)}, u32[]{:S(2)}, u32[]{:S(2)}) collective-permute-start(f32[4,8,8,256]{3,2,0,1:T(8,128)S(1)} %constant_dynamic-slice_fusion.3), channel_id=1, source_target_pairs={{0,8},{1,9},{2,10},{3,11},{4,12},{5,13},{6,14},{7,15},{8,0},{9,1},... | collective-permute-start | bytes 786440 | tf_op jit(solution)/shard_map/ppermute | solution.py:181
  151.5 10.9 %collective-permute-start.18 = (f32[4,4,8,256]{3,2,0,1:T(8,128)S(1)}, f32[4,4,8,256]{3,2,0,1:T(8,128)S(1)}, u32[]{:S(2)}, u32[]{:S(2)}) collective-permute-start(f32[4,4,8,256]{3,2,0,1:T(8,128)S(1)} %constant_dynamic-slice_fusion.2), channel_id=1, source_target_pairs={{0,4},{1,5},{2,6},{3,7},{4,0},{5,1},{6,2},{7,3},{8,12},{9,13},{10,... | collective-permute-start | bytes 393224 | tf_op jit(solution)/shard_map/ppermute | solution.py:181
  157.5 19.5 %collective-permute-start.15 = (bf16[8,128,256]{2,1,0:T(8,128)(2,1)}, bf16[8,128,256]{2,1,0:T(8,128)(2,1)S(1)}, u32[]{:S(2)}, u32[]{:S(2)}) collective-permute-start(bf16[8,128,256]{2,1,0:T(8,128)(2,1)} %slice_dynamic-update-slice_fusion), channel_id=1, source_target_pairs={{0,32},{32,0},{64,96},{96,64},{128,160},{160,128},{192,224},{224,1... | collective-permute-start | bytes 1572872 | tf_op jit(solution)/shard_map/ppermute | solution.py:205
  162.5 7.1 %collective-permute-start.19 = (f32[4,2,8,256]{3,2,0,1:T(8,128)S(1)}, f32[4,2,8,256]{3,2,0,1:T(8,128)S(1)}, u32[]{:S(2)}, u32[]{:S(2)}) collective-permute-start(f32[4,2,8,256]{3,2,0,1:T(8,128)S(1)} %constant_dynamic-slice_fusion.1), channel_id=1, source_target_pairs={{0,2},{1,3},{2,0},{3,1},{4,6},{5,7},{6,4},{7,5},{8,10},{9,11},{10,... | collective-permute-start | bytes 196616 | tf_op jit(solution)/shard_map/ppermute | solution.py:181
  169.6 12.7 %collective-permute-start.20 = (f32[4,1,8,256]{3,2,0,1:T(8,128)S(1)}, f32[4,1,8,256]{3,2,0,1:T(8,128)S(1)}, u32[]{:S(2)}, u32[]{:S(2)}) collective-permute-start(f32[4,1,8,256]{3,2,0,1:T(8,128)S(1)} %constant_dynamic-slice_fusion), channel_id=1, source_target_pairs={{0,1},{1,0},{2,3},{3,2},{4,5},{5,4},{6,7},{7,6},{8,9},{9,8},{10,11... | collective-permute-start | bytes 98312 | tf_op jit(solution)/shard_map/ppermute | solution.py:181
  (44 other events, 433.3 us)

commit v2 on v0

v2 whole, which is shorter than its diff:
```python
import jax
import jax.numpy as jnp
from jax import lax
from jax.experimental import pallas as pl
from jax.experimental.pallas import tpu as pltpu
from jax.sharding import PartitionSpec as P

D = 256
B = 128
NB_DEV = 8
TILES = 16
RELS = 4
F32 = jnp.float32
BF16 = jnp.bfloat16

PARAMS = pltpu.CompilerParams(vmem_limit_bytes=24 * 1024 * 1024)
VMEM = pl.BlockSpec(memory_space=pltpu.VMEM)
SMEM = pl.BlockSpec(memory_space=pltpu.SMEM)


def sds(*shape, dtype=BF16):
    return jax.ShapeDtypeStruct(shape, dtype)


def tiles(n):
    return sds(n, B, D)


def dot(a, b, dims):
    return lax.dot_general(a, b, (dims, ((), ())), preferred_element_type=F32)


NN = ((1,), (0,))
NT = ((1,), (1,))
TN = ((0,), (0,))


def call(body, ins, outs, mflops, scratch=(), alias=None):
    return pl.pallas_call(
        body,
        out_shape=outs,
        in_specs=ins,
        out_specs=jax.tree.map(lambda _: VMEM, outs),
        scratch_shapes=scratch,
        compiler_params=PARAMS,
        input_output_aliases=alias or {},
        cost_estimate=pl.CostEstimate(
            flops=mflops << 20, bytes_accessed=4 << 20, transcendentals=0
        ),
    )


def routes(z, c):
    sign = 1 - 2 * c

    def at(dz, core):
        return ((z + dz + 8) % 8) * 2 + core

    give, keep, org = [at(0, 1 - c)], [], [at(0, c), at(0, 1 - c)]
    for j in (1, 2, 3):
        give += [at(-sign * j, 1 - c), at(-sign * j, c)]
        keep += [at(sign * j, c), at(sign * j, 1 - c)]
        org += [at(-sign * j, c), at(-sign * j, 1 - c)]
    far = [at(4, c), at(4, 1 - c)]
    org += far[:1]
    for j in (1, 2, 3):
        org += [at(sign * j, 1 - c), at(sign * j, c)]
    return jnp.stack(give + keep + far + [at(0, c)]), jnp.stack(org + far[1:])


PLACE = (15, 0, 2, 1, 4, 3, 6, 5, 13, 8, 7, 10, 9, 12, 11, 14)


def swap(v):
    return lax.ppermute(v, "group", [(i, i ^ 1) for i in range(16)])


def zmove(v, j):
    pairs = []
    for a in range(8):
        pairs += [(a * 2, ((a + j) % 8) * 2), (a * 2 + 1, ((a - j) % 8) * 2 + 1)]
    return lax.ppermute(v, "group", pairs)


def mix_body(own, arrived, *outs):
    for j in range(3):
        outs[j][0] = own[2 * j]
        outs[j][1] = own[2 * j + 1]
        outs[j][2] = arrived[1 + 2 * j]
        outs[j][3] = arrived[2 + 2 * j]


def pack_body(arrived, r1, r2, r3, r4, packed, mine):
    mine[0] = arrived[0]
    for j, r in enumerate((r1, r2, r3)):
        packed[2 * j] = r[1]
        packed[2 * j + 1] = r[3]
        mine[1 + 2 * j] = r[0]
        mine[2 + 2 * j] = r[2]
    packed[6] = r4[1]
    mine[7] = r4[0]


def exchange(give, own, far):
    arrived = swap(give)
    sends = call(mix_body, [VMEM] * 2, [tiles(4)] * 3, 0)(own, arrived)
    got = [zmove(v, j + 1) for j, v in enumerate(sends)] + [zmove(far, 4)]
    packed, mine = call(pack_body, [VMEM] * 5, [tiles(7), tiles(8)], 0)(arrived, *got)
    return mine, swap(packed)


def slots(mine, last):
    return [(mine, i) for i in range(8)] + [(last, i) for i in range(7)]


ASKED, ORG, SRC, DST, REL, ORDER = (16 * i for i in range(6))


def pick_body(idx, blocks, out):
    for p in range(32):
        out[p] = blocks[idx[p]]


def pre_body(idx, blocks, give, own, far):
    n = 0
    for out in (give, own, far):
        for i in range(out.shape[0]):
            out[i] = blocks[idx[ASKED + idx[ORDER + n]]]
            n += 1


def tile_body(idx, blocks, rels, received, mask, mine, last, back, acc, gn, racc):
    acc[...] = jnp.zeros(acc.shape, F32)
    racc[...] = jnp.zeros(racc.shape, F32)
    stays = (blocks, idx[ASKED + idx[ORG]])
    for i, (ref, at) in enumerate([stays] + slots(mine, last)):
        k = idx[ORG + i]
        j, r, d = idx[SRC + k], idx[REL + k], idx[DST + k]
        own, op = blocks[j], rels[r]
        h = dot(own, op, NN).astype(BF16)
        both = jnp.concatenate([received[d], ref[at]], axis=0)
        scores = dot(h, both, NT)
        gp = -mask[k].astype(F32) * jax.nn.sigmoid(-scores[:, :B])
        gq = 0.125 * jax.nn.sigmoid(scores[:, B:])
        g = jnp.concatenate([gp, gq], axis=1).astype(BF16)
        gb = dot(g, h, TN).astype(BF16)
        back[d, :B] = gb[:B]
        gn[PLACE[i]] = gb[B:]
        gh = dot(g, both, NN).astype(BF16)
        acc[j] += dot(gh, op, NT)
        racc[r] += dot(own, gh, TN)
    for p in range(32):
        rows = [racc[r, 8 * p : 8 * p + 8] for r in range(RELS)]
        back[p, B:] = jnp.concatenate(rows, axis=0).astype(BF16)


def add_neg_body(idx, acc_in, gn, mine, last, acc):
    for i, (ref, at) in enumerate([(gn, 15)] + slots(mine, last)):
        acc[idx[ASKED + idx[ORG + i]]] += ref[at].astype(F32)


def add_dst_body(which, wanted, acc_in, back, acc, rel_out):
    rel_out[...] = jnp.zeros(rel_out.shape, F32)
    for p in range(32):
        rel_out[...] += back[p, B:].astype(F32)

        @pl.when(wanted[p] > 0)
        def _():
            acc[which[p]] += back[p, :B].astype(F32)


def per_device(entities, relations, src_block, dst_member, dst_block, rel_id, neg_block, pos_mask):
    me = lax.axis_index("member")
    grp = lax.axis_index("group")
    blocks = entities.reshape(NB_DEV, B, D)
    mask = pos_mask[0, 0]

    match = dst_member[0] == me
    wanted = jnp.any(match, axis=1).astype(jnp.int32)
    which = jnp.sum(jnp.where(match, dst_block[0], 0), axis=1)
    outgoing = call(pick_body, [SMEM, VMEM], tiles(32), 0)(which, blocks)
    received = lax.all_to_all(outgoing, "member", split_axis=0, concat_axis=0, tiled=True)

    src = lax.dynamic_index_in_dim(src_block[0], me, 0, keepdims=False)
    dst = lax.dynamic_index_in_dim(dst_member[0], me, 0, keepdims=False)
    rel = lax.dynamic_index_in_dim(rel_id[0], me, 0, keepdims=False)
    asked = lax.dynamic_index_in_dim(neg_block[:, 0, :], grp, 1, keepdims=False)
    order, org = routes(grp // 2, grp % 2)
    idx = jnp.concatenate([asked, org, src, dst, rel, order])

    sends = call(pre_body, [SMEM, VMEM], [tiles(7), tiles(6), tiles(2)], 0)(idx, blocks)
    mine, last = exchange(*sends)
    sums = sds(NB_DEV, B, D, dtype=F32)
    back, acc, gn = call(
        tile_body,
        [SMEM] + [VMEM] * 6,
        [sds(32, B + RELS * 8, D), sums, tiles(TILES)],
        1600,
        [pltpu.VMEM((RELS, D, D), F32)],
    )(idx, blocks, relations, received, mask, mine, last)
    back_in = lax.all_to_all(back, "member", split_axis=0, concat_axis=0, tiled=True)

    mine, last = exchange(gn[:7], gn[7:13], gn[13:15])
    acc = call(add_neg_body, [SMEM] + [VMEM] * 4, sums, 1, alias={1: 0})(
        idx, acc, gn, mine, last
    )
    back_in, acc = lax.optimization_barrier((back_in, acc))
    out, relation_grad = call(
        add_dst_body,
        [SMEM] * 2 + [VMEM] * 2,
        [sums, sds(RELS * 8, D, dtype=F32)],
        1,
        alias={2: 0},
    )(which, wanted, acc, back_in)
    return out.reshape(NB_DEV * B, D), relation_grad.reshape(RELS, 8, D)


def solution(mesh):
    placed = (
        P(("group", "member"), None),
        P("group", None, None),
        P("group", None, None),
        P("group", None, None),
        P("group", None, None),
        P("group", None, None),
        P(None, "member", None),
        P("group", "member", None, None, None),
    )
    return jax.shard_map(
        per_device,
        mesh=mesh,
        in_specs=placed,
        out_specs=(P(("group", "member"), None), P("group", "member", None)),
        check_vma=False,
    )
```

time: 358 us -> 152 us (0.42)
  the two profiles are of different devices: /device:TPU:64 before, /device:TPU:256 now
where the time goes in v2:
time: 152 us; the launch traced here: 151 us
  waiting for transfers between devices  63.4 us (42%)
  starting transfers between devices  57.6 us (38%)
  Pallas kernels  16.3 us (11%)
  local copies, waits for them, and re-layouts  11.5 us (8%)
    ppermute x8, starting transfers between devices, zmove(): return lax.ppermute(v, 'group', pairs)  33 us
    ppermute x8, waiting for transfers between devices, zmove(): return lax.ppermute(v, 'group', pairs)  24.3 us
    all_to_all x1, waiting for transfers between devices, per_device(): lax.all_to_all(back, 'member', split_axis=0, concat_axis=0, tiled=True)  23.3 us
    all_to_all x1, waiting for transfers between devices, per_device(): lax.all_to_all(outgoing, 'member', split_axis=0, concat_axis=0, tiled=True)  10.4 us
    all_to_all x1, starting transfers between devices, per_device(): lax.all_to_all(outgoing, 'member', split_axis=0, concat_axis=0, tiled=True)  10.1 us
    pallas_call x1, Pallas kernels, per_device(): call(tile_body, [SMEM] + [VMEM] * 6, [sds(32, B + RELS * 8, D), sums, til...  8.43 us
    unnamed x30, local copies, waits for them, and re-layouts  8.39 us
    ppermute x4, starting transfers between devices, swap(): return lax.ppermute(v, 'group', [(i, i ^ 1) for i in range(16)])  8.34 us
  transfers between devices with their start and end apart: 14, of which 8 were waited for; matrix products, arithmetic and copies ran while one was open for 2% of the time, Pallas kernels for 2%

profile of v2, /device:TPU:256, one launch (start us, length us, event | category | flops | bytes accessed | tf_op | source)
XLA Modules:
  0.0 151.4 jit_solution(10275762113820085874)
XLA Ops:
  2.1 1.0 copy-done.4
  3.1 2.0 %shard_map.95 = bf16[32,128,256]{2,1,0:T(8,128)(2,1)} custom-call(s32[32]{0:T(128)S(1)} %select_reduce_fusion.idx.which, bf16[8,128,256]{2,1,0:T(8,128)(2,1)S(1)} %bitcast.20), custom_call_target="tpu_custom_call" | custom-call | bytes 4194304 | tf_op jit(solution)/shard_map/pallas_call | solution.py:181
  5.1 10.1 %all-to-all-start = ((bf16[32,128,256]{2,1,0:T(8,128)(2,1)}), bf16[32,128,256]{2,1,0:T(8,128)(2,1)S(1)}, u32[]{:S(2)}, u32[]{:S(2)}) async-start(bf16[32,128,256]{2,1,0:T(8,128)(2,1)} %shard_map.95), calls=%async_computation | async-start | bytes 4194304 | tf_op jit(solution)/shard_map/all_to_all | solution.py:182
  17.0 1.9 %collective-permute-start = (bf16[7,128,256]{2,1,0:T(8,128)(2,1)S(1)}, bf16[7,128,256]{2,1,0:T(8,128)(2,1)S(1)}, u32[]{:S(2)}, u32[]{:S(2)}) collective-permute-start(bf16[7,128,256]{2,1,0:T(8,128)(2,1)S(1)} %get-tuple-element.22), channel_id=1, source_target_pairs={{0,32},{32,0},{64,96},{96,64},{128,160},{160,128},{192,224},{224,1... | collective-permute-start | bytes 1376264 | tf_op jit(solution)/shard_map/ppermute | solution.py:75
  19.0 1.8 %collective-permute-done.arrived = bf16[7,128,256]{2,1,0:T(8,128)(2,1)S(1)} collective-permute-done((bf16[7,128,256]{2,1,0:T(8,128)(2,1)S(1)}, bf16[7,128,256]{2,1,0:T(8,128)(2,1)S(1)}, u32[]{:S(2)}, u32[]{:S(2)}) %collective-permute-start) | collective-permute-done | bytes 458784 | tf_op jit(solution)/shard_map/ppermute | solution.py:75
  20.8 3.4 %collective-permute-start.1 = (bf16[4,128,256]{2,1,0:T(8,128)(2,1)S(1)}, bf16[4,128,256]{2,1,0:T(8,128)(2,1)S(1)}, u32[]{:S(2)}, u32[]{:S(2)}) collective-permute-start(bf16[4,128,256]{2,1,0:T(8,128)(2,1)S(1)} %get-tuple-element.24), channel_id=1, source_target_pairs={{0,64},{32,480},{64,128},{96,32},{128,192},{160,96},{192,256},{224... | collective-permute-start | bytes 786440 | tf_op jit(solution)/shard_map/ppermute | solution.py:82
  24.2 4.3 %collective-permute-start.2 = (bf16[4,128,256]{2,1,0:T(8,128)(2,1)S(1)}, bf16[4,128,256]{2,1,0:T(8,128)(2,1)S(1)}, u32[]{:S(2)}, u32[]{:S(2)}) collective-permute-start(bf16[4,128,256]{2,1,0:T(8,128)(2,1)S(1)} %get-tuple-element.25), channel_id=1, source_target_pairs={{0,128},{32,416},{64,192},{96,480},{128,256},{160,32},{192,320},{2... | collective-permute-start | bytes 786440 | tf_op jit(solution)/shard_map/ppermute | solution.py:82
  28.5 1.9 %collective-permute-start.3 = (bf16[4,128,256]{2,1,0:T(8,128)(2,1)S(1)}, bf16[4,128,256]{2,1,0:T(8,128)(2,1)S(1)}, u32[]{:S(2)}, u32[]{:S(2)}) collective-permute-start(bf16[4,128,256]{2,1,0:T(8,128)(2,1)S(1)} %get-tuple-element.26), channel_id=1, source_target_pairs={{0,192},{32,352},{64,256},{96,416},{128,320},{160,480},{192,384},{... | collective-permute-start | bytes 786440 | tf_op jit(solution)/shard_map/ppermute | solution.py:82
  30.4 6.9 %collective-permute-start.4 = (bf16[2,128,256]{2,1,0:T(8,128)(2,1)S(1)}, bf16[2,128,256]{2,1,0:T(8,128)(2,1)S(1)}, u32[]{:S(2)}, u32[]{:S(2)}) collective-permute-start(bf16[2,128,256]{2,1,0:T(8,128)(2,1)S(1)} %get-tuple-element.27), channel_id=1, source_target_pairs={{0,256},{32,288},{64,320},{96,352},{128,384},{160,416},{192,448},{... | collective-permute-start | bytes 393224 | tf_op jit(solution)/shard_map/ppermute | solution.py:82
  37.4 12.2 %collective-permute-done.4.r4 = bf16[2,128,256]{2,1,0:T(8,128)(2,1)S(1)} collective-permute-done((bf16[2,128,256]{2,1,0:T(8,128)(2,1)S(1)}, bf16[2,128,256]{2,1,0:T(8,128)(2,1)S(1)}, u32[]{:S(2)}, u32[]{:S(2)}) %collective-permute-start.4) | collective-permute-done | bytes 131104 | tf_op jit(solution)/shard_map/ppermute | solution.py:82
  50.4 2.2 %collective-permute-start.5 = (bf16[7,128,256]{2,1,0:T(8,128)(2,1)S(1)}, bf16[7,128,256]{2,1,0:T(8,128)(2,1)S(1)}, u32[]{:S(2)}, u32[]{:S(2)}) collective-permute-start(bf16[7,128,256]{2,1,0:T(8,128)(2,1)S(1)} %get-tuple-element.29), channel_id=1, source_target_pairs={{0,32},{32,0},{64,96},{96,64},{128,160},{160,128},{192,224},{224,1... | collective-permute-start | bytes 1376264 | tf_op jit(solution)/shard_map/ppermute | solution.py:75
  52.7 1.5 collective-permute-done.5.last
  54.9 10.4 %all-to-all-done.received = bf16[32,128,256]{2,1,0:T(8,128)(2,1)S(1)} async-done(((bf16[32,128,256]{2,1,0:T(8,128)(2,1)}), bf16[32,128,256]{2,1,0:T(8,128)(2,1)S(1)}, u32[]{:S(2)}, u32[]{:S(2)}) %all-to-all-start) | async-done | bytes 2097184 | tf_op jit(solution)/shard_map/all_to_all | solution.py:182
  65.3 1.2 copy-done.6
  66.5 1.0 copy-done.9
  67.6 1.0 copy-done.11
  68.6 8.4 %shard_map.99 = (bf16[32,160,256]{2,1,0:T(8,128)(2,1)S(1)}, f32[8,128,256]{2,1,0:T(8,128)}, bf16[16,128,256]{2,1,0:T(8,128)(2,1)S(1)}) custom-call(s32[96]{0:T(128)S(1)} %concatenate.3.idx, bf16[8,128,256]{2,1,0:T(8,128)(2,1)S(1)} %bitcast.22, bf16[4,256,256]{2,1,0:T(8,128)(2,1)S(1)} %copy-done.7, bf16[32,128,256]{2,1,0:T(8,128)(2,1)S(1)} %all-to-all-done.received, ...), custom_call_target="tpu_custom_call" | custom-call | flops 1677721600 | bytes 4194304 | tf_op jit(solution)/shard_map/pallas_call | solution.py:194
  78.0 1.5 copy-done.3
  79.5 6.1 %all-to-all-start.1 = ((bf16[32,160,256]{2,1,0:T(8,128)(2,1)}), bf16[32,160,256]{2,1,0:T(8,128)(2,1)S(1)}, u32[]{:S(2)}, u32[]{:S(2)}) async-start(bf16[32,160,256]{2,1,0:T(8,128)(2,1)} %copy-done.3), calls=%async_computation.1 | async-start | bytes 5242880 | tf_op jit(solution)/shard_map/all_to_all | solution.py:201
  85.6 1.1 slice.9
  86.8 1.9 %collective-permute-start.6 = (bf16[7,128,256]{2,1,0:T(8,128)(2,1)S(1)}, bf16[7,128,256]{2,1,0:T(8,128)(2,1)S(1)}, u32[]{:S(2)}, u32[]{:S(2)}) collective-permute-start(bf16[7,128,256]{2,1,0:T(8,128)(2,1)S(1)} %slice.9), channel_id=1, source_target_pairs={{0,32},{32,0},{64,96},{96,64},{128,160},{160,128},{192,224},{224,1... | collective-permute-start | bytes 1376264 | tf_op jit(solution)/shard_map/ppermute | solution.py:75
  88.7 1.0 slice.10.own
  90.5 3.4 %collective-permute-start.7 = (bf16[4,128,256]{2,1,0:T(8,128)(2,1)S(1)}, bf16[4,128,256]{2,1,0:T(8,128)(2,1)S(1)}, u32[]{:S(2)}, u32[]{:S(2)}) collective-permute-start(bf16[4,128,256]{2,1,0:T(8,128)(2,1)S(1)} %get-tuple-element.33), channel_id=1, source_target_pairs={{0,64},{32,480},{64,128},{96,32},{128,192},{160,96},{192,256},{224... | collective-permute-start | bytes 786440 | tf_op jit(solution)/shard_map/ppermute | solution.py:82
  93.9 4.3 %collective-permute-start.8 = (bf16[4,128,256]{2,1,0:T(8,128)(2,1)S(1)}, bf16[4,128,256]{2,1,0:T(8,128)(2,1)S(1)}, u32[]{:S(2)}, u32[]{:S(2)}) collective-permute-start(bf16[4,128,256]{2,1,0:T(8,128)(2,1)S(1)} %get-tuple-element.34), channel_id=1, source_target_pairs={{0,128},{32,416},{64,192},{96,480},{128,256},{160,32},{192,320},{2... | collective-permute-start | bytes 786440 | tf_op jit(solution)/shard_map/ppermute | solution.py:82
  98.2 1.9 %collective-permute-start.9 = (bf16[4,128,256]{2,1,0:T(8,128)(2,1)S(1)}, bf16[4,128,256]{2,1,0:T(8,128)(2,1)S(1)}, u32[]{:S(2)}, u32[]{:S(2)}) collective-permute-start(bf16[4,128,256]{2,1,0:T(8,128)(2,1)S(1)} %get-tuple-element.35), channel_id=1, source_target_pairs={{0,192},{32,352},{64,256},{96,416},{128,320},{160,480},{192,384},{... | collective-permute-start | bytes 786440 | tf_op jit(solution)/shard_map/ppermute | solution.py:82
  100.2 6.9 %collective-permute-start.10 = (bf16[2,128,256]{2,1,0:T(8,128)(2,1)S(1)}, bf16[2,128,256]{2,1,0:T(8,128)(2,1)S(1)}, u32[]{:S(2)}, u32[]{:S(2)}) collective-permute-start(bf16[2,128,256]{2,1,0:T(8,128)(2,1)S(1)} %slice.11), channel_id=1, source_target_pairs={{0,256},{32,288},{64,320},{96,352},{128,384},{160,416},{192,448},{... | collective-permute-start | bytes 393224 | tf_op jit(solution)/shard_map/ppermute | solution.py:82
  107.1 12.1 %collective-permute-done.10.r4 = bf16[2,128,256]{2,1,0:T(8,128)(2,1)S(1)} collective-permute-done((bf16[2,128,256]{2,1,0:T(8,128)(2,1)S(1)}, bf16[2,128,256]{2,1,0:T(8,128)(2,1)S(1)}, u32[]{:S(2)}, u32[]{:S(2)}) %collective-permute-start.10) | collective-permute-done | bytes 131104 | tf_op jit(solution)/shard_map/ppermute | solution.py:82
  119.3 2.3 %collective-permute-start.11 = (bf16[7,128,256]{2,1,0:T(8,128)(2,1)S(1)}, bf16[7,128,256]{2,1,0:T(8,128)(2,1)S(1)}, u32[]{:S(2)}, u32[]{:S(2)}) collective-permute-start(bf16[7,128,256]{2,1,0:T(8,128)(2,1)S(1)} %get-tuple-element.37), channel_id=1, source_target_pairs={{0,32},{32,0},{64,96},{96,64},{128,160},{160,128},{192,224},{224,1... | collective-permute-start | bytes 1376264 | tf_op jit(solution)/shard_map/ppermute | solution.py:75
  121.6 1.4 collective-permute-done.11.last
  123.0 2.4 %shard_map.102.acc_in = f32[8,128,256]{2,1,0:T(8,128)} custom-call(s32[96]{0:T(128)S(1)} %concatenate.3.idx, f32[8,128,256]{2,1,0:T(8,128)} %get-tuple-element.31.acc_in, bf16[16,128,256]{2,1,0:T(8,128)(2,1)S(1)} %copy-done.2, bf16[8,128,256]{2,1,0:T(8,128)(2,1)S(1)} %get-tuple-element.36.mine, ...), custom_call_target="tpu_custom_call", output_to_operand_aliasing={{}: (1, {})} | custom-call | flops 1048576 | bytes 4194304 | tf_op jit(solution)/shard_map/pallas_call | solution.py:204
  125.5 23.3 %all-to-all-done.1.back = bf16[32,160,256]{2,1,0:T(8,128)(2,1)S(1)} async-done(((bf16[32,160,256]{2,1,0:T(8,128)(2,1)}), bf16[32,160,256]{2,1,0:T(8,128)(2,1)S(1)}, u32[]{:S(2)}, u32[]{:S(2)}) %all-to-all-start.1) | async-done | bytes 2621472 | tf_op jit(solution)/shard_map/all_to_all | solution.py:201
  148.8 2.6 %shard_map.103 = (f32[8,128,256]{2,1,0:T(8,128)}, f32[32,256]{1,0:T(8,128)}) custom-call(s32[32]{0:T(128)S(1)} %select_reduce_fusion.idx.which, s32[32]{0:T(128)S(1)} %convert_element_type.3.wanted, f32[8,128,256]{2,1,0:T(8,128)} %shard_map.102.acc_in, bf16[32,160,256]{2,1,0:T(8,128)(2,1)S(1)} %all-to-all-done.1.back), custom_call_target="tpu_custom_call", output_to_operand_aliasing={{0}: (2, {})} | custom-call | flops 1048576 | bytes 4194304 | tf_op jit(solution)/shard_map/pallas_call | solution.py:208
  (45 shorter events, 6.6 us)
Async XLA Ops:
  0.6 14.8 %copy-start = (s32[1,32,16]{1,2,0:T(8,128)S(1)}, s32[1,32,16]{1,2,0:T(8,128)}, u32[]{:S(2)}) copy-start(s32[1,32,16]{1,2,0:T(8,128)} %param.10) | copy-start | bytes 6148
  2.1 1.0 copy-start.4
  5.1 10.5 %copy-start.12 = (s32[1,32,16]{1,2,0:T(8,128)S(1)}, s32[1,32,16]{1,2,0:T(8,128)}, u32[]{:S(2)}) copy-start(s32[1,32,16]{1,2,0:T(8,128)} %param.11) | copy-start | bytes 6148
  5.1 10.5 %copy-start.14 = (s32[1,32,16]{1,2,0:T(8,128)S(1)}, s32[1,32,16]{1,2,0:T(8,128)}, u32[]{:S(2)}) copy-start(s32[1,32,16]{1,2,0:T(8,128)} %param.13) | copy-start | bytes 6148
  5.1 10.7 %copy-start.13 = (s32[16,1,16]{2,1,0:T(1,128)S(1)}, s32[16,1,16]{2,1,0:T(1,128)}, u32[]{:S(2)}) copy-start(s32[16,1,16]{2,1,0:T(1,128)} %param.14) | copy-start | bytes 3076
  5.1 11.3 %copy-start.5 = (bf16[1024,256]{1,0:T(8,128)(2,1)S(1)}, bf16[1024,256]{1,0:T(8,128)(2,1)}, u32[]{:S(2)}) copy-start(bf16[1024,256]{1,0:T(8,128)(2,1)} %param.8) | copy-start | bytes 1572868
  5.1 60.1 %all-to-all-start = ((bf16[32,128,256]{2,1,0:T(8,128)(2,1)}), bf16[32,128,256]{2,1,0:T(8,128)(2,1)S(1)}, u32[]{:S(2)}, u32[]{:S(2)}) async-start(bf16[32,128,256]{2,1,0:T(8,128)(2,1)} %shard_map.95), calls=%async_computation | async-start | bytes 4194304 | tf_op jit(solution)/shard_map/all_to_all | solution.py:182
  15.2 50.0 %copy-start.7 = (bf16[4,256,256]{2,1,0:T(8,128)(2,1)S(1)}, bf16[4,256,256]{2,1,0:T(8,128)(2,1)}, u32[]{:S(2)}) copy-start(bf16[4,256,256]{2,1,0:T(8,128)(2,1)} %rels.1) | copy-start | bytes 1572868
  17.0 3.7 %collective-permute-start = (bf16[7,128,256]{2,1,0:T(8,128)(2,1)S(1)}, bf16[7,128,256]{2,1,0:T(8,128)(2,1)S(1)}, u32[]{:S(2)}, u32[]{:S(2)}) collective-permute-start(bf16[7,128,256]{2,1,0:T(8,128)(2,1)S(1)} %get-tuple-element.22), channel_id=1, source_target_pairs={{0,32},{32,0},{64,96},{96,64},{128,160},{160,128},{192,224},{224,1... | collective-permute-start | bytes 1376264 | tf_op jit(solution)/shard_map/ppermute | solution.py:75
  20.8 28.7 %collective-permute-start.1 = (bf16[4,128,256]{2,1,0:T(8,128)(2,1)S(1)}, bf16[4,128,256]{2,1,0:T(8,128)(2,1)S(1)}, u32[]{:S(2)}, u32[]{:S(2)}) collective-permute-start(bf16[4,128,256]{2,1,0:T(8,128)(2,1)S(1)} %get-tuple-element.24), channel_id=1, source_target_pairs={{0,64},{32,480},{64,128},{96,32},{128,192},{160,96},{192,256},{224... | collective-permute-start | bytes 786440 | tf_op jit(solution)/shard_map/ppermute | solution.py:82
  24.2 25.3 %collective-permute-start.2 = (bf16[4,128,256]{2,1,0:T(8,128)(2,1)S(1)}, bf16[4,128,256]{2,1,0:T(8,128)(2,1)S(1)}, u32[]{:S(2)}, u32[]{:S(2)}) collective-permute-start(bf16[4,128,256]{2,1,0:T(8,128)(2,1)S(1)} %get-tuple-element.25), channel_id=1, source_target_pairs={{0,128},{32,416},{64,192},{96,480},{128,256},{160,32},{192,320},{2... | collective-permute-start | bytes 786440 | tf_op jit(solution)/shard_map/ppermute | solution.py:82
  28.5 21.0 %collective-permute-start.3 = (bf16[4,128,256]{2,1,0:T(8,128)(2,1)S(1)}, bf16[4,128,256]{2,1,0:T(8,128)(2,1)S(1)}, u32[]{:S(2)}, u32[]{:S(2)}) collective-permute-start(bf16[4,128,256]{2,1,0:T(8,128)(2,1)S(1)} %get-tuple-element.26), channel_id=1, source_target_pairs={{0,192},{32,352},{64,256},{96,416},{128,320},{160,480},{192,384},{... | collective-permute-start | bytes 786440 | tf_op jit(solution)/shard_map/ppermute | solution.py:82
  30.4 19.1 %collective-permute-start.4 = (bf16[2,128,256]{2,1,0:T(8,128)(2,1)S(1)}, bf16[2,128,256]{2,1,0:T(8,128)(2,1)S(1)}, u32[]{:S(2)}, u32[]{:S(2)}) collective-permute-start(bf16[2,128,256]{2,1,0:T(8,128)(2,1)S(1)} %get-tuple-element.27), channel_id=1, source_target_pairs={{0,256},{32,288},{64,320},{96,352},{128,384},{160,416},{192,448},{... | collective-permute-start | bytes 393224 | tf_op jit(solution)/shard_map/ppermute | solution.py:82
  49.6 0.8 copy-start.8
  50.4 3.7 %collective-permute-start.5 = (bf16[7,128,256]{2,1,0:T(8,128)(2,1)S(1)}, bf16[7,128,256]{2,1,0:T(8,128)(2,1)S(1)}, u32[]{:S(2)}, u32[]{:S(2)}) collective-permute-start(bf16[7,128,256]{2,1,0:T(8,128)(2,1)S(1)} %get-tuple-element.29), channel_id=1, source_target_pairs={{0,32},{32,0},{64,96},{96,64},{128,160},{160,128},{192,224},{224,1... | collective-permute-start | bytes 1376264 | tf_op jit(solution)/shard_map/ppermute | solution.py:75
  54.1 0.8 copy-start.10
  65.3 1.2 copy-start.6
  66.5 1.0 copy-start.9
  67.6 1.0 copy-start.11
  77.0 1.0 copy-start.1
  78.0 1.5 copy-start.3
  79.5 69.3 %all-to-all-start.1 = ((bf16[32,160,256]{2,1,0:T(8,128)(2,1)}), bf16[32,160,256]{2,1,0:T(8,128)(2,1)S(1)}, u32[]{:S(2)}, u32[]{:S(2)}) async-start(bf16[32,160,256]{2,1,0:T(8,128)(2,1)} %copy-done.3), calls=%async_computation.1 | async-start | bytes 5242880 | tf_op jit(solution)/shard_map/all_to_all | solution.py:201
  85.6 14.5 %copy-start.2 = (bf16[16,128,256]{2,1,0:T(8,128)(2,1)S(1)}, bf16[16,128,256]{2,1,0:T(8,128)(2,1)}, u32[]{:S(2)}) copy-start(bf16[16,128,256]{2,1,0:T(8,128)(2,1)} %copy-done.1) | copy-start | bytes 3145732
  86.8 3.7 %collective-permute-start.6 = (bf16[7,128,256]{2,1,0:T(8,128)(2,1)S(1)}, bf16[7,128,256]{2,1,0:T(8,128)(2,1)S(1)}, u32[]{:S(2)}, u32[]{:S(2)}) collective-permute-start(bf16[7,128,256]{2,1,0:T(8,128)(2,1)S(1)} %slice.9), channel_id=1, source_target_pairs={{0,32},{32,0},{64,96},{96,64},{128,160},{160,128},{192,224},{224,1... | collective-permute-start | bytes 1376264 | tf_op jit(solution)/shard_map/ppermute | solution.py:75
  90.5 28.7 %collective-permute-start.7 = (bf16[4,128,256]{2,1,0:T(8,128)(2,1)S(1)}, bf16[4,128,256]{2,1,0:T(8,128)(2,1)S(1)}, u32[]{:S(2)}, u32[]{:S(2)}) collective-permute-start(bf16[4,128,256]{2,1,0:T(8,128)(2,1)S(1)} %get-tuple-element.33), channel_id=1, source_target_pairs={{0,64},{32,480},{64,128},{96,32},{128,192},{160,96},{192,256},{224... | collective-permute-start | bytes 786440 | tf_op jit(solution)/shard_map/ppermute | solution.py:82
  93.9 25.3 %collective-permute-start.8 = (bf16[4,128,256]{2,1,0:T(8,128)(2,1)S(1)}, bf16[4,128,256]{2,1,0:T(8,128)(2,1)S(1)}, u32[]{:S(2)}, u32[]{:S(2)}) collective-permute-start(bf16[4,128,256]{2,1,0:T(8,128)(2,1)S(1)} %get-tuple-element.34), channel_id=1, source_target_pairs={{0,128},{32,416},{64,192},{96,480},{128,256},{160,32},{192,320},{2... | collective-permute-start | bytes 786440 | tf_op jit(solution)/shard_map/ppermute | solution.py:82
  98.2 21.0 %collective-permute-start.9 = (bf16[4,128,256]{2,1,0:T(8,128)(2,1)S(1)}, bf16[4,128,256]{2,1,0:T(8,128)(2,1)S(1)}, u32[]{:S(2)}, u32[]{:S(2)}) collective-permute-start(bf16[4,128,256]{2,1,0:T(8,128)(2,1)S(1)} %get-tuple-element.35), channel_id=1, source_target_pairs={{0,192},{32,352},{64,256},{96,416},{128,320},{160,480},{192,384},{... | collective-permute-start | bytes 786440 | tf_op jit(solution)/shard_map/ppermute | solution.py:82
  100.2 19.1 %collective-permute-start.10 = (bf16[2,128,256]{2,1,0:T(8,128)(2,1)S(1)}, bf16[2,128,256]{2,1,0:T(8,128)(2,1)S(1)}, u32[]{:S(2)}, u32[]{:S(2)}) collective-permute-start(bf16[2,128,256]{2,1,0:T(8,128)(2,1)S(1)} %slice.11), channel_id=1, source_target_pairs={{0,256},{32,288},{64,320},{96,352},{128,384},{160,416},{192,448},{... | collective-permute-start | bytes 393224 | tf_op jit(solution)/shard_map/ppermute | solution.py:82
  119.3 3.7 %collective-permute-start.11 = (bf16[7,128,256]{2,1,0:T(8,128)(2,1)S(1)}, bf16[7,128,256]{2,1,0:T(8,128)(2,1)S(1)}, u32[]{:S(2)}, u32[]{:S(2)}) collective-permute-start(bf16[7,128,256]{2,1,0:T(8,128)(2,1)S(1)} %get-tuple-element.37), channel_id=1, source_target_pairs={{0,32},{32,0},{64,96},{96,64},{128,160},{160,128},{192,224},{224,1... | collective-permute-start | bytes 1376264 | tf_op jit(solution)/shard_map/ppermute | solution.py:75

commit v3 on v2

--- a/solution.py
+++ b/solution.py
@@ -35,7 +35,7 @@
 TN = ((0,), (0,))
 
 
-def call(body, ins, outs, mflops, scratch=(), alias=None):
+def call(body, ins, outs, mflops, scratch=()):
     return pl.pallas_call(
         body,
         out_shape=outs,
@@ -43,7 +43,6 @@
         out_specs=jax.tree.map(lambda _: VMEM, outs),
         scratch_shapes=scratch,
         compiler_params=PARAMS,
-        input_output_aliases=alias or {},
         cost_estimate=pl.CostEstimate(
             flops=mflops << 20, bytes_accessed=4 << 20, transcendentals=0
         ),
@@ -116,9 +115,9 @@
 ASKED, ORG, SRC, DST, REL, ORDER = (16 * i for i in range(6))
 
 
-def pick_body(idx, blocks, out):
+def pick_body(code, blocks, out):
     for p in range(32):
-        out[p] = blocks[idx[p]]
+        out[p] = blocks[jnp.maximum(code[p] - 1, 0)]
 
 
 def pre_body(idx, blocks, give, own, far):
@@ -129,44 +128,74 @@
             n += 1
 
 
-def tile_body(idx, blocks, rels, received, mask, mine, last, back, acc, gn, racc):
+def stage_body(idx, blocks, rels, mask, mine, last, stage, h_v):
+    stays = (blocks, idx[ASKED + idx[ORG]])
+    work = []
+    for i, (ref, at) in enumerate([stays] + slots(mine, last)):
+        k = idx[ORG + i]
+        work.append((i, k, idx[SRC + k], idx[REL + k], ref, at))
+    for i, k, j, r, ref, at in work:
+        h_v[i] = dot(blocks[j], rels[r], NN).astype(BF16)
+    for i, k, j, r, ref, at in work:
+        neg = ref[at]
+        stage[i] = neg
+        gq = 0.125 * jax.nn.sigmoid(dot(h_v[i], neg, NT))
+        pair = [mask[k].astype(F32), gq]
+        stage[TILES + i] = jnp.concatenate(pair, axis=1).astype(BF16)
+
+
+def tile_body(idx, blocks, rels, received, stage, back, acc, racc, h_v, g_v, gh_v):
+    work = []
+    for i in range(TILES):
+        k = idx[ORG + i]
+        work.append((i, idx[SRC + k], idx[REL + k], idx[DST + k]))
     acc[...] = jnp.zeros(acc.shape, F32)
     racc[...] = jnp.zeros(racc.shape, F32)
-    stays = (blocks, idx[ASKED + idx[ORG]])
-    for i, (ref, at) in enumerate([stays] + slots(mine, last)):
-        k = idx[ORG + i]
-        j, r, d = idx[SRC + k], idx[REL + k], idx[DST + k]
-        own, op = blocks[j], rels[r]
-        h = dot(own, op, NN).astype(BF16)
-        both = jnp.concatenate([received[d], ref[at]], axis=0)
-        scores = dot(h, both, NT)
-        gp = -mask[k].astype(F32) * jax.nn.sigmoid(-scores[:, :B])
-        gq = 0.125 * jax.nn.sigmoid(scores[:, B:])
-        g = jnp.concatenate([gp, gq], axis=1).astype(BF16)
-        gb = dot(g, h, TN).astype(BF16)
-        back[d, :B] = gb[:B]
-        gn[PLACE[i]] = gb[B:]
-        gh = dot(g, both, NN).astype(BF16)
-        acc[j] += dot(gh, op, NT)
-        racc[r] += dot(own, gh, TN)
+    for i, j, r, d in work:
+        h_v[i] = dot(blocks[j], rels[r], NN).astype(BF16)
+    for i, j, r, d in work:
+        mask = stage[TILES + i, :, :B].astype(F32)
+        gp = -mask * jax.nn.sigmoid(-dot(h_v[i], received[d], NT))
+        g_v[i, :, :B] = gp.astype(BF16)
+        g_v[i, :, B:] = stage[TILES + i, :, B:]
+    for i, j, r, d in work:
+        both = jnp.concatenate([received[d], stage[i]], axis=0)
+        gh_v[i] = dot(g_v[i], both, NN).astype(BF16)
+    for i, j, r, d in work:
+        back[d, :B] = dot(g_v[i, :, :B], h_v[i], TN).astype(BF16)
+    for i, j, r, d in work:
+        racc[r] += dot(blocks[j], gh_v[i], TN)
+        acc[j] += dot(gh_v[i], rels[r], NT)
     for p in range(32):
         rows = [racc[r, 8 * p : 8 * p + 8] for r in range(RELS)]
         back[p, B:] = jnp.concatenate(rows, axis=0).astype(BF16)
 
 
-def add_neg_body(idx, acc_in, gn, mine, last, acc):
-    for i, (ref, at) in enumerate([(gn, 15)] + slots(mine, last)):
+def neg_body(idx, blocks, rels, stage, give, own, far, stays, h_v):
+    for i in range(TILES):
+        k = idx[ORG + i]
+        h_v[i] = dot(blocks[idx[SRC + k]], rels[idx[REL + k]], NN).astype(BF16)
+    outs = [(ref, at) for ref in (give, own, far, stays) for at in range(ref.shape[0])]
+    for i in range(TILES):
+        ref, at = outs[PLACE[i]]
+        ref[at] = dot(stage[TILES + i, :, B:], h_v[i], TN).astype(BF16)
+
+
+def add_neg_body(idx, acc_in, stays, mine, last, acc):
+    acc[...] = acc_in[...]
+    for i, (ref, at) in enumerate([(stays, 0)] + slots(mine, last)):
         acc[idx[ASKED + idx[ORG + i]]] += ref[at].astype(F32)
 
 
-def add_dst_body(which, wanted, acc_in, back, acc, rel_out):
+def add_dst_body(code, acc_in, back, acc, rel_out):
+    acc[...] = acc_in[...]
     rel_out[...] = jnp.zeros(rel_out.shape, F32)
     for p in range(32):
         rel_out[...] += back[p, B:].astype(F32)
 
-        @pl.when(wanted[p] > 0)
+        @pl.when(code[p] > 0)
         def _():
-            acc[which[p]] += back[p, :B].astype(F32)
+            acc[code[p] - 1] += back[p, :B].astype(F32)
 
 
 def per_device(entities, relations, src_block, dst_member, dst_block, rel_id, neg_block, pos_mask):
@@ -176,9 +205,8 @@
     mask = pos_mask[0, 0]
 
     match = dst_member[0] == me
-    wanted = jnp.any(match, axis=1).astype(jnp.int32)
-    which = jnp.sum(jnp.where(match, dst_block[0], 0), axis=1)
-    outgoing = call(pick_body, [SMEM, VMEM], tiles(32), 0)(which, blocks)
+    code = jnp.sum(jnp.where(match, dst_block[0] + 1, 0), axis=1)
+    outgoing = call(pick_body, [SMEM, VMEM], tiles(32), 0)(code, blocks)
     received = lax.all_to_all(outgoing, "member", split_axis=0, concat_axis=0, tiled=True)
 
     src = lax.dynamic_index_in_dim(src_block[0], me, 0, keepdims=False)
@@ -191,27 +219,38 @@
     sends = call(pre_body, [SMEM, VMEM], [tiles(7), tiles(6), tiles(2)], 0)(idx, blocks)
     mine, last = exchange(*sends)
     sums = sds(NB_DEV, B, D, dtype=F32)
-    back, acc, gn = call(
+    tile_store = pltpu.VMEM((TILES, B, D), BF16)
+    stage = call(stage_body, [SMEM] + [VMEM] * 5, tiles(TILES * 2), 256, [tile_store])(
+        idx, blocks, relations, mask, mine, last
+    )
+    back, acc = call(
         tile_body,
-        [SMEM] + [VMEM] * 6,
-        [sds(32, B + RELS * 8, D), sums, tiles(TILES)],
+        [SMEM] + [VMEM] * 4,
+        [sds(32, B + RELS * 8, D), sums],
         1600,
-        [pltpu.VMEM((RELS, D, D), F32)],
-    )(idx, blocks, relations, received, mask, mine, last)
+        [pltpu.VMEM((RELS, D, D), F32)] + [tile_store] * 3,
+    )(idx, blocks, relations, received, stage)
+    back, stage = lax.optimization_barrier((back, stage))
     back_in = lax.all_to_all(back, "member", split_axis=0, concat_axis=0, tiled=True)
 
-    mine, last = exchange(gn[:7], gn[7:13], gn[13:15])
-    acc = call(add_neg_body, [SMEM] + [VMEM] * 4, sums, 1, alias={1: 0})(
-        idx, acc, gn, mine, last
+    give, own, far, stays = call(
+        neg_body,
+        [SMEM] + [VMEM] * 3,
+        [tiles(7), tiles(6), tiles(2), tiles(1)],
+        512,
+        [tile_store],
+    )(idx, blocks, relations, stage)
+    mine, last = exchange(give, own, far)
+    acc = call(add_neg_body, [SMEM] + [VMEM] * 4, sums, 1)(
+        idx, acc, stays, mine, last
     )
     back_in, acc = lax.optimization_barrier((back_in, acc))
     out, relation_grad = call(
         add_dst_body,
-        [SMEM] * 2 + [VMEM] * 2,
+        [SMEM] + [VMEM] * 2,
         [sums, sds(RELS * 8, D, dtype=F32)],
         1,
-        alias={2: 0},
-    )(which, wanted, acc, back_in)
+    )(code, acc, back_in)
     return out.reshape(NB_DEV * B, D), relation_grad.reshape(RELS, 8, D)
 
 

time: 152 us -> 146 us (0.961)
  the two profiles are of different devices: /device:TPU:256 before, /device:TPU:128 now
where the time goes in v3:
time: 146 us
  starting transfers between devices  63.1 us (43%)
  waiting for transfers between devices  57.5 us (39%)
  Pallas kernels  12.7 us (9%)
  local copies, waits for them, and re-layouts  10.5 us (7%)
    ppermute x8, starting transfers between devices, zmove(): return lax.ppermute(v, 'group', pairs)  38.1 us
    ppermute x8, waiting for transfers between devices, zmove(): return lax.ppermute(v, 'group', pairs)  30.2 us
    all_to_all x1, waiting for transfers between devices, per_device(): lax.all_to_all(back, 'member', split_axis=0, concat_axis=0, tiled=True)  16.7 us
    all_to_all x1, starting transfers between devices, per_device(): lax.all_to_all(outgoing, 'member', split_axis=0, concat_axis=0, tiled=True)  10.2 us
    unnamed x32, local copies, waits for them, and re-layouts  9.57 us
    ppermute x4, starting transfers between devices, swap(): return lax.ppermute(v, 'group', [(i, i ^ 1) for i in range(16)])  7.68 us
    ppermute x4, waiting for transfers between devices, swap(): return lax.ppermute(v, 'group', [(i, i ^ 1) for i in range(16)])  7.13 us
    all_to_all x1, starting transfers between devices, per_device(): lax.all_to_all(back, 'member', split_axis=0, concat_axis=0, tiled=True)  7.03 us
  transfers between devices with their start and end apart: 14, of which 8 were waited for; matrix products, arithmetic and copies ran while one was open for 1% of the time, Pallas kernels for 3%

profile of v3, /device:TPU:128, one launch (start us, length us, event | category | flops | bytes accessed | tf_op | source)
XLA Modules:
  0.0 145.6 jit_solution(16623694889523326813)
XLA Ops:
  2.4 2.0 %shard_map.95 = bf16[32,128,256]{2,1,0:T(8,128)(2,1)} custom-call(s32[32]{0:T(128)S(1)} %select_reduce_fusion.code, bf16[8,128,256]{2,1,0:T(8,128)(2,1)S(1)} %bitcast.20), custom_call_target="tpu_custom_call" | custom-call | bytes 4194304 | tf_op jit(solution)/shard_map/pallas_call | solution.py:209
  4.4 10.2 %all-to-all-start = ((bf16[32,128,256]{2,1,0:T(8,128)(2,1)}), bf16[32,128,256]{2,1,0:T(8,128)(2,1)}, u32[]{:S(2)}, u32[]{:S(2)}) async-start(bf16[32,128,256]{2,1,0:T(8,128)(2,1)} %shard_map.95), calls=%async_computation | async-start | bytes 4194304 | tf_op jit(solution)/shard_map/all_to_all | solution.py:210
  16.4 1.9 %collective-permute-start = (bf16[7,128,256]{2,1,0:T(8,128)(2,1)S(1)}, bf16[7,128,256]{2,1,0:T(8,128)(2,1)S(1)}, u32[]{:S(2)}, u32[]{:S(2)}) collective-permute-start(bf16[7,128,256]{2,1,0:T(8,128)(2,1)S(1)} %get-tuple-element.27), channel_id=1, source_target_pairs={{0,32},{32,0},{64,96},{96,64},{128,160},{160,128},{192,224},{224,1... | collective-permute-start | bytes 1376264 | tf_op jit(solution)/shard_map/ppermute | solution.py:74
  18.4 1.8 %collective-permute-done.arrived = bf16[7,128,256]{2,1,0:T(8,128)(2,1)S(1)} collective-permute-done((bf16[7,128,256]{2,1,0:T(8,128)(2,1)S(1)}, bf16[7,128,256]{2,1,0:T(8,128)(2,1)S(1)}, u32[]{:S(2)}, u32[]{:S(2)}) %collective-permute-start) | collective-permute-done | bytes 458784 | tf_op jit(solution)/shard_map/ppermute | solution.py:74
  20.2 4.3 %collective-permute-start.1 = (bf16[4,128,256]{2,1,0:T(8,128)(2,1)S(1)}, bf16[4,128,256]{2,1,0:T(8,128)(2,1)S(1)}, u32[]{:S(2)}, u32[]{:S(2)}) collective-permute-start(bf16[4,128,256]{2,1,0:T(8,128)(2,1)S(1)} %get-tuple-element.29), channel_id=1, source_target_pairs={{0,64},{32,480},{64,128},{96,32},{128,192},{160,96},{192,256},{224... | collective-permute-start | bytes 786440 | tf_op jit(solution)/shard_map/ppermute | solution.py:81
  24.5 6.4 %collective-permute-start.2 = (bf16[4,128,256]{2,1,0:T(8,128)(2,1)S(1)}, bf16[4,128,256]{2,1,0:T(8,128)(2,1)S(1)}, u32[]{:S(2)}, u32[]{:S(2)}) collective-permute-start(bf16[4,128,256]{2,1,0:T(8,128)(2,1)S(1)} %get-tuple-element.30), channel_id=1, source_target_pairs={{0,128},{32,416},{64,192},{96,480},{128,256},{160,32},{192,320},{2... | collective-permute-start | bytes 786440 | tf_op jit(solution)/shard_map/ppermute | solution.py:81
  30.9 3.7 %collective-permute-start.3 = (bf16[4,128,256]{2,1,0:T(8,128)(2,1)S(1)}, bf16[4,128,256]{2,1,0:T(8,128)(2,1)S(1)}, u32[]{:S(2)}, u32[]{:S(2)}) collective-permute-start(bf16[4,128,256]{2,1,0:T(8,128)(2,1)S(1)} %get-tuple-element.31), channel_id=1, source_target_pairs={{0,192},{32,352},{64,256},{96,416},{128,320},{160,480},{192,384},{... | collective-permute-start | bytes 786440 | tf_op jit(solution)/shard_map/ppermute | solution.py:81
  34.7 5.1 %collective-permute-start.4 = (bf16[2,128,256]{2,1,0:T(8,128)(2,1)S(1)}, bf16[2,128,256]{2,1,0:T(8,128)(2,1)S(1)}, u32[]{:S(2)}, u32[]{:S(2)}) collective-permute-start(bf16[2,128,256]{2,1,0:T(8,128)(2,1)S(1)} %get-tuple-element.32), channel_id=1, source_target_pairs={{0,256},{32,288},{64,320},{96,352},{128,384},{160,416},{192,448},{... | collective-permute-start | bytes 393224 | tf_op jit(solution)/shard_map/ppermute | solution.py:81
  39.8 15.1 %collective-permute-done.4.r4 = bf16[2,128,256]{2,1,0:T(8,128)(2,1)S(1)} collective-permute-done((bf16[2,128,256]{2,1,0:T(8,128)(2,1)S(1)}, bf16[2,128,256]{2,1,0:T(8,128)(2,1)S(1)}, u32[]{:S(2)}, u32[]{:S(2)}) %collective-permute-start.4) | collective-permute-done | bytes 131104 | tf_op jit(solution)/shard_map/ppermute | solution.py:81
  54.9 1.9 %collective-permute-start.5 = (bf16[7,128,256]{2,1,0:T(8,128)(2,1)S(1)}, bf16[7,128,256]{2,1,0:T(8,128)(2,1)S(1)}, u32[]{:S(2)}, u32[]{:S(2)}) collective-permute-start(bf16[7,128,256]{2,1,0:T(8,128)(2,1)S(1)} %get-tuple-element.34), channel_id=1, source_target_pairs={{0,32},{32,0},{64,96},{96,64},{128,160},{160,128},{192,224},{224,1... | collective-permute-start | bytes 1376264 | tf_op jit(solution)/shard_map/ppermute | solution.py:74
  56.9 1.8 %collective-permute-done.5.last = bf16[7,128,256]{2,1,0:T(8,128)(2,1)S(1)} collective-permute-done((bf16[7,128,256]{2,1,0:T(8,128)(2,1)S(1)}, bf16[7,128,256]{2,1,0:T(8,128)(2,1)S(1)}, u32[]{:S(2)}, u32[]{:S(2)}) %collective-permute-start.5) | collective-permute-done | bytes 458784 | tf_op jit(solution)/shard_map/ppermute | solution.py:74
  58.7 1.2 copy-done.12
  59.9 1.3 shard_map.99.stage
  61.2 3.4 %all-to-all-done.received = bf16[32,128,256]{2,1,0:T(8,128)(2,1)} async-done(((bf16[32,128,256]{2,1,0:T(8,128)(2,1)}), bf16[32,128,256]{2,1,0:T(8,128)(2,1)}, u32[]{:S(2)}, u32[]{:S(2)}) %all-to-all-start) | async-done | bytes 2097184 | tf_op jit(solution)/shard_map/all_to_all | solution.py:210
  64.7 4.4 %shard_map.100 = (bf16[32,160,256]{2,1,0:T(8,128)(2,1)S(1)}, f32[8,128,256]{2,1,0:T(8,128)S(1)}) custom-call(s32[96]{0:T(128)S(1)} %concatenate.3.idx, bf16[8,128,256]{2,1,0:T(8,128)(2,1)S(1)} %bitcast.23, bf16[4,256,256]{2,1,0:T(8,128)(2,1)S(1)} %copy-done.8, bf16[32,128,256]{2,1,0:T(8,128)(2,1)} %all-to-all-done.received, ...), custom_call_target="tpu_custom_call" | custom-call | flops 1677721600 | bytes 4194304 | tf_op jit(solution)/shard_map/pallas_call | solution.py:226
  69.1 1.5 %copy-done.7 = bf16[32,160,256]{2,1,0:T(8,128)(2,1)} copy-done((bf16[32,160,256]{2,1,0:T(8,128)(2,1)}, bf16[32,160,256]{2,1,0:T(8,128)(2,1)S(1)}, u32[]{:S(2)}) %copy-start.7) | copy-done | bytes 2621464
  71.6 7.0 %all-to-all-start.1 = ((bf16[32,160,256]{2,1,0:T(8,128)(2,1)}), bf16[32,160,256]{2,1,0:T(8,128)(2,1)S(1)}, u32[]{:S(2)}, u32[]{:S(2)}) async-start(bf16[32,160,256]{2,1,0:T(8,128)(2,1)} %copy-done.7), calls=%async_computation.1 | async-start | bytes 5242880 | tf_op jit(solution)/shard_map/all_to_all | solution.py:234
  78.7 1.6 %copy-done.2 = bf16[32,128,256]{2,1,0:T(8,128)(2,1)S(1)} copy-done((bf16[32,128,256]{2,1,0:T(8,128)(2,1)S(1)}, bf16[32,128,256]{2,1,0:T(8,128)(2,1)}, u32[]{:S(2)}) %copy-start.2) | copy-done | bytes 2097176
  80.2 1.0 copy-done.9
  81.3 1.3 shard_map.101
  82.6 1.9 %collective-permute-start.6 = (bf16[7,128,256]{2,1,0:T(8,128)(2,1)S(1)}, bf16[7,128,256]{2,1,0:T(8,128)(2,1)S(1)}, u32[]{:S(2)}, u32[]{:S(2)}) collective-permute-start(bf16[7,128,256]{2,1,0:T(8,128)(2,1)S(1)} %get-tuple-element.40), channel_id=1, source_target_pairs={{0,32},{32,0},{64,96},{96,64},{128,160},{160,128},{192,224},{224,1... | collective-permute-start | bytes 1376264 | tf_op jit(solution)/shard_map/ppermute | solution.py:74
  84.5 1.8 %collective-permute-done.6.arrived = bf16[7,128,256]{2,1,0:T(8,128)(2,1)S(1)} collective-permute-done((bf16[7,128,256]{2,1,0:T(8,128)(2,1)S(1)}, bf16[7,128,256]{2,1,0:T(8,128)(2,1)S(1)}, u32[]{:S(2)}, u32[]{:S(2)}) %collective-permute-start.6) | collective-permute-done | bytes 458784 | tf_op jit(solution)/shard_map/ppermute | solution.py:74
  86.3 3.4 %collective-permute-start.7 = (bf16[4,128,256]{2,1,0:T(8,128)(2,1)S(1)}, bf16[4,128,256]{2,1,0:T(8,128)(2,1)S(1)}, u32[]{:S(2)}, u32[]{:S(2)}) collective-permute-start(bf16[4,128,256]{2,1,0:T(8,128)(2,1)S(1)} %get-tuple-element.42), channel_id=1, source_target_pairs={{0,64},{32,480},{64,128},{96,32},{128,192},{160,96},{192,256},{224... | collective-permute-start | bytes 786440 | tf_op jit(solution)/shard_map/ppermute | solution.py:81
  89.7 6.4 %collective-permute-start.8 = (bf16[4,128,256]{2,1,0:T(8,128)(2,1)S(1)}, bf16[4,128,256]{2,1,0:T(8,128)(2,1)S(1)}, u32[]{:S(2)}, u32[]{:S(2)}) collective-permute-start(bf16[4,128,256]{2,1,0:T(8,128)(2,1)S(1)} %get-tuple-element.43), channel_id=1, source_target_pairs={{0,128},{32,416},{64,192},{96,480},{128,256},{160,32},{192,320},{2... | collective-permute-start | bytes 786440 | tf_op jit(solution)/shard_map/ppermute | solution.py:81
  96.1 3.7 %collective-permute-start.9 = (bf16[4,128,256]{2,1,0:T(8,128)(2,1)S(1)}, bf16[4,128,256]{2,1,0:T(8,128)(2,1)S(1)}, u32[]{:S(2)}, u32[]{:S(2)}) collective-permute-start(bf16[4,128,256]{2,1,0:T(8,128)(2,1)S(1)} %get-tuple-element.44), channel_id=1, source_target_pairs={{0,192},{32,352},{64,256},{96,416},{128,320},{160,480},{192,384},{... | collective-permute-start | bytes 786440 | tf_op jit(solution)/shard_map/ppermute | solution.py:81
  99.9 5.1 %collective-permute-start.10 = (bf16[2,128,256]{2,1,0:T(8,128)(2,1)S(1)}, bf16[2,128,256]{2,1,0:T(8,128)(2,1)S(1)}, u32[]{:S(2)}, u32[]{:S(2)}) collective-permute-start(bf16[2,128,256]{2,1,0:T(8,128)(2,1)S(1)} %get-tuple-element.45), channel_id=1, source_target_pairs={{0,256},{32,288},{64,320},{96,352},{128,384},{160,416},{192,448},{... | collective-permute-start | bytes 393224 | tf_op jit(solution)/shard_map/ppermute | solution.py:81
  105.0 15.1 %collective-permute-done.10.r4 = bf16[2,128,256]{2,1,0:T(8,128)(2,1)S(1)} collective-permute-done((bf16[2,128,256]{2,1,0:T(8,128)(2,1)S(1)}, bf16[2,128,256]{2,1,0:T(8,128)(2,1)S(1)}, u32[]{:S(2)}, u32[]{:S(2)}) %collective-permute-start.10) | collective-permute-done | bytes 131104 | tf_op jit(solution)/shard_map/ppermute | solution.py:81
  120.1 1.9 %collective-permute-start.11 = (bf16[7,128,256]{2,1,0:T(8,128)(2,1)S(1)}, bf16[7,128,256]{2,1,0:T(8,128)(2,1)S(1)}, u32[]{:S(2)}, u32[]{:S(2)}) collective-permute-start(bf16[7,128,256]{2,1,0:T(8,128)(2,1)S(1)} %get-tuple-element.47), channel_id=1, source_target_pairs={{0,32},{32,0},{64,96},{96,64},{128,160},{160,128},{192,224},{224,1... | collective-permute-start | bytes 1376264 | tf_op jit(solution)/shard_map/ppermute | solution.py:74
  122.1 1.8 %collective-permute-done.11.last = bf16[7,128,256]{2,1,0:T(8,128)(2,1)S(1)} collective-permute-done((bf16[7,128,256]{2,1,0:T(8,128)(2,1)S(1)}, bf16[7,128,256]{2,1,0:T(8,128)(2,1)S(1)}, u32[]{:S(2)}, u32[]{:S(2)}) %collective-permute-start.11) | collective-permute-done | bytes 458784 | tf_op jit(solution)/shard_map/ppermute | solution.py:74
  125.6 16.7 %all-to-all-done.1.back = bf16[32,160,256]{2,1,0:T(8,128)(2,1)S(1)} async-done(((bf16[32,160,256]{2,1,0:T(8,128)(2,1)}), bf16[32,160,256]{2,1,0:T(8,128)(2,1)S(1)}, u32[]{:S(2)}, u32[]{:S(2)}) %all-to-all-start.1) | async-done | bytes 2621472 | tf_op jit(solution)/shard_map/all_to_all | solution.py:234
  142.4 1.2 copy-done.6
  143.6 2.0 %shard_map.105 = (f32[8,128,256]{2,1,0:T(8,128)}, f32[32,256]{1,0:T(8,128)}) custom-call(s32[32]{0:T(128)S(1)} %select_reduce_fusion.code, f32[8,128,256]{2,1,0:T(8,128)S(1)} %copy-done.6, bf16[32,160,256]{2,1,0:T(8,128)(2,1)S(1)} %all-to-all-done.1.back), custom_call_target="tpu_custom_call" | custom-call | flops 1048576 | bytes 4194304 | tf_op jit(solution)/shard_map/pallas_call | solution.py:248
  (44 shorter events, 6.4 us)
Async XLA Ops:
  0.6 14.2 %copy-start = (s32[1,32,16]{1,2,0:T(8,128)S(1)}, s32[1,32,16]{1,2,0:T(8,128)}, u32[]{:S(2)}) copy-start(s32[1,32,16]{1,2,0:T(8,128)} %param.10) | copy-start | bytes 6148
  1.4 1.0 copy-start.3
  4.4 10.6 %copy-start.13 = (s32[1,32,16]{1,2,0:T(8,128)S(1)}, s32[1,32,16]{1,2,0:T(8,128)}, u32[]{:S(2)}) copy-start(s32[1,32,16]{1,2,0:T(8,128)} %param.11) | copy-start | bytes 6148
  4.4 10.6 %copy-start.15 = (s32[1,32,16]{1,2,0:T(8,128)S(1)}, s32[1,32,16]{1,2,0:T(8,128)}, u32[]{:S(2)}) copy-start(s32[1,32,16]{1,2,0:T(8,128)} %param.13) | copy-start | bytes 6148
  4.4 10.8 %copy-start.14 = (s32[16,1,16]{2,1,0:T(1,128)S(1)}, s32[16,1,16]{2,1,0:T(1,128)}, u32[]{:S(2)}) copy-start(s32[16,1,16]{2,1,0:T(1,128)} %param.14) | copy-start | bytes 3076
  4.4 11.4 %copy-start.4 = (bf16[1024,256]{1,0:T(8,128)(2,1)S(1)}, bf16[1024,256]{1,0:T(8,128)(2,1)}, u32[]{:S(2)}) copy-start(bf16[1024,256]{1,0:T(8,128)(2,1)} %param.8) | copy-start | bytes 1572868
  4.4 60.3 %all-to-all-start = ((bf16[32,128,256]{2,1,0:T(8,128)(2,1)}), bf16[32,128,256]{2,1,0:T(8,128)(2,1)}, u32[]{:S(2)}, u32[]{:S(2)}) async-start(bf16[32,128,256]{2,1,0:T(8,128)(2,1)} %shard_map.95), calls=%async_computation | async-start | bytes 4194304 | tf_op jit(solution)/shard_map/all_to_all | solution.py:210
  14.7 44.0 %copy-start.8 = (bf16[4,256,256]{2,1,0:T(8,128)(2,1)S(1)}, bf16[4,256,256]{2,1,0:T(8,128)(2,1)}, u32[]{:S(2)}) copy-start(bf16[4,256,256]{2,1,0:T(8,128)(2,1)} %rels.5) | copy-start | bytes 1572868
  16.4 3.7 %collective-permute-start = (bf16[7,128,256]{2,1,0:T(8,128)(2,1)S(1)}, bf16[7,128,256]{2,1,0:T(8,128)(2,1)S(1)}, u32[]{:S(2)}, u32[]{:S(2)}) collective-permute-start(bf16[7,128,256]{2,1,0:T(8,128)(2,1)S(1)} %get-tuple-element.27), channel_id=1, source_target_pairs={{0,32},{32,0},{64,96},{96,64},{128,160},{160,128},{192,224},{224,1... | collective-permute-start | bytes 1376264 | tf_op jit(solution)/shard_map/ppermute | solution.py:74
  20.2 34.6 %collective-permute-start.1 = (bf16[4,128,256]{2,1,0:T(8,128)(2,1)S(1)}, bf16[4,128,256]{2,1,0:T(8,128)(2,1)S(1)}, u32[]{:S(2)}, u32[]{:S(2)}) collective-permute-start(bf16[4,128,256]{2,1,0:T(8,128)(2,1)S(1)} %get-tuple-element.29), channel_id=1, source_target_pairs={{0,64},{32,480},{64,128},{96,32},{128,192},{160,96},{192,256},{224... | collective-permute-start | bytes 786440 | tf_op jit(solution)/shard_map/ppermute | solution.py:81
  24.5 30.4 %collective-permute-start.2 = (bf16[4,128,256]{2,1,0:T(8,128)(2,1)S(1)}, bf16[4,128,256]{2,1,0:T(8,128)(2,1)S(1)}, u32[]{:S(2)}, u32[]{:S(2)}) collective-permute-start(bf16[4,128,256]{2,1,0:T(8,128)(2,1)S(1)} %get-tuple-element.30), channel_id=1, source_target_pairs={{0,128},{32,416},{64,192},{96,480},{128,256},{160,32},{192,320},{2... | collective-permute-start | bytes 786440 | tf_op jit(solution)/shard_map/ppermute | solution.py:81
  30.9 23.9 %collective-permute-start.3 = (bf16[4,128,256]{2,1,0:T(8,128)(2,1)S(1)}, bf16[4,128,256]{2,1,0:T(8,128)(2,1)S(1)}, u32[]{:S(2)}, u32[]{:S(2)}) collective-permute-start(bf16[4,128,256]{2,1,0:T(8,128)(2,1)S(1)} %get-tuple-element.31), channel_id=1, source_target_pairs={{0,192},{32,352},{64,256},{96,416},{128,320},{160,480},{192,384},{... | collective-permute-start | bytes 786440 | tf_op jit(solution)/shard_map/ppermute | solution.py:81
  34.7 20.2 %collective-permute-start.4 = (bf16[2,128,256]{2,1,0:T(8,128)(2,1)S(1)}, bf16[2,128,256]{2,1,0:T(8,128)(2,1)S(1)}, u32[]{:S(2)}, u32[]{:S(2)}) collective-permute-start(bf16[2,128,256]{2,1,0:T(8,128)(2,1)S(1)} %get-tuple-element.32), channel_id=1, source_target_pairs={{0,256},{32,288},{64,320},{96,352},{128,384},{160,416},{192,448},{... | collective-permute-start | bytes 393224 | tf_op jit(solution)/shard_map/ppermute | solution.py:81
  54.9 3.7 %collective-permute-start.5 = (bf16[7,128,256]{2,1,0:T(8,128)(2,1)S(1)}, bf16[7,128,256]{2,1,0:T(8,128)(2,1)S(1)}, u32[]{:S(2)}, u32[]{:S(2)}) collective-permute-start(bf16[7,128,256]{2,1,0:T(8,128)(2,1)S(1)} %get-tuple-element.34), channel_id=1, source_target_pairs={{0,32},{32,0},{64,96},{96,64},{128,160},{160,128},{192,224},{224,1... | collective-permute-start | bytes 1376264 | tf_op jit(solution)/shard_map/ppermute | solution.py:74
  58.6 1.2 copy-start.12
  61.2 7.9 %copy-start.1 = (bf16[32,128,256]{2,1,0:T(8,128)(2,1)}, bf16[32,128,256]{2,1,0:T(8,128)(2,1)S(1)}, u32[]{:S(2)}) copy-start(bf16[32,128,256]{2,1,0:T(8,128)(2,1)S(1)} %shard_map.99.stage) | copy-start | bytes 6291460
  69.1 1.5 %copy-start.7 = (bf16[32,160,256]{2,1,0:T(8,128)(2,1)}, bf16[32,160,256]{2,1,0:T(8,128)(2,1)S(1)}, u32[]{:S(2)}) copy-start(bf16[32,160,256]{2,1,0:T(8,128)(2,1)S(1)} %get-tuple-element.36) | copy-start | bytes 7864324
  70.6 1.0 copy-start.10
  71.6 70.8 %all-to-all-start.1 = ((bf16[32,160,256]{2,1,0:T(8,128)(2,1)}), bf16[32,160,256]{2,1,0:T(8,128)(2,1)S(1)}, u32[]{:S(2)}, u32[]{:S(2)}) async-start(bf16[32,160,256]{2,1,0:T(8,128)(2,1)} %copy-done.7), calls=%async_computation.1 | async-start | bytes 5242880 | tf_op jit(solution)/shard_map/all_to_all | solution.py:234
  78.6 1.6 %copy-start.2 = (bf16[32,128,256]{2,1,0:T(8,128)(2,1)S(1)}, bf16[32,128,256]{2,1,0:T(8,128)(2,1)}, u32[]{:S(2)}) copy-start(bf16[32,128,256]{2,1,0:T(8,128)(2,1)} %copy-done.1) | copy-start | bytes 6291460
  80.2 1.0 copy-start.9
  81.3 42.6 %copy-start.11 = (f32[8,128,256]{2,1,0:T(8,128)S(1)}, f32[8,128,256]{2,1,0:T(8,128)}, u32[]{:S(2)}) copy-start(f32[8,128,256]{2,1,0:T(8,128)} %copy-done.10) | copy-start | bytes 3145732
  82.6 3.7 %collective-permute-start.6 = (bf16[7,128,256]{2,1,0:T(8,128)(2,1)S(1)}, bf16[7,128,256]{2,1,0:T(8,128)(2,1)S(1)}, u32[]{:S(2)}, u32[]{:S(2)}) collective-permute-start(bf16[7,128,256]{2,1,0:T(8,128)(2,1)S(1)} %get-tuple-element.40), channel_id=1, source_target_pairs={{0,32},{32,0},{64,96},{96,64},{128,160},{160,128},{192,224},{224,1... | collective-permute-start | bytes 1376264 | tf_op jit(solution)/shard_map/ppermute | solution.py:74
  86.3 33.7 %collective-permute-start.7 = (bf16[4,128,256]{2,1,0:T(8,128)(2,1)S(1)}, bf16[4,128,256]{2,1,0:T(8,128)(2,1)S(1)}, u32[]{:S(2)}, u32[]{:S(2)}) collective-permute-start(bf16[4,128,256]{2,1,0:T(8,128)(2,1)S(1)} %get-tuple-element.42), channel_id=1, source_target_pairs={{0,64},{32,480},{64,128},{96,32},{128,192},{160,96},{192,256},{224... | collective-permute-start | bytes 786440 | tf_op jit(solution)/shard_map/ppermute | solution.py:81
  89.7 30.3 %collective-permute-start.8 = (bf16[4,128,256]{2,1,0:T(8,128)(2,1)S(1)}, bf16[4,128,256]{2,1,0:T(8,128)(2,1)S(1)}, u32[]{:S(2)}, u32[]{:S(2)}) collective-permute-start(bf16[4,128,256]{2,1,0:T(8,128)(2,1)S(1)} %get-tuple-element.43), channel_id=1, source_target_pairs={{0,128},{32,416},{64,192},{96,480},{128,256},{160,32},{192,320},{2... | collective-permute-start | bytes 786440 | tf_op jit(solution)/shard_map/ppermute | solution.py:81
  96.1 23.9 %collective-permute-start.9 = (bf16[4,128,256]{2,1,0:T(8,128)(2,1)S(1)}, bf16[4,128,256]{2,1,0:T(8,128)(2,1)S(1)}, u32[]{:S(2)}, u32[]{:S(2)}) collective-permute-start(bf16[4,128,256]{2,1,0:T(8,128)(2,1)S(1)} %get-tuple-element.44), channel_id=1, source_target_pairs={{0,192},{32,352},{64,256},{96,416},{128,320},{160,480},{192,384},{... | collective-permute-start | bytes 786440 | tf_op jit(solution)/shard_map/ppermute | solution.py:81
  99.9 20.2 %collective-permute-start.10 = (bf16[2,128,256]{2,1,0:T(8,128)(2,1)S(1)}, bf16[2,128,256]{2,1,0:T(8,128)(2,1)S(1)}, u32[]{:S(2)}, u32[]{:S(2)}) collective-permute-start(bf16[2,128,256]{2,1,0:T(8,128)(2,1)S(1)} %get-tuple-element.45), channel_id=1, source_target_pairs={{0,256},{32,288},{64,320},{96,352},{128,384},{160,416},{192,448},{... | collective-permute-start | bytes 393224 | tf_op jit(solution)/shard_map/ppermute | solution.py:81
  120.1 3.7 %collective-permute-start.11 = (bf16[7,128,256]{2,1,0:T(8,128)(2,1)S(1)}, bf16[7,128,256]{2,1,0:T(8,128)(2,1)S(1)}, u32[]{:S(2)}, u32[]{:S(2)}) collective-permute-start(bf16[7,128,256]{2,1,0:T(8,128)(2,1)S(1)} %get-tuple-element.47), channel_id=1, source_target_pairs={{0,32},{32,0},{64,96},{96,64},{128,160},{160,128},{192,224},{224,1... | collective-permute-start | bytes 1376264 | tf_op jit(solution)/shard_map/ppermute | solution.py:74
  124.7 1.0 copy-start.5
  142.4 1.2 copy-start.6

commit v4 on v3

--- a/solution.py
+++ b/solution.py
@@ -144,12 +144,11 @@
         stage[TILES + i] = jnp.concatenate(pair, axis=1).astype(BF16)
 
 
-def tile_body(idx, blocks, rels, received, stage, back, acc, racc, h_v, g_v, gh_v):
+def tile_body(idx, blocks, rels, received, stage, back, gh_v, racc, h_v, g_v):
     work = []
     for i in range(TILES):
         k = idx[ORG + i]
         work.append((i, idx[SRC + k], idx[REL + k], idx[DST + k]))
-    acc[...] = jnp.zeros(acc.shape, F32)
     racc[...] = jnp.zeros(racc.shape, F32)
     for i, j, r, d in work:
         h_v[i] = dot(blocks[j], rels[r], NN).astype(BF16)
@@ -165,7 +164,6 @@
         back[d, :B] = dot(g_v[i, :, :B], h_v[i], TN).astype(BF16)
     for i, j, r, d in work:
         racc[r] += dot(blocks[j], gh_v[i], TN)
-        acc[j] += dot(gh_v[i], rels[r], NT)
     for p in range(32):
         rows = [racc[r, 8 * p : 8 * p + 8] for r in range(RELS)]
         back[p, B:] = jnp.concatenate(rows, axis=0).astype(BF16)
@@ -181,8 +179,11 @@
         ref[at] = dot(stage[TILES + i, :, B:], h_v[i], TN).astype(BF16)
 
 
-def add_neg_body(idx, acc_in, stays, mine, last, acc):
-    acc[...] = acc_in[...]
+def add_neg_body(idx, rels, gh, stays, mine, last, acc):
+    acc[...] = jnp.zeros(acc.shape, F32)
+    for i in range(TILES):
+        k = idx[ORG + i]
+        acc[idx[SRC + k]] += dot(gh[i], rels[idx[REL + k]], NT)
     for i, (ref, at) in enumerate([(stays, 0)] + slots(mine, last)):
         acc[idx[ASKED + idx[ORG + i]]] += ref[at].astype(F32)
 
@@ -223,12 +224,12 @@
     stage = call(stage_body, [SMEM] + [VMEM] * 5, tiles(TILES * 2), 256, [tile_store])(
         idx, blocks, relations, mask, mine, last
     )
-    back, acc = call(
+    back, gh = call(
         tile_body,
         [SMEM] + [VMEM] * 4,
-        [sds(32, B + RELS * 8, D), sums],
+        [sds(32, B + RELS * 8, D), tiles(TILES)],
         1600,
-        [pltpu.VMEM((RELS, D, D), F32)] + [tile_store] * 3,
+        [pltpu.VMEM((RELS, D, D), F32)] + [tile_store] * 2,
     )(idx, blocks, relations, received, stage)
     back, stage = lax.optimization_barrier((back, stage))
     back_in = lax.all_to_all(back, "member", split_axis=0, concat_axis=0, tiled=True)
@@ -241,8 +242,8 @@
         [tile_store],
     )(idx, blocks, relations, stage)
     mine, last = exchange(give, own, far)
-    acc = call(add_neg_body, [SMEM] + [VMEM] * 4, sums, 1)(
-        idx, acc, stays, mine, last
+    acc = call(add_neg_body, [SMEM] + [VMEM] * 5, sums, 256)(
+        idx, relations, gh, stays, mine, last
     )
     back_in, acc = lax.optimization_barrier((back_in, acc))
     out, relation_grad = call(

time: 146 us -> 146 us (level)
    unnamed x32 -> x34, local copies, waits for them, and re-layouts: 9.57 us -> 9.59 us
where the time goes in v4:
time: 146 us; the launch traced here: 145 us
  starting transfers between devices  63.1 us (43%)
  waiting for transfers between devices  56.7 us (39%)
  Pallas kernels  12.8 us (9%)
  local copies, waits for them, and re-layouts  10.5 us (7%)
    ppermute x8, starting transfers between devices, zmove(): return lax.ppermute(v, 'group', pairs)  38.2 us
    ppermute x8, waiting for transfers between devices, zmove(): return lax.ppermute(v, 'group', pairs)  30.2 us
    all_to_all x1, waiting for transfers between devices, per_device(): lax.all_to_all(back, 'member', split_axis=0, concat_axis=0, tiled=True)  15.9 us
    all_to_all x1, starting transfers between devices, per_device(): lax.all_to_all(outgoing, 'member', split_axis=0, concat_axis=0, tiled=True)  10.2 us
    unnamed x34, local copies, waits for them, and re-layouts  9.59 us
    ppermute x4, starting transfers between devices, swap(): return lax.ppermute(v, 'group', [(i, i ^ 1) for i in range(16)])  7.68 us
    ppermute x4, waiting for transfers between devices, swap(): return lax.ppermute(v, 'group', [(i, i ^ 1) for i in range(16)])  7.13 us
    all_to_all x1, starting transfers between devices, per_device(): lax.all_to_all(back, 'member', split_axis=0, concat_axis=0, tiled=True)  7.02 us
  transfers between devices with their start and end apart: 14, of which 8 were waited for; matrix products, arithmetic and copies ran while one was open for 1% of the time, Pallas kernels for 3%

profile of v4, /device:TPU:128, one launch (start us, length us, event | category | flops | bytes accessed | tf_op | source)
XLA Modules:
  0.0 144.9 jit_solution(18242905358843284330)
XLA Ops:
  2.4 2.0 %shard_map.95 = bf16[32,128,256]{2,1,0:T(8,128)(2,1)} custom-call(s32[32]{0:T(128)S(1)} %select_reduce_fusion.code, bf16[8,128,256]{2,1,0:T(8,128)(2,1)S(1)} %bitcast.20), custom_call_target="tpu_custom_call" | custom-call | bytes 4194304 | tf_op jit(solution)/shard_map/pallas_call | solution.py:210
  4.4 10.2 %all-to-all-start = ((bf16[32,128,256]{2,1,0:T(8,128)(2,1)}), bf16[32,128,256]{2,1,0:T(8,128)(2,1)}, u32[]{:S(2)}, u32[]{:S(2)}) async-start(bf16[32,128,256]{2,1,0:T(8,128)(2,1)} %shard_map.95), calls=%async_computation | async-start | bytes 4194304 | tf_op jit(solution)/shard_map/all_to_all | solution.py:211
  16.4 1.9 %collective-permute-start = (bf16[7,128,256]{2,1,0:T(8,128)(2,1)S(1)}, bf16[7,128,256]{2,1,0:T(8,128)(2,1)S(1)}, u32[]{:S(2)}, u32[]{:S(2)}) collective-permute-start(bf16[7,128,256]{2,1,0:T(8,128)(2,1)S(1)} %get-tuple-element.27), channel_id=1, source_target_pairs={{0,32},{32,0},{64,96},{96,64},{128,160},{160,128},{192,224},{224,1... | collective-permute-start | bytes 1376264 | tf_op jit(solution)/shard_map/ppermute | solution.py:74
  18.4 1.8 %collective-permute-done.arrived = bf16[7,128,256]{2,1,0:T(8,128)(2,1)S(1)} collective-permute-done((bf16[7,128,256]{2,1,0:T(8,128)(2,1)S(1)}, bf16[7,128,256]{2,1,0:T(8,128)(2,1)S(1)}, u32[]{:S(2)}, u32[]{:S(2)}) %collective-permute-start) | collective-permute-done | bytes 458784 | tf_op jit(solution)/shard_map/ppermute | solution.py:74
  20.2 4.3 %collective-permute-start.1 = (bf16[4,128,256]{2,1,0:T(8,128)(2,1)S(1)}, bf16[4,128,256]{2,1,0:T(8,128)(2,1)S(1)}, u32[]{:S(2)}, u32[]{:S(2)}) collective-permute-start(bf16[4,128,256]{2,1,0:T(8,128)(2,1)S(1)} %get-tuple-element.29), channel_id=1, source_target_pairs={{0,64},{32,480},{64,128},{96,32},{128,192},{160,96},{192,256},{224... | collective-permute-start | bytes 786440 | tf_op jit(solution)/shard_map/ppermute | solution.py:81
  24.5 6.4 %collective-permute-start.2 = (bf16[4,128,256]{2,1,0:T(8,128)(2,1)S(1)}, bf16[4,128,256]{2,1,0:T(8,128)(2,1)S(1)}, u32[]{:S(2)}, u32[]{:S(2)}) collective-permute-start(bf16[4,128,256]{2,1,0:T(8,128)(2,1)S(1)} %get-tuple-element.30), channel_id=1, source_target_pairs={{0,128},{32,416},{64,192},{96,480},{128,256},{160,32},{192,320},{2... | collective-permute-start | bytes 786440 | tf_op jit(solution)/shard_map/ppermute | solution.py:81
  30.9 3.7 %collective-permute-start.3 = (bf16[4,128,256]{2,1,0:T(8,128)(2,1)S(1)}, bf16[4,128,256]{2,1,0:T(8,128)(2,1)S(1)}, u32[]{:S(2)}, u32[]{:S(2)}) collective-permute-start(bf16[4,128,256]{2,1,0:T(8,128)(2,1)S(1)} %get-tuple-element.31), channel_id=1, source_target_pairs={{0,192},{32,352},{64,256},{96,416},{128,320},{160,480},{192,384},{... | collective-permute-start | bytes 786440 | tf_op jit(solution)/shard_map/ppermute | solution.py:81
  34.7 5.1 %collective-permute-start.4 = (bf16[2,128,256]{2,1,0:T(8,128)(2,1)S(1)}, bf16[2,128,256]{2,1,0:T(8,128)(2,1)S(1)}, u32[]{:S(2)}, u32[]{:S(2)}) collective-permute-start(bf16[2,128,256]{2,1,0:T(8,128)(2,1)S(1)} %get-tuple-element.32), channel_id=1, source_target_pairs={{0,256},{32,288},{64,320},{96,352},{128,384},{160,416},{192,448},{... | collective-permute-start | bytes 393224 | tf_op jit(solution)/shard_map/ppermute | solution.py:81
  39.8 15.1 %collective-permute-done.4.r4 = bf16[2,128,256]{2,1,0:T(8,128)(2,1)S(1)} collective-permute-done((bf16[2,128,256]{2,1,0:T(8,128)(2,1)S(1)}, bf16[2,128,256]{2,1,0:T(8,128)(2,1)S(1)}, u32[]{:S(2)}, u32[]{:S(2)}) %collective-permute-start.4) | collective-permute-done | bytes 131104 | tf_op jit(solution)/shard_map/ppermute | solution.py:81
  54.9 1.9 %collective-permute-start.5 = (bf16[7,128,256]{2,1,0:T(8,128)(2,1)S(1)}, bf16[7,128,256]{2,1,0:T(8,128)(2,1)S(1)}, u32[]{:S(2)}, u32[]{:S(2)}) collective-permute-start(bf16[7,128,256]{2,1,0:T(8,128)(2,1)S(1)} %get-tuple-element.34), channel_id=1, source_target_pairs={{0,32},{32,0},{64,96},{96,64},{128,160},{160,128},{192,224},{224,1... | collective-permute-start | bytes 1376264 | tf_op jit(solution)/shard_map/ppermute | solution.py:74
  56.9 1.8 %collective-permute-done.5.last = bf16[7,128,256]{2,1,0:T(8,128)(2,1)S(1)} collective-permute-done((bf16[7,128,256]{2,1,0:T(8,128)(2,1)S(1)}, bf16[7,128,256]{2,1,0:T(8,128)(2,1)S(1)}, u32[]{:S(2)}, u32[]{:S(2)}) %collective-permute-start.5) | collective-permute-done | bytes 458784 | tf_op jit(solution)/shard_map/ppermute | solution.py:74
  58.6 1.2 copy-done.11
  59.9 1.3 shard_map.99.stage
  61.2 3.5 %all-to-all-done.received = bf16[32,128,256]{2,1,0:T(8,128)(2,1)} async-done(((bf16[32,128,256]{2,1,0:T(8,128)(2,1)}), bf16[32,128,256]{2,1,0:T(8,128)(2,1)}, u32[]{:S(2)}, u32[]{:S(2)}) %all-to-all-start) | async-done | bytes 2097184 | tf_op jit(solution)/shard_map/all_to_all | solution.py:211
  64.7 3.8 %shard_map.100 = (bf16[32,160,256]{2,1,0:T(8,128)(2,1)S(1)}, bf16[16,128,256]{2,1,0:T(8,128)(2,1)S(1)}) custom-call(s32[96]{0:T(128)S(1)} %concatenate.3.idx, bf16[8,128,256]{2,1,0:T(8,128)(2,1)S(1)} %bitcast.23, bf16[4,256,256]{2,1,0:T(8,128)(2,1)S(1)} %copy-done.5, bf16[32,128,256]{2,1,0:T(8,128)(2,1)} %all-to-all-done.received, ...), custom_call_target="tpu_custom_call" | custom-call | flops 1677721600 | bytes 4194304 | tf_op jit(solution)/shard_map/pallas_call | solution.py:227
  68.5 1.5 %copy-done.10 = bf16[32,160,256]{2,1,0:T(8,128)(2,1)} copy-done((bf16[32,160,256]{2,1,0:T(8,128)(2,1)}, bf16[32,160,256]{2,1,0:T(8,128)(2,1)S(1)}, u32[]{:S(2)}) %copy-start.10) | copy-done | bytes 2621464
  70.9 7.0 %all-to-all-start.1 = ((bf16[32,160,256]{2,1,0:T(8,128)(2,1)}), bf16[32,160,256]{2,1,0:T(8,128)(2,1)S(1)}, u32[]{:S(2)}, u32[]{:S(2)}) async-start(bf16[32,160,256]{2,1,0:T(8,128)(2,1)} %copy-done.10), calls=%async_computation.1 | async-start | bytes 5242880 | tf_op jit(solution)/shard_map/all_to_all | solution.py:235
  78.0 1.6 %copy-done.2 = bf16[32,128,256]{2,1,0:T(8,128)(2,1)S(1)} copy-done((bf16[32,128,256]{2,1,0:T(8,128)(2,1)S(1)}, bf16[32,128,256]{2,1,0:T(8,128)(2,1)}, u32[]{:S(2)}) %copy-start.2) | copy-done | bytes 2097176
  80.6 1.3 shard_map.101
  81.9 1.9 %collective-permute-start.6 = (bf16[7,128,256]{2,1,0:T(8,128)(2,1)S(1)}, bf16[7,128,256]{2,1,0:T(8,128)(2,1)S(1)}, u32[]{:S(2)}, u32[]{:S(2)}) collective-permute-start(bf16[7,128,256]{2,1,0:T(8,128)(2,1)S(1)} %get-tuple-element.40), channel_id=1, source_target_pairs={{0,32},{32,0},{64,96},{96,64},{128,160},{160,128},{192,224},{224,1... | collective-permute-start | bytes 1376264 | tf_op jit(solution)/shard_map/ppermute | solution.py:74
  83.8 1.8 %collective-permute-done.6.arrived = bf16[7,128,256]{2,1,0:T(8,128)(2,1)S(1)} collective-permute-done((bf16[7,128,256]{2,1,0:T(8,128)(2,1)S(1)}, bf16[7,128,256]{2,1,0:T(8,128)(2,1)S(1)}, u32[]{:S(2)}, u32[]{:S(2)}) %collective-permute-start.6) | collective-permute-done | bytes 458784 | tf_op jit(solution)/shard_map/ppermute | solution.py:74
  85.7 3.4 %collective-permute-start.7 = (bf16[4,128,256]{2,1,0:T(8,128)(2,1)S(1)}, bf16[4,128,256]{2,1,0:T(8,128)(2,1)S(1)}, u32[]{:S(2)}, u32[]{:S(2)}) collective-permute-start(bf16[4,128,256]{2,1,0:T(8,128)(2,1)S(1)} %get-tuple-element.42), channel_id=1, source_target_pairs={{0,64},{32,480},{64,128},{96,32},{128,192},{160,96},{192,256},{224... | collective-permute-start | bytes 786440 | tf_op jit(solution)/shard_map/ppermute | solution.py:81
  89.1 6.4 %collective-permute-start.8 = (bf16[4,128,256]{2,1,0:T(8,128)(2,1)S(1)}, bf16[4,128,256]{2,1,0:T(8,128)(2,1)S(1)}, u32[]{:S(2)}, u32[]{:S(2)}) collective-permute-start(bf16[4,128,256]{2,1,0:T(8,128)(2,1)S(1)} %get-tuple-element.43), channel_id=1, source_target_pairs={{0,128},{32,416},{64,192},{96,480},{128,256},{160,32},{192,320},{2... | collective-permute-start | bytes 786440 | tf_op jit(solution)/shard_map/ppermute | solution.py:81
  95.5 3.7 %collective-permute-start.9 = (bf16[4,128,256]{2,1,0:T(8,128)(2,1)S(1)}, bf16[4,128,256]{2,1,0:T(8,128)(2,1)S(1)}, u32[]{:S(2)}, u32[]{:S(2)}) collective-permute-start(bf16[4,128,256]{2,1,0:T(8,128)(2,1)S(1)} %get-tuple-element.44), channel_id=1, source_target_pairs={{0,192},{32,352},{64,256},{96,416},{128,320},{160,480},{192,384},{... | collective-permute-start | bytes 786440 | tf_op jit(solution)/shard_map/ppermute | solution.py:81
  99.2 5.1 %collective-permute-start.10 = (bf16[2,128,256]{2,1,0:T(8,128)(2,1)S(1)}, bf16[2,128,256]{2,1,0:T(8,128)(2,1)S(1)}, u32[]{:S(2)}, u32[]{:S(2)}) collective-permute-start(bf16[2,128,256]{2,1,0:T(8,128)(2,1)S(1)} %get-tuple-element.45), channel_id=1, source_target_pairs={{0,256},{32,288},{64,320},{96,352},{128,384},{160,416},{192,448},{... | collective-permute-start | bytes 393224 | tf_op jit(solution)/shard_map/ppermute | solution.py:81
  104.3 15.1 %collective-permute-done.10.r4 = bf16[2,128,256]{2,1,0:T(8,128)(2,1)S(1)} collective-permute-done((bf16[2,128,256]{2,1,0:T(8,128)(2,1)S(1)}, bf16[2,128,256]{2,1,0:T(8,128)(2,1)S(1)}, u32[]{:S(2)}, u32[]{:S(2)}) %collective-permute-start.10) | collective-permute-done | bytes 131104 | tf_op jit(solution)/shard_map/ppermute | solution.py:81
  119.5 1.9 %collective-permute-start.11 = (bf16[7,128,256]{2,1,0:T(8,128)(2,1)S(1)}, bf16[7,128,256]{2,1,0:T(8,128)(2,1)S(1)}, u32[]{:S(2)}, u32[]{:S(2)}) collective-permute-start(bf16[7,128,256]{2,1,0:T(8,128)(2,1)S(1)} %get-tuple-element.47), channel_id=1, source_target_pairs={{0,32},{32,0},{64,96},{96,64},{128,160},{160,128},{192,224},{224,1... | collective-permute-start | bytes 1376264 | tf_op jit(solution)/shard_map/ppermute | solution.py:74
  121.4 1.8 %collective-permute-done.11.last = bf16[7,128,256]{2,1,0:T(8,128)(2,1)S(1)} collective-permute-done((bf16[7,128,256]{2,1,0:T(8,128)(2,1)S(1)}, bf16[7,128,256]{2,1,0:T(8,128)(2,1)S(1)}, u32[]{:S(2)}, u32[]{:S(2)}) %collective-permute-start.11) | collective-permute-done | bytes 458784 | tf_op jit(solution)/shard_map/ppermute | solution.py:74
  123.2 1.6 %shard_map.104.acc_in = f32[8,128,256]{2,1,0:T(8,128)S(1)} custom-call(s32[96]{0:T(128)S(1)} %concatenate.3.idx, bf16[4,256,256]{2,1,0:T(8,128)(2,1)S(1)} %copy-done.7, bf16[16,128,256]{2,1,0:T(8,128)(2,1)S(1)} %copy-done.13, bf16[1,128,256]{2,1,0:T(8,128)(2,1)S(1)} %get-tuple-element.39.stays, bf16[8,128,256]{2,1,0:T(8,128)(2,1)S(1)} %get-tuple-element.46.mine, ...), custom_call_target="tpu_custom_call" | custom-call | flops 268435456 | bytes 4194304 | tf_op jit(solution)/shard_map/pallas_call | solution.py:245
  125.8 15.9 %all-to-all-done.1.back = bf16[32,160,256]{2,1,0:T(8,128)(2,1)S(1)} async-done(((bf16[32,160,256]{2,1,0:T(8,128)(2,1)}), bf16[32,160,256]{2,1,0:T(8,128)(2,1)S(1)}, u32[]{:S(2)}, u32[]{:S(2)}) %all-to-all-start.1) | async-done | bytes 2621472 | tf_op jit(solution)/shard_map/all_to_all | solution.py:235
  141.7 1.2 copy-done.9
  142.9 2.0 %shard_map.105 = (f32[8,128,256]{2,1,0:T(8,128)}, f32[32,256]{1,0:T(8,128)}) custom-call(s32[32]{0:T(128)S(1)} %select_reduce_fusion.code, f32[8,128,256]{2,1,0:T(8,128)S(1)} %copy-done.9, bf16[32,160,256]{2,1,0:T(8,128)(2,1)S(1)} %all-to-all-done.1.back), custom_call_target="tpu_custom_call" | custom-call | flops 1048576 | bytes 4194304 | tf_op jit(solution)/shard_map/pallas_call | solution.py:249
  (46 shorter events, 6.6 us)
Async XLA Ops:
  0.6 14.2 %copy-start = (s32[1,32,16]{1,2,0:T(8,128)S(1)}, s32[1,32,16]{1,2,0:T(8,128)}, u32[]{:S(2)}) copy-start(s32[1,32,16]{1,2,0:T(8,128)} %param.10) | copy-start | bytes 6148
  1.4 1.0 copy-start.3
  4.4 10.6 %copy-start.14 = (s32[1,32,16]{1,2,0:T(8,128)S(1)}, s32[1,32,16]{1,2,0:T(8,128)}, u32[]{:S(2)}) copy-start(s32[1,32,16]{1,2,0:T(8,128)} %param.11) | copy-start | bytes 6148
  4.4 10.6 %copy-start.16 = (s32[1,32,16]{1,2,0:T(8,128)S(1)}, s32[1,32,16]{1,2,0:T(8,128)}, u32[]{:S(2)}) copy-start(s32[1,32,16]{1,2,0:T(8,128)} %param.13) | copy-start | bytes 6148
  4.4 10.8 %copy-start.15 = (s32[16,1,16]{2,1,0:T(1,128)S(1)}, s32[16,1,16]{2,1,0:T(1,128)}, u32[]{:S(2)}) copy-start(s32[16,1,16]{2,1,0:T(1,128)} %param.14) | copy-start | bytes 3076
  4.4 11.4 %copy-start.4 = (bf16[1024,256]{1,0:T(8,128)(2,1)S(1)}, bf16[1024,256]{1,0:T(8,128)(2,1)}, u32[]{:S(2)}) copy-start(bf16[1024,256]{1,0:T(8,128)(2,1)} %param.8) | copy-start | bytes 1572868
  4.4 60.3 %all-to-all-start = ((bf16[32,128,256]{2,1,0:T(8,128)(2,1)}), bf16[32,128,256]{2,1,0:T(8,128)(2,1)}, u32[]{:S(2)}, u32[]{:S(2)}) async-start(bf16[32,128,256]{2,1,0:T(8,128)(2,1)} %shard_map.95), calls=%async_computation | async-start | bytes 4194304 | tf_op jit(solution)/shard_map/all_to_all | solution.py:211
  14.6 44.0 %copy-start.5 = (bf16[4,256,256]{2,1,0:T(8,128)(2,1)S(1)}, bf16[4,256,256]{2,1,0:T(8,128)(2,1)}, u32[]{:S(2)}) copy-start(bf16[4,256,256]{2,1,0:T(8,128)(2,1)} %rels.7) | copy-start | bytes 1572868
  16.4 3.7 %collective-permute-start = (bf16[7,128,256]{2,1,0:T(8,128)(2,1)S(1)}, bf16[7,128,256]{2,1,0:T(8,128)(2,1)S(1)}, u32[]{:S(2)}, u32[]{:S(2)}) collective-permute-start(bf16[7,128,256]{2,1,0:T(8,128)(2,1)S(1)} %get-tuple-element.27), channel_id=1, source_target_pairs={{0,32},{32,0},{64,96},{96,64},{128,160},{160,128},{192,224},{224,1... | collective-permute-start | bytes 1376264 | tf_op jit(solution)/shard_map/ppermute | solution.py:74
  20.2 34.6 %collective-permute-start.1 = (bf16[4,128,256]{2,1,0:T(8,128)(2,1)S(1)}, bf16[4,128,256]{2,1,0:T(8,128)(2,1)S(1)}, u32[]{:S(2)}, u32[]{:S(2)}) collective-permute-start(bf16[4,128,256]{2,1,0:T(8,128)(2,1)S(1)} %get-tuple-element.29), channel_id=1, source_target_pairs={{0,64},{32,480},{64,128},{96,32},{128,192},{160,96},{192,256},{224... | collective-permute-start | bytes 786440 | tf_op jit(solution)/shard_map/ppermute | solution.py:81
  24.5 30.4 %collective-permute-start.2 = (bf16[4,128,256]{2,1,0:T(8,128)(2,1)S(1)}, bf16[4,128,256]{2,1,0:T(8,128)(2,1)S(1)}, u32[]{:S(2)}, u32[]{:S(2)}) collective-permute-start(bf16[4,128,256]{2,1,0:T(8,128)(2,1)S(1)} %get-tuple-element.30), channel_id=1, source_target_pairs={{0,128},{32,416},{64,192},{96,480},{128,256},{160,32},{192,320},{2... | collective-permute-start | bytes 786440 | tf_op jit(solution)/shard_map/ppermute | solution.py:81
  30.9 23.9 %collective-permute-start.3 = (bf16[4,128,256]{2,1,0:T(8,128)(2,1)S(1)}, bf16[4,128,256]{2,1,0:T(8,128)(2,1)S(1)}, u32[]{:S(2)}, u32[]{:S(2)}) collective-permute-start(bf16[4,128,256]{2,1,0:T(8,128)(2,1)S(1)} %get-tuple-element.31), channel_id=1, source_target_pairs={{0,192},{32,352},{64,256},{96,416},{128,320},{160,480},{192,384},{... | collective-permute-start | bytes 786440 | tf_op jit(solution)/shard_map/ppermute | solution.py:81
  34.7 20.2 %collective-permute-start.4 = (bf16[2,128,256]{2,1,0:T(8,128)(2,1)S(1)}, bf16[2,128,256]{2,1,0:T(8,128)(2,1)S(1)}, u32[]{:S(2)}, u32[]{:S(2)}) collective-permute-start(bf16[2,128,256]{2,1,0:T(8,128)(2,1)S(1)} %get-tuple-element.32), channel_id=1, source_target_pairs={{0,256},{32,288},{64,320},{96,352},{128,384},{160,416},{192,448},{... | collective-permute-start | bytes 393224 | tf_op jit(solution)/shard_map/ppermute | solution.py:81
  54.9 3.7 %collective-permute-start.5 = (bf16[7,128,256]{2,1,0:T(8,128)(2,1)S(1)}, bf16[7,128,256]{2,1,0:T(8,128)(2,1)S(1)}, u32[]{:S(2)}, u32[]{:S(2)}) collective-permute-start(bf16[7,128,256]{2,1,0:T(8,128)(2,1)S(1)} %get-tuple-element.34), channel_id=1, source_target_pairs={{0,32},{32,0},{64,96},{96,64},{128,160},{160,128},{192,224},{224,1... | collective-permute-start | bytes 1376264 | tf_op jit(solution)/shard_map/ppermute | solution.py:74
  58.6 1.2 copy-start.11
  61.2 7.2 %copy-start.1 = (bf16[32,128,256]{2,1,0:T(8,128)(2,1)}, bf16[32,128,256]{2,1,0:T(8,128)(2,1)S(1)}, u32[]{:S(2)}) copy-start(bf16[32,128,256]{2,1,0:T(8,128)(2,1)S(1)} %shard_map.99.stage) | copy-start | bytes 6291460
  68.5 1.5 %copy-start.10 = (bf16[32,160,256]{2,1,0:T(8,128)(2,1)}, bf16[32,160,256]{2,1,0:T(8,128)(2,1)S(1)}, u32[]{:S(2)}) copy-start(bf16[32,160,256]{2,1,0:T(8,128)(2,1)S(1)} %get-tuple-element.36) | copy-start | bytes 7864324
  70.0 1.0 copy-start.12
  70.9 70.8 %all-to-all-start.1 = ((bf16[32,160,256]{2,1,0:T(8,128)(2,1)}), bf16[32,160,256]{2,1,0:T(8,128)(2,1)S(1)}, u32[]{:S(2)}, u32[]{:S(2)}) async-start(bf16[32,160,256]{2,1,0:T(8,128)(2,1)} %copy-done.10), calls=%async_computation.1 | async-start | bytes 5242880 | tf_op jit(solution)/shard_map/all_to_all | solution.py:235
  78.0 1.6 %copy-start.2 = (bf16[32,128,256]{2,1,0:T(8,128)(2,1)S(1)}, bf16[32,128,256]{2,1,0:T(8,128)(2,1)}, u32[]{:S(2)}) copy-start(bf16[32,128,256]{2,1,0:T(8,128)(2,1)} %copy-done.1) | copy-start | bytes 6291460
  79.6 1.0 copy-start.6
  80.6 42.6 %copy-start.7 = (bf16[4,256,256]{2,1,0:T(8,128)(2,1)S(1)}, bf16[4,256,256]{2,1,0:T(8,128)(2,1)}, u32[]{:S(2)}) copy-start(bf16[4,256,256]{2,1,0:T(8,128)(2,1)} %rels.7) | copy-start | bytes 1572868
  80.6 42.6 %copy-start.13 = (bf16[16,128,256]{2,1,0:T(8,128)(2,1)S(1)}, bf16[16,128,256]{2,1,0:T(8,128)(2,1)}, u32[]{:S(2)}) copy-start(bf16[16,128,256]{2,1,0:T(8,128)(2,1)} %copy-done.12) | copy-start | bytes 3145732
  81.9 3.7 %collective-permute-start.6 = (bf16[7,128,256]{2,1,0:T(8,128)(2,1)S(1)}, bf16[7,128,256]{2,1,0:T(8,128)(2,1)S(1)}, u32[]{:S(2)}, u32[]{:S(2)}) collective-permute-start(bf16[7,128,256]{2,1,0:T(8,128)(2,1)S(1)} %get-tuple-element.40), channel_id=1, source_target_pairs={{0,32},{32,0},{64,96},{96,64},{128,160},{160,128},{192,224},{224,1... | collective-permute-start | bytes 1376264 | tf_op jit(solution)/shard_map/ppermute | solution.py:74
  85.7 33.7 %collective-permute-start.7 = (bf16[4,128,256]{2,1,0:T(8,128)(2,1)S(1)}, bf16[4,128,256]{2,1,0:T(8,128)(2,1)S(1)}, u32[]{:S(2)}, u32[]{:S(2)}) collective-permute-start(bf16[4,128,256]{2,1,0:T(8,128)(2,1)S(1)} %get-tuple-element.42), channel_id=1, source_target_pairs={{0,64},{32,480},{64,128},{96,32},{128,192},{160,96},{192,256},{224... | collective-permute-start | bytes 786440 | tf_op jit(solution)/shard_map/ppermute | solution.py:81
  89.1 30.3 %collective-permute-start.8 = (bf16[4,128,256]{2,1,0:T(8,128)(2,1)S(1)}, bf16[4,128,256]{2,1,0:T(8,128)(2,1)S(1)}, u32[]{:S(2)}, u32[]{:S(2)}) collective-permute-start(bf16[4,128,256]{2,1,0:T(8,128)(2,1)S(1)} %get-tuple-element.43), channel_id=1, source_target_pairs={{0,128},{32,416},{64,192},{96,480},{128,256},{160,32},{192,320},{2... | collective-permute-start | bytes 786440 | tf_op jit(solution)/shard_map/ppermute | solution.py:81
  95.5 23.9 %collective-permute-start.9 = (bf16[4,128,256]{2,1,0:T(8,128)(2,1)S(1)}, bf16[4,128,256]{2,1,0:T(8,128)(2,1)S(1)}, u32[]{:S(2)}, u32[]{:S(2)}) collective-permute-start(bf16[4,128,256]{2,1,0:T(8,128)(2,1)S(1)} %get-tuple-element.44), channel_id=1, source_target_pairs={{0,192},{32,352},{64,256},{96,416},{128,320},{160,480},{192,384},{... | collective-permute-start | bytes 786440 | tf_op jit(solution)/shard_map/ppermute | solution.py:81
  99.2 20.2 %collective-permute-start.10 = (bf16[2,128,256]{2,1,0:T(8,128)(2,1)S(1)}, bf16[2,128,256]{2,1,0:T(8,128)(2,1)S(1)}, u32[]{:S(2)}, u32[]{:S(2)}) collective-permute-start(bf16[2,128,256]{2,1,0:T(8,128)(2,1)S(1)} %get-tuple-element.45), channel_id=1, source_target_pairs={{0,256},{32,288},{64,320},{96,352},{128,384},{160,416},{192,448},{... | collective-permute-start | bytes 393224 | tf_op jit(solution)/shard_map/ppermute | solution.py:81
  119.5 3.7 %collective-permute-start.11 = (bf16[7,128,256]{2,1,0:T(8,128)(2,1)S(1)}, bf16[7,128,256]{2,1,0:T(8,128)(2,1)S(1)}, u32[]{:S(2)}, u32[]{:S(2)}) collective-permute-start(bf16[7,128,256]{2,1,0:T(8,128)(2,1)S(1)} %get-tuple-element.47), channel_id=1, source_target_pairs={{0,32},{32,0},{64,96},{96,64},{128,160},{160,128},{192,224},{224,1... | collective-permute-start | bytes 1376264 | tf_op jit(solution)/shard_map/ppermute | solution.py:74
  124.8 1.0 copy-start.8
  141.7 1.2 copy-start.9

commit v5 on v4

--- a/solution.py
+++ b/solution.py
@@ -190,10 +190,8 @@
 
 def add_dst_body(code, acc_in, back, acc, rel_out):
     acc[...] = acc_in[...]
-    rel_out[...] = jnp.zeros(rel_out.shape, F32)
+    rel_out[...] = sum(back[p, B:].astype(F32) for p in range(32))
     for p in range(32):
-        rel_out[...] += back[p, B:].astype(F32)
-
         @pl.when(code[p] > 0)
         def _():
             acc[code[p] - 1] += back[p, :B].astype(F32)

time: 146 us -> 146 us (level)
  no operation moved by 1% of the time
where the time goes in v5:
time: 146 us; the launch traced here: 145 us
  starting transfers between devices  63.1 us (43%)
  waiting for transfers between devices  56.7 us (39%)
  Pallas kernels  12.9 us (9%)
  local copies, waits for them, and re-layouts  10.5 us (7%)
    ppermute x8, starting transfers between devices, zmove(): return lax.ppermute(v, 'group', pairs)  38.2 us
    ppermute x8, waiting for transfers between devices, zmove(): return lax.ppermute(v, 'group', pairs)  30.2 us
    all_to_all x1, waiting for transfers between devices, per_device(): lax.all_to_all(back, 'member', split_axis=0, concat_axis=0, tiled=True)  15.9 us
    all_to_all x1, starting transfers between devices, per_device(): lax.all_to_all(outgoing, 'member', split_axis=0, concat_axis=0, tiled=True)  10.2 us
    unnamed x34, local copies, waits for them, and re-layouts  9.59 us
    ppermute x4, starting transfers between devices, swap(): return lax.ppermute(v, 'group', [(i, i ^ 1) for i in range(16)])  7.68 us
    ppermute x4, waiting for transfers between devices, swap(): return lax.ppermute(v, 'group', [(i, i ^ 1) for i in range(16)])  7.13 us
    all_to_all x1, starting transfers between devices, per_device(): lax.all_to_all(back, 'member', split_axis=0, concat_axis=0, tiled=True)  7.02 us
  transfers between devices with their start and end apart: 14, of which 8 were waited for; matrix products, arithmetic and copies ran while one was open for 1% of the time, Pallas kernels for 3%

profile of v5, /device:TPU:128, one launch (start us, length us, event | category | flops | bytes accessed | tf_op | source)
XLA Modules:
  0.0 145.0 jit_solution(13727395175738507716)
XLA Ops:
  2.4 2.0 %shard_map.95 = bf16[32,128,256]{2,1,0:T(8,128)(2,1)} custom-call(s32[32]{0:T(128)S(1)} %select_reduce_fusion.code, bf16[8,128,256]{2,1,0:T(8,128)(2,1)S(1)} %bitcast.20), custom_call_target="tpu_custom_call" | custom-call | bytes 4194304 | tf_op jit(solution)/shard_map/pallas_call | solution.py:208
  4.4 10.2 %all-to-all-start = ((bf16[32,128,256]{2,1,0:T(8,128)(2,1)}), bf16[32,128,256]{2,1,0:T(8,128)(2,1)}, u32[]{:S(2)}, u32[]{:S(2)}) async-start(bf16[32,128,256]{2,1,0:T(8,128)(2,1)} %shard_map.95), calls=%async_computation | async-start | bytes 4194304 | tf_op jit(solution)/shard_map/all_to_all | solution.py:209
  16.4 1.9 %collective-permute-start = (bf16[7,128,256]{2,1,0:T(8,128)(2,1)S(1)}, bf16[7,128,256]{2,1,0:T(8,128)(2,1)S(1)}, u32[]{:S(2)}, u32[]{:S(2)}) collective-permute-start(bf16[7,128,256]{2,1,0:T(8,128)(2,1)S(1)} %get-tuple-element.27), channel_id=1, source_target_pairs={{0,32},{32,0},{64,96},{96,64},{128,160},{160,128},{192,224},{224,1... | collective-permute-start | bytes 1376264 | tf_op jit(solution)/shard_map/ppermute | solution.py:74
  18.4 1.8 %collective-permute-done.arrived = bf16[7,128,256]{2,1,0:T(8,128)(2,1)S(1)} collective-permute-done((bf16[7,128,256]{2,1,0:T(8,128)(2,1)S(1)}, bf16[7,128,256]{2,1,0:T(8,128)(2,1)S(1)}, u32[]{:S(2)}, u32[]{:S(2)}) %collective-permute-start) | collective-permute-done | bytes 458784 | tf_op jit(solution)/shard_map/ppermute | solution.py:74
  20.2 4.3 %collective-permute-start.1 = (bf16[4,128,256]{2,1,0:T(8,128)(2,1)S(1)}, bf16[4,128,256]{2,1,0:T(8,128)(2,1)S(1)}, u32[]{:S(2)}, u32[]{:S(2)}) collective-permute-start(bf16[4,128,256]{2,1,0:T(8,128)(2,1)S(1)} %get-tuple-element.29), channel_id=1, source_target_pairs={{0,64},{32,480},{64,128},{96,32},{128,192},{160,96},{192,256},{224... | collective-permute-start | bytes 786440 | tf_op jit(solution)/shard_map/ppermute | solution.py:81
  24.5 6.4 %collective-permute-start.2 = (bf16[4,128,256]{2,1,0:T(8,128)(2,1)S(1)}, bf16[4,128,256]{2,1,0:T(8,128)(2,1)S(1)}, u32[]{:S(2)}, u32[]{:S(2)}) collective-permute-start(bf16[4,128,256]{2,1,0:T(8,128)(2,1)S(1)} %get-tuple-element.30), channel_id=1, source_target_pairs={{0,128},{32,416},{64,192},{96,480},{128,256},{160,32},{192,320},{2... | collective-permute-start | bytes 786440 | tf_op jit(solution)/shard_map/ppermute | solution.py:81
  30.9 3.7 %collective-permute-start.3 = (bf16[4,128,256]{2,1,0:T(8,128)(2,1)S(1)}, bf16[4,128,256]{2,1,0:T(8,128)(2,1)S(1)}, u32[]{:S(2)}, u32[]{:S(2)}) collective-permute-start(bf16[4,128,256]{2,1,0:T(8,128)(2,1)S(1)} %get-tuple-element.31), channel_id=1, source_target_pairs={{0,192},{32,352},{64,256},{96,416},{128,320},{160,480},{192,384},{... | collective-permute-start | bytes 786440 | tf_op jit(solution)/shard_map/ppermute | solution.py:81
  34.7 5.1 %collective-permute-start.4 = (bf16[2,128,256]{2,1,0:T(8,128)(2,1)S(1)}, bf16[2,128,256]{2,1,0:T(8,128)(2,1)S(1)}, u32[]{:S(2)}, u32[]{:S(2)}) collective-permute-start(bf16[2,128,256]{2,1,0:T(8,128)(2,1)S(1)} %get-tuple-element.32), channel_id=1, source_target_pairs={{0,256},{32,288},{64,320},{96,352},{128,384},{160,416},{192,448},{... | collective-permute-start | bytes 393224 | tf_op jit(solution)/shard_map/ppermute | solution.py:81
  39.8 15.1 %collective-permute-done.4.r4 = bf16[2,128,256]{2,1,0:T(8,128)(2,1)S(1)} collective-permute-done((bf16[2,128,256]{2,1,0:T(8,128)(2,1)S(1)}, bf16[2,128,256]{2,1,0:T(8,128)(2,1)S(1)}, u32[]{:S(2)}, u32[]{:S(2)}) %collective-permute-start.4) | collective-permute-done | bytes 131104 | tf_op jit(solution)/shard_map/ppermute | solution.py:81
  54.9 1.9 %collective-permute-start.5 = (bf16[7,128,256]{2,1,0:T(8,128)(2,1)S(1)}, bf16[7,128,256]{2,1,0:T(8,128)(2,1)S(1)}, u32[]{:S(2)}, u32[]{:S(2)}) collective-permute-start(bf16[7,128,256]{2,1,0:T(8,128)(2,1)S(1)} %get-tuple-element.34), channel_id=1, source_target_pairs={{0,32},{32,0},{64,96},{96,64},{128,160},{160,128},{192,224},{224,1... | collective-permute-start | bytes 1376264 | tf_op jit(solution)/shard_map/ppermute | solution.py:74
  56.9 1.8 %collective-permute-done.5.last = bf16[7,128,256]{2,1,0:T(8,128)(2,1)S(1)} collective-permute-done((bf16[7,128,256]{2,1,0:T(8,128)(2,1)S(1)}, bf16[7,128,256]{2,1,0:T(8,128)(2,1)S(1)}, u32[]{:S(2)}, u32[]{:S(2)}) %collective-permute-start.5) | collective-permute-done | bytes 458784 | tf_op jit(solution)/shard_map/ppermute | solution.py:74
  58.6 1.2 copy-done.11
  59.9 1.3 shard_map.99.stage
  61.2 3.5 %all-to-all-done.received = bf16[32,128,256]{2,1,0:T(8,128)(2,1)} async-done(((bf16[32,128,256]{2,1,0:T(8,128)(2,1)}), bf16[32,128,256]{2,1,0:T(8,128)(2,1)}, u32[]{:S(2)}, u32[]{:S(2)}) %all-to-all-start) | async-done | bytes 2097184 | tf_op jit(solution)/shard_map/all_to_all | solution.py:209
  64.7 3.8 %shard_map.100 = (bf16[32,160,256]{2,1,0:T(8,128)(2,1)S(1)}, bf16[16,128,256]{2,1,0:T(8,128)(2,1)S(1)}) custom-call(s32[96]{0:T(128)S(1)} %concatenate.3.idx, bf16[8,128,256]{2,1,0:T(8,128)(2,1)S(1)} %bitcast.23, bf16[4,256,256]{2,1,0:T(8,128)(2,1)S(1)} %copy-done.5, bf16[32,128,256]{2,1,0:T(8,128)(2,1)} %all-to-all-done.received, ...), custom_call_target="tpu_custom_call" | custom-call | flops 1677721600 | bytes 4194304 | tf_op jit(solution)/shard_map/pallas_call | solution.py:225
  68.5 1.5 %copy-done.10 = bf16[32,160,256]{2,1,0:T(8,128)(2,1)} copy-done((bf16[32,160,256]{2,1,0:T(8,128)(2,1)}, bf16[32,160,256]{2,1,0:T(8,128)(2,1)S(1)}, u32[]{:S(2)}) %copy-start.10) | copy-done | bytes 2621464
  70.9 7.0 %all-to-all-start.1 = ((bf16[32,160,256]{2,1,0:T(8,128)(2,1)}), bf16[32,160,256]{2,1,0:T(8,128)(2,1)S(1)}, u32[]{:S(2)}, u32[]{:S(2)}) async-start(bf16[32,160,256]{2,1,0:T(8,128)(2,1)} %copy-done.10), calls=%async_computation.1 | async-start | bytes 5242880 | tf_op jit(solution)/shard_map/all_to_all | solution.py:233
  78.0 1.6 %copy-done.2 = bf16[32,128,256]{2,1,0:T(8,128)(2,1)S(1)} copy-done((bf16[32,128,256]{2,1,0:T(8,128)(2,1)S(1)}, bf16[32,128,256]{2,1,0:T(8,128)(2,1)}, u32[]{:S(2)}) %copy-start.2) | copy-done | bytes 2097176
  80.6 1.3 shard_map.101
  81.9 1.9 %collective-permute-start.6 = (bf16[7,128,256]{2,1,0:T(8,128)(2,1)S(1)}, bf16[7,128,256]{2,1,0:T(8,128)(2,1)S(1)}, u32[]{:S(2)}, u32[]{:S(2)}) collective-permute-start(bf16[7,128,256]{2,1,0:T(8,128)(2,1)S(1)} %get-tuple-element.40), channel_id=1, source_target_pairs={{0,32},{32,0},{64,96},{96,64},{128,160},{160,128},{192,224},{224,1... | collective-permute-start | bytes 1376264 | tf_op jit(solution)/shard_map/ppermute | solution.py:74
  83.8 1.8 %collective-permute-done.6.arrived = bf16[7,128,256]{2,1,0:T(8,128)(2,1)S(1)} collective-permute-done((bf16[7,128,256]{2,1,0:T(8,128)(2,1)S(1)}, bf16[7,128,256]{2,1,0:T(8,128)(2,1)S(1)}, u32[]{:S(2)}, u32[]{:S(2)}) %collective-permute-start.6) | collective-permute-done | bytes 458784 | tf_op jit(solution)/shard_map/ppermute | solution.py:74
  85.7 3.4 %collective-permute-start.7 = (bf16[4,128,256]{2,1,0:T(8,128)(2,1)S(1)}, bf16[4,128,256]{2,1,0:T(8,128)(2,1)S(1)}, u32[]{:S(2)}, u32[]{:S(2)}) collective-permute-start(bf16[4,128,256]{2,1,0:T(8,128)(2,1)S(1)} %get-tuple-element.42), channel_id=1, source_target_pairs={{0,64},{32,480},{64,128},{96,32},{128,192},{160,96},{192,256},{224... | collective-permute-start | bytes 786440 | tf_op jit(solution)/shard_map/ppermute | solution.py:81
  89.1 6.4 %collective-permute-start.8 = (bf16[4,128,256]{2,1,0:T(8,128)(2,1)S(1)}, bf16[4,128,256]{2,1,0:T(8,128)(2,1)S(1)}, u32[]{:S(2)}, u32[]{:S(2)}) collective-permute-start(bf16[4,128,256]{2,1,0:T(8,128)(2,1)S(1)} %get-tuple-element.43), channel_id=1, source_target_pairs={{0,128},{32,416},{64,192},{96,480},{128,256},{160,32},{192,320},{2... | collective-permute-start | bytes 786440 | tf_op jit(solution)/shard_map/ppermute | solution.py:81
  95.5 3.7 %collective-permute-start.9 = (bf16[4,128,256]{2,1,0:T(8,128)(2,1)S(1)}, bf16[4,128,256]{2,1,0:T(8,128)(2,1)S(1)}, u32[]{:S(2)}, u32[]{:S(2)}) collective-permute-start(bf16[4,128,256]{2,1,0:T(8,128)(2,1)S(1)} %get-tuple-element.44), channel_id=1, source_target_pairs={{0,192},{32,352},{64,256},{96,416},{128,320},{160,480},{192,384},{... | collective-permute-start | bytes 786440 | tf_op jit(solution)/shard_map/ppermute | solution.py:81
  99.2 5.1 %collective-permute-start.10 = (bf16[2,128,256]{2,1,0:T(8,128)(2,1)S(1)}, bf16[2,128,256]{2,1,0:T(8,128)(2,1)S(1)}, u32[]{:S(2)}, u32[]{:S(2)}) collective-permute-start(bf16[2,128,256]{2,1,0:T(8,128)(2,1)S(1)} %get-tuple-element.45), channel_id=1, source_target_pairs={{0,256},{32,288},{64,320},{96,352},{128,384},{160,416},{192,448},{... | collective-permute-start | bytes 393224 | tf_op jit(solution)/shard_map/ppermute | solution.py:81
  104.3 15.1 %collective-permute-done.10.r4 = bf16[2,128,256]{2,1,0:T(8,128)(2,1)S(1)} collective-permute-done((bf16[2,128,256]{2,1,0:T(8,128)(2,1)S(1)}, bf16[2,128,256]{2,1,0:T(8,128)(2,1)S(1)}, u32[]{:S(2)}, u32[]{:S(2)}) %collective-permute-start.10) | collective-permute-done | bytes 131104 | tf_op jit(solution)/shard_map/ppermute | solution.py:81
  119.5 1.9 %collective-permute-start.11 = (bf16[7,128,256]{2,1,0:T(8,128)(2,1)S(1)}, bf16[7,128,256]{2,1,0:T(8,128)(2,1)S(1)}, u32[]{:S(2)}, u32[]{:S(2)}) collective-permute-start(bf16[7,128,256]{2,1,0:T(8,128)(2,1)S(1)} %get-tuple-element.47), channel_id=1, source_target_pairs={{0,32},{32,0},{64,96},{96,64},{128,160},{160,128},{192,224},{224,1... | collective-permute-start | bytes 1376264 | tf_op jit(solution)/shard_map/ppermute | solution.py:74
  121.4 1.8 %collective-permute-done.11.last = bf16[7,128,256]{2,1,0:T(8,128)(2,1)S(1)} collective-permute-done((bf16[7,128,256]{2,1,0:T(8,128)(2,1)S(1)}, bf16[7,128,256]{2,1,0:T(8,128)(2,1)S(1)}, u32[]{:S(2)}, u32[]{:S(2)}) %collective-permute-start.11) | collective-permute-done | bytes 458784 | tf_op jit(solution)/shard_map/ppermute | solution.py:74
  123.2 1.6 %shard_map.104.acc_in = f32[8,128,256]{2,1,0:T(8,128)S(1)} custom-call(s32[96]{0:T(128)S(1)} %concatenate.3.idx, bf16[4,256,256]{2,1,0:T(8,128)(2,1)S(1)} %copy-done.7, bf16[16,128,256]{2,1,0:T(8,128)(2,1)S(1)} %copy-done.13, bf16[1,128,256]{2,1,0:T(8,128)(2,1)S(1)} %get-tuple-element.39.stays, bf16[8,128,256]{2,1,0:T(8,128)(2,1)S(1)} %get-tuple-element.46.mine, ...), custom_call_target="tpu_custom_call" | custom-call | flops 268435456 | bytes 4194304 | tf_op jit(solution)/shard_map/pallas_call | solution.py:243
  125.8 15.9 %all-to-all-done.1.back = bf16[32,160,256]{2,1,0:T(8,128)(2,1)S(1)} async-done(((bf16[32,160,256]{2,1,0:T(8,128)(2,1)}), bf16[32,160,256]{2,1,0:T(8,128)(2,1)S(1)}, u32[]{:S(2)}, u32[]{:S(2)}) %all-to-all-start.1) | async-done | bytes 2621472 | tf_op jit(solution)/shard_map/all_to_all | solution.py:233
  141.7 1.2 copy-done.9
  142.9 2.1 %shard_map.105 = (f32[8,128,256]{2,1,0:T(8,128)}, f32[32,256]{1,0:T(8,128)}) custom-call(s32[32]{0:T(128)S(1)} %select_reduce_fusion.code, f32[8,128,256]{2,1,0:T(8,128)S(1)} %copy-done.9, bf16[32,160,256]{2,1,0:T(8,128)(2,1)S(1)} %all-to-all-done.1.back), custom_call_target="tpu_custom_call" | custom-call | flops 1048576 | bytes 4194304 | tf_op jit(solution)/shard_map/pallas_call | solution.py:247
  (46 shorter events, 6.6 us)
Async XLA Ops:
  0.6 14.2 %copy-start = (s32[1,32,16]{1,2,0:T(8,128)S(1)}, s32[1,32,16]{1,2,0:T(8,128)}, u32[]{:S(2)}) copy-start(s32[1,32,16]{1,2,0:T(8,128)} %param.10) | copy-start | bytes 6148
  1.4 1.0 copy-start.3
  4.4 10.6 %copy-start.14 = (s32[1,32,16]{1,2,0:T(8,128)S(1)}, s32[1,32,16]{1,2,0:T(8,128)}, u32[]{:S(2)}) copy-start(s32[1,32,16]{1,2,0:T(8,128)} %param.11) | copy-start | bytes 6148
  4.4 10.6 %copy-start.16 = (s32[1,32,16]{1,2,0:T(8,128)S(1)}, s32[1,32,16]{1,2,0:T(8,128)}, u32[]{:S(2)}) copy-start(s32[1,32,16]{1,2,0:T(8,128)} %param.13) | copy-start | bytes 6148
  4.4 10.8 %copy-start.15 = (s32[16,1,16]{2,1,0:T(1,128)S(1)}, s32[16,1,16]{2,1,0:T(1,128)}, u32[]{:S(2)}) copy-start(s32[16,1,16]{2,1,0:T(1,128)} %param.14) | copy-start | bytes 3076
  4.4 11.4 %copy-start.4 = (bf16[1024,256]{1,0:T(8,128)(2,1)S(1)}, bf16[1024,256]{1,0:T(8,128)(2,1)}, u32[]{:S(2)}) copy-start(bf16[1024,256]{1,0:T(8,128)(2,1)} %param.8) | copy-start | bytes 1572868
  4.4 60.3 %all-to-all-start = ((bf16[32,128,256]{2,1,0:T(8,128)(2,1)}), bf16[32,128,256]{2,1,0:T(8,128)(2,1)}, u32[]{:S(2)}, u32[]{:S(2)}) async-start(bf16[32,128,256]{2,1,0:T(8,128)(2,1)} %shard_map.95), calls=%async_computation | async-start | bytes 4194304 | tf_op jit(solution)/shard_map/all_to_all | solution.py:209
  14.6 44.0 %copy-start.5 = (bf16[4,256,256]{2,1,0:T(8,128)(2,1)S(1)}, bf16[4,256,256]{2,1,0:T(8,128)(2,1)}, u32[]{:S(2)}) copy-start(bf16[4,256,256]{2,1,0:T(8,128)(2,1)} %rels.7) | copy-start | bytes 1572868
  16.4 3.7 %collective-permute-start = (bf16[7,128,256]{2,1,0:T(8,128)(2,1)S(1)}, bf16[7,128,256]{2,1,0:T(8,128)(2,1)S(1)}, u32[]{:S(2)}, u32[]{:S(2)}) collective-permute-start(bf16[7,128,256]{2,1,0:T(8,128)(2,1)S(1)} %get-tuple-element.27), channel_id=1, source_target_pairs={{0,32},{32,0},{64,96},{96,64},{128,160},{160,128},{192,224},{224,1... | collective-permute-start | bytes 1376264 | tf_op jit(solution)/shard_map/ppermute | solution.py:74
  20.2 34.6 %collective-permute-start.1 = (bf16[4,128,256]{2,1,0:T(8,128)(2,1)S(1)}, bf16[4,128,256]{2,1,0:T(8,128)(2,1)S(1)}, u32[]{:S(2)}, u32[]{:S(2)}) collective-permute-start(bf16[4,128,256]{2,1,0:T(8,128)(2,1)S(1)} %get-tuple-element.29), channel_id=1, source_target_pairs={{0,64},{32,480},{64,128},{96,32},{128,192},{160,96},{192,256},{224... | collective-permute-start | bytes 786440 | tf_op jit(solution)/shard_map/ppermute | solution.py:81
  24.5 30.4 %collective-permute-start.2 = (bf16[4,128,256]{2,1,0:T(8,128)(2,1)S(1)}, bf16[4,128,256]{2,1,0:T(8,128)(2,1)S(1)}, u32[]{:S(2)}, u32[]{:S(2)}) collective-permute-start(bf16[4,128,256]{2,1,0:T(8,128)(2,1)S(1)} %get-tuple-element.30), channel_id=1, source_target_pairs={{0,128},{32,416},{64,192},{96,480},{128,256},{160,32},{192,320},{2... | collective-permute-start | bytes 786440 | tf_op jit(solution)/shard_map/ppermute | solution.py:81
  30.9 23.9 %collective-permute-start.3 = (bf16[4,128,256]{2,1,0:T(8,128)(2,1)S(1)}, bf16[4,128,256]{2,1,0:T(8,128)(2,1)S(1)}, u32[]{:S(2)}, u32[]{:S(2)}) collective-permute-start(bf16[4,128,256]{2,1,0:T(8,128)(2,1)S(1)} %get-tuple-element.31), channel_id=1, source_target_pairs={{0,192},{32,352},{64,256},{96,416},{128,320},{160,480},{192,384},{... | collective-permute-start | bytes 786440 | tf_op jit(solution)/shard_map/ppermute | solution.py:81
  34.7 20.2 %collective-permute-start.4 = (bf16[2,128,256]{2,1,0:T(8,128)(2,1)S(1)}, bf16[2,128,256]{2,1,0:T(8,128)(2,1)S(1)}, u32[]{:S(2)}, u32[]{:S(2)}) collective-permute-start(bf16[2,128,256]{2,1,0:T(8,128)(2,1)S(1)} %get-tuple-element.32), channel_id=1, source_target_pairs={{0,256},{32,288},{64,320},{96,352},{128,384},{160,416},{192,448},{... | collective-permute-start | bytes 393224 | tf_op jit(solution)/shard_map/ppermute | solution.py:81
  54.9 3.7 %collective-permute-start.5 = (bf16[7,128,256]{2,1,0:T(8,128)(2,1)S(1)}, bf16[7,128,256]{2,1,0:T(8,128)(2,1)S(1)}, u32[]{:S(2)}, u32[]{:S(2)}) collective-permute-start(bf16[7,128,256]{2,1,0:T(8,128)(2,1)S(1)} %get-tuple-element.34), channel_id=1, source_target_pairs={{0,32},{32,0},{64,96},{96,64},{128,160},{160,128},{192,224},{224,1... | collective-permute-start | bytes 1376264 | tf_op jit(solution)/shard_map/ppermute | solution.py:74
  58.6 1.2 copy-start.11
  61.2 7.2 %copy-start.1 = (bf16[32,128,256]{2,1,0:T(8,128)(2,1)}, bf16[32,128,256]{2,1,0:T(8,128)(2,1)S(1)}, u32[]{:S(2)}) copy-start(bf16[32,128,256]{2,1,0:T(8,128)(2,1)S(1)} %shard_map.99.stage) | copy-start | bytes 6291460
  68.5 1.5 %copy-start.10 = (bf16[32,160,256]{2,1,0:T(8,128)(2,1)}, bf16[32,160,256]{2,1,0:T(8,128)(2,1)S(1)}, u32[]{:S(2)}) copy-start(bf16[32,160,256]{2,1,0:T(8,128)(2,1)S(1)} %get-tuple-element.36) | copy-start | bytes 7864324
  70.0 1.0 copy-start.12
  70.9 70.8 %all-to-all-start.1 = ((bf16[32,160,256]{2,1,0:T(8,128)(2,1)}), bf16[32,160,256]{2,1,0:T(8,128)(2,1)S(1)}, u32[]{:S(2)}, u32[]{:S(2)}) async-start(bf16[32,160,256]{2,1,0:T(8,128)(2,1)} %copy-done.10), calls=%async_computation.1 | async-start | bytes 5242880 | tf_op jit(solution)/shard_map/all_to_all | solution.py:233
  78.0 1.6 %copy-start.2 = (bf16[32,128,256]{2,1,0:T(8,128)(2,1)S(1)}, bf16[32,128,256]{2,1,0:T(8,128)(2,1)}, u32[]{:S(2)}) copy-start(bf16[32,128,256]{2,1,0:T(8,128)(2,1)} %copy-done.1) | copy-start | bytes 6291460
  79.6 1.0 copy-start.6
  80.6 42.6 %copy-start.7 = (bf16[4,256,256]{2,1,0:T(8,128)(2,1)S(1)}, bf16[4,256,256]{2,1,0:T(8,128)(2,1)}, u32[]{:S(2)}) copy-start(bf16[4,256,256]{2,1,0:T(8,128)(2,1)} %rels.7) | copy-start | bytes 1572868
  80.6 42.6 %copy-start.13 = (bf16[16,128,256]{2,1,0:T(8,128)(2,1)S(1)}, bf16[16,128,256]{2,1,0:T(8,128)(2,1)}, u32[]{:S(2)}) copy-start(bf16[16,128,256]{2,1,0:T(8,128)(2,1)} %copy-done.12) | copy-start | bytes 3145732
  81.9 3.7 %collective-permute-start.6 = (bf16[7,128,256]{2,1,0:T(8,128)(2,1)S(1)}, bf16[7,128,256]{2,1,0:T(8,128)(2,1)S(1)}, u32[]{:S(2)}, u32[]{:S(2)}) collective-permute-start(bf16[7,128,256]{2,1,0:T(8,128)(2,1)S(1)} %get-tuple-element.40), channel_id=1, source_target_pairs={{0,32},{32,0},{64,96},{96,64},{128,160},{160,128},{192,224},{224,1... | collective-permute-start | bytes 1376264 | tf_op jit(solution)/shard_map/ppermute | solution.py:74
  85.7 33.7 %collective-permute-start.7 = (bf16[4,128,256]{2,1,0:T(8,128)(2,1)S(1)}, bf16[4,128,256]{2,1,0:T(8,128)(2,1)S(1)}, u32[]{:S(2)}, u32[]{:S(2)}) collective-permute-start(bf16[4,128,256]{2,1,0:T(8,128)(2,1)S(1)} %get-tuple-element.42), channel_id=1, source_target_pairs={{0,64},{32,480},{64,128},{96,32},{128,192},{160,96},{192,256},{224... | collective-permute-start | bytes 786440 | tf_op jit(solution)/shard_map/ppermute | solution.py:81
  89.1 30.3 %collective-permute-start.8 = (bf16[4,128,256]{2,1,0:T(8,128)(2,1)S(1)}, bf16[4,128,256]{2,1,0:T(8,128)(2,1)S(1)}, u32[]{:S(2)}, u32[]{:S(2)}) collective-permute-start(bf16[4,128,256]{2,1,0:T(8,128)(2,1)S(1)} %get-tuple-element.43), channel_id=1, source_target_pairs={{0,128},{32,416},{64,192},{96,480},{128,256},{160,32},{192,320},{2... | collective-permute-start | bytes 786440 | tf_op jit(solution)/shard_map/ppermute | solution.py:81
  95.5 23.9 %collective-permute-start.9 = (bf16[4,128,256]{2,1,0:T(8,128)(2,1)S(1)}, bf16[4,128,256]{2,1,0:T(8,128)(2,1)S(1)}, u32[]{:S(2)}, u32[]{:S(2)}) collective-permute-start(bf16[4,128,256]{2,1,0:T(8,128)(2,1)S(1)} %get-tuple-element.44), channel_id=1, source_target_pairs={{0,192},{32,352},{64,256},{96,416},{128,320},{160,480},{192,384},{... | collective-permute-start | bytes 786440 | tf_op jit(solution)/shard_map/ppermute | solution.py:81
  99.2 20.2 %collective-permute-start.10 = (bf16[2,128,256]{2,1,0:T(8,128)(2,1)S(1)}, bf16[2,128,256]{2,1,0:T(8,128)(2,1)S(1)}, u32[]{:S(2)}, u32[]{:S(2)}) collective-permute-start(bf16[2,128,256]{2,1,0:T(8,128)(2,1)S(1)} %get-tuple-element.45), channel_id=1, source_target_pairs={{0,256},{32,288},{64,320},{96,352},{128,384},{160,416},{192,448},{... | collective-permute-start | bytes 393224 | tf_op jit(solution)/shard_map/ppermute | solution.py:81
  119.5 3.7 %collective-permute-start.11 = (bf16[7,128,256]{2,1,0:T(8,128)(2,1)S(1)}, bf16[7,128,256]{2,1,0:T(8,128)(2,1)S(1)}, u32[]{:S(2)}, u32[]{:S(2)}) collective-permute-start(bf16[7,128,256]{2,1,0:T(8,128)(2,1)S(1)} %get-tuple-element.47), channel_id=1, source_target_pairs={{0,32},{32,0},{64,96},{96,64},{128,160},{160,128},{192,224},{224,1... | collective-permute-start | bytes 1376264 | tf_op jit(solution)/shard_map/ppermute | solution.py:74
  124.8 1.0 copy-start.8
  141.7 1.2 copy-start.9
